TPU v7x, 128 devices: a whole 4x4x4 slice. The times are simulated.
128 devices in a mesh: scan: 16 (over y, z_hi, core), tx: 4 (over x), ty: 2 (over z_lo).
Axes of the slice: x: 4, y: 4, z: 4 (z_hi: 2, z_lo: 2; z = z_hi * 2 + z_lo), core: 2. Of those that a mesh axis runs over, the one named last changes fastest.
Arguments:
- object_slices: float32 [2, 2, 1024, 512], P(None, None, 'tx', 'ty'), may hold values from -0.9 to 0.9
- probe_modes: float32 [2, 8, 256, 256], replicated, may hold values from -1.2 to 1.2
- corners: int32 [4, 2, 16, 2], P('tx', 'ty', 'scan'), may hold values from 0 to 127, as said below
- measured: float32 [4, 2, 16, 256, 256], P('tx', 'ty', 'scan'), may hold values from 0.2 to 2.5
Outputs:
- updated_object: float32 [2, 2, 1024, 512], P(None, None, 'tx', 'ty')
Inputs may be any that keep to these rules, and one draw needn't show every extreme that they name: corners place every window inside its own tile and the 128 pixels below and to the right of it.
All inputs are finite; a program needn't handle non-finite values.
Results may differ from a plain program's by a relative error of at most 0.0001.
Values sent between devices are 32-bit elements; how exact they have to be, the bound alone decides.
No kernel may reach another device: no remote copies, remote signals or barrier semaphores. Data moves between devices by JAX's collectives and lax.ppermute only.
A program may use at most 64 MiB of HBM per device.

v0:
```python
import math

import jax
import jax.numpy as jnp
from jax import lax
from jax.sharding import PartitionSpec as P

fresnel_coef = 0.1
step_size = 4.0
precise = lax.Precision.HIGHEST


def from_behind(array, axis, by):
    count = lax.axis_size(axis)
    pairs = [(i, i + by) for i in range(count) if 0 <= i + by < count]
    return lax.ppermute(array, axis, pairs)


def laplacian(field):
    padded = jnp.pad(field, ((0, 0), (0, 0), (1, 1), (1, 1)))
    return (
        padded[:, :, :-2, 1:-1]
        + padded[:, :, 2:, 1:-1]
        + padded[:, :, 1:-1, :-2]
        + padded[:, :, 1:-1, 2:]
        - 4.0 * field
    )


def propagate(field, sign_value):
    lap_once = laplacian(field)
    lap_twice = laplacian(lap_once)
    damping = 0.5 * fresnel_coef**2
    real_part = field[0] - sign_value * fresnel_coef * lap_once[1] - damping * lap_twice[0]
    imag_part = field[1] + sign_value * fresnel_coef * lap_once[0] - damping * lap_twice[1]
    return jnp.stack([real_part, imag_part])


def times_complex(first_factor, second_factor):
    real_part = first_factor[0] * second_factor[0] - first_factor[1] * second_factor[1]
    imag_part = first_factor[0] * second_factor[1] + first_factor[1] * second_factor[0]
    return jnp.stack([real_part, imag_part])


def conj_times(first_factor, second_factor):
    real_part = first_factor[0] * second_factor[0] + first_factor[1] * second_factor[1]
    imag_part = first_factor[0] * second_factor[1] - first_factor[1] * second_factor[0]
    return jnp.stack([real_part, imag_part])


def left_apply(table, field):
    return jnp.einsum("yk,mkx->myx", table, field, precision=precise)


def right_apply(field, table):
    return jnp.einsum("myk,kx->myx", field, table, precision=precise)


def fourier(field, cosine_table, sine_table):
    half_real = left_apply(cosine_table, field[0]) - left_apply(sine_table, field[1])
    half_imag = left_apply(cosine_table, field[1]) + left_apply(sine_table, field[0])
    full_real = right_apply(half_real, cosine_table) - right_apply(half_imag, sine_table)
    full_imag = right_apply(half_real, sine_table) + right_apply(half_imag, cosine_table)
    return jnp.stack([full_real, full_imag])


def position_terms(
    extended, probe_modes, row_start, col_start, measured_one, cosine_table, sine_table
):
    layers = extended.shape[0]
    pixels = probe_modes.shape[-1]
    window = lax.dynamic_slice(extended, (0, 0, row_start, col_start), (layers, 2, pixels, pixels))
    transmit = window.at[:, 0].add(1.0)
    stored = []
    field_now = probe_modes
    exit_wave = field_now
    for layer_index in range(layers):
        stored.append(field_now)
        exit_wave = times_complex(field_now, transmit[layer_index][:, None])
        if layer_index + 1 < layers:
            field_now = propagate(exit_wave, 1.0)
    far_field = fourier(exit_wave, cosine_table, -sine_table)
    misfit = jnp.sum(far_field[0] ** 2 + far_field[1] ** 2, axis=0) - measured_one
    backward = fourier(2.0 * misfit[None, None] * far_field, cosine_table, sine_table)
    gradients = [None] * layers
    for layer_index in reversed(range(layers)):
        field_now = stored[layer_index]
        grad_term = jnp.sum(conj_times(field_now, backward), axis=1)
        lighting = jnp.sum(field_now[0] ** 2 + field_now[1] ** 2, axis=0)
        gradients[layer_index] = jnp.concatenate([grad_term, lighting[None]], axis=0)
        if layer_index > 0:
            backward = propagate(conj_times(transmit[layer_index][:, None], backward), -1.0)
    return jnp.stack(gradients)


def extend_tile(current, rim_width):
    below_rim = from_behind(current[:, :, :rim_width, :], "tx", -1)
    taller = jnp.concatenate([current, below_rim], axis=2)
    right_rim = from_behind(taller[:, :, :, :rim_width], "ty", -1)
    return jnp.concatenate([taller, right_rim], axis=3)


def return_rims(accumulated, tile_side, rim_width):
    spilled = from_behind(accumulated[:, :, :, tile_side:], "ty", 1)
    narrowed = accumulated[:, :, :, :tile_side].at[:, :, :, :rim_width].add(spilled)
    lower_rim = from_behind(narrowed[:, :, tile_side:, :], "tx", 1)
    return narrowed[:, :, :tile_side, :].at[:, :, :rim_width, :].add(lower_rim)


def on_device(object_slices, probe_modes, corners, measured):
    layers = object_slices.shape[0]
    tile_side = object_slices.shape[2]
    pixels = probe_modes.shape[-1]
    rim_width = pixels // 2
    positions = corners.shape[2]
    pixel_index = jnp.arange(pixels, dtype=jnp.int32)
    angles = (pixel_index[:, None] * pixel_index[None, :] % pixels).astype(jnp.float32) * (
        2.0 * math.pi / pixels
    )
    cosine_table = jnp.cos(angles) / math.sqrt(pixels)
    sine_table = jnp.sin(angles) / math.sqrt(pixels)
    current = object_slices
    extended = extend_tile(current, rim_width)

    def visit(position, accumulated):
        row_start = corners[0, 0, position, 0]
        col_start = corners[0, 0, position, 1]
        grad_terms = position_terms(
            extended,
            probe_modes,
            row_start,
            col_start,
            measured[0, 0, position],
            cosine_table,
            sine_table,
        )
        updated = (
            lax.dynamic_slice(accumulated, (0, 0, row_start, col_start), grad_terms.shape)
            + grad_terms
        )
        return lax.dynamic_update_slice(accumulated, updated, (0, 0, row_start, col_start))

    initial = jnp.zeros((layers, 3, tile_side + rim_width, tile_side + rim_width), jnp.float32)
    accumulated = lax.fori_loop(0, positions, visit, initial)
    totals = lax.psum(accumulated, "scan")
    summed = return_rims(totals, tile_side, rim_width)
    current = current - step_size * summed[:, :2] / (summed[:, 2:3] + 1.0)
    return current


def solution(mesh):
    placed = (
        P(None, None, "tx", "ty"),
        P(),
        P("tx", "ty", "scan", None),
        P("tx", "ty", "scan", None, None),
    )
    return jax.shard_map(
        on_device, mesh=mesh, in_specs=placed, out_specs=P(None, None, "tx", "ty"), check_vma=False
    )
```

profile of v0, /device:TPU:34, one launch (start us, length us, event | category | flops | bytes accessed | tf_op | source)
XLA Modules:
  0.0 380.1 jit_solution(17187173089697609395)
XLA Ops:
  6.5 1.1 slice.282
  7.6 2.4 collective-permute-start
  10.1 1.3 constant_dynamic-update-slice_fusion.1
  11.4 11.8 %collective-permute-done = f32[2,2,128,256]{3,2,1,0:T(8,128)S(1)} collective-permute-done((f32[2,2,128,256]{3,2,1,0:T(8,128)S(1)}, f32[2,2,128,256]{3,2,1,0:T(8,128)S(1)}, u32[]{:S(2)}, u32[]{:S(2)}) %collective-permute-start) | collective-permute-done | bytes 524320 | tf_op jit(solution)/shard_map/ppermute | solution.py:16
  23.2 0.1 slice.323
  23.3 2.1 collective-permute-start.1
  25.4 0.6 fusion.197
  29.9 11.3 %collective-permute-done.1 = f32[2,2,384,128]{3,2,1,0:T(8,128)S(1)} collective-permute-done((f32[2,2,384,128]{3,2,1,0:T(8,128)S(1)}, f32[2,2,384,128]{3,2,1,0:T(8,128)S(1)}, u32[]{:S(2)}, u32[]{:S(2)}) %collective-permute-start.1) | collective-permute-done | bytes 786464 | tf_op jit(solution)/shard_map/ppermute | solution.py:16
  41.2 0.6 fusion.75
  41.8 0.0 copy-start
  41.9 0.4 fusion.80
  42.2 0.1 slice_bitcast_fusion.10
  42.3 1.7 copy-done
  44.0 0.6 multiply_subtract_fusion.2
  44.6 0.3 pad_maximum_fusion
  44.9 2.9 fusion.3
  47.8 2.9 fusion.7
  50.7 1.7 add_reduce_fusion
  52.4 4.6 %fusion.82 = f32[8,256,256]{2,1,0:T(8,128)S(1)} fusion(f32[8,256,256]{2,1,0:T(8,128)S(1)} %get-tuple-element.78, f32[8,256,256]{2,1,0:T(8,128)S(1)} %get-tuple-element.77, f32[256,256]{1,0:T(8,128)S(1)} %get-tuple-element.89, f32[256,256]{1,0:T(8,128)S(1)} %get-tuple-element.98), kind=kOutput, calls=%fused_computation.138 | convolution fusion | flops 1613168640 | bytes 6815744 | tf_op jit(solution)/shard_map/while/body/eval_jaxpr/yk,mkx->myx/dot_general | solution.py:52
  57.0 4.6 %fusion.83 = f32[8,256,256]{2,1,0:T(8,128)S(1)} fusion(f32[8,256,256]{2,1,0:T(8,128)S(1)} %get-tuple-element.78, f32[8,256,256]{2,1,0:T(8,128)S(1)} %get-tuple-element.77, f32[256,256]{1,0:T(8,128)S(1)} %get-tuple-element.89, f32[256,256]{1,0:T(8,128)S(1)} %get-tuple-element.98), kind=kOutput, calls=%fused_computation.139 | convolution fusion | flops 1613168640 | bytes 6815744 | tf_op jit(solution)/shard_map/while/body/eval_jaxpr/yk,mkx->myx/dot_general | solution.py:52
  61.6 4.8 %convolution_add_fusion = f32[8,256,256]{2,1,0:T(8,128)S(1)} fusion(f32[8,256,256]{2,1,0:T(8,128)S(1)} %fusion.83, f32[8,256,256]{2,1,0:T(8,128)S(1)} %get-tuple-element.78, f32[8,256,256]{2,1,0:T(8,128)S(1)} %get-tuple-element.77, f32[256,256]{1,0:T(8,128)S(1)} %get-tuple-element.89, f32[256,256]{1,0:T(8,128)S(1)} %get-tuple-element.98), kind=kOutput, calls=%fused_computation.121 | convolution fusion | flops 1613758464 | bytes 8912896 | tf_op jit(solution)/shard_map/while/body/eval_jaxpr/yk,mkx->myx/dot_general | solution.py:52
  66.4 4.5 %fusion.42 = f32[8,256,256]{2,1,0:T(8,128)S(1)} fusion(f32[8,256,256]{2,1,0:T(8,128)S(1)} %convolution_add_fusion), kind=kOutput, calls=%fused_computation.77 | convolution fusion | flops 1611661312 | bytes 4194304 | tf_op jit(solution)/shard_map/while/body/eval_jaxpr/myk,kx->myx/dot_general | solution.py:56
  70.9 4.5 %fusion.40 = f32[8,256,256]{2,1,0:T(8,128)S(1)} fusion(f32[8,256,256]{2,1,0:T(8,128)S(1)} %convolution_add_fusion), kind=kOutput, calls=%fused_computation.75 | convolution fusion | flops 1611595776 | bytes 4194304 | tf_op jit(solution)/shard_map/while/body/eval_jaxpr/myk,kx->myx/dot_general | solution.py:56
  75.4 5.0 %convolution_subtract_fusion = f32[8,256,256]{2,1,0:T(8,128)S(1)} fusion(f32[8,256,256]{2,1,0:T(8,128)S(1)} %fusion.82, f32[8,256,256]{2,1,0:T(8,128)S(1)} %get-tuple-element.78, f32[8,256,256]{2,1,0:T(8,128)S(1)} %get-tuple-element.77, f32[256,256]{1,0:T(8,128)S(1)} %get-tuple-element.89, f32[256,256]{1,0:T(8,128)S(1)} %get-tuple-element.98), kind=kOutput, calls=%fused_computation.122 | convolution fusion | flops 1613758464 | bytes 8912896 | tf_op jit(solution)/shard_map/while/body/eval_jaxpr/yk,mkx->myx/dot_general | solution.py:52
  80.4 4.5 %fusion.62 = f32[8,256,256]{2,1,0:T(8,128)S(1)} fusion(f32[8,256,256]{2,1,0:T(8,128)S(1)} %fusion.42, f32[8,256,256]{2,1,0:T(8,128)S(1)} %convolution_subtract_fusion), kind=kOutput, calls=%fused_computation.117 | convolution fusion | flops 1612120064 | bytes 6291456 | tf_op jit(solution)/shard_map/while/body/eval_jaxpr/myk,kx->myx/dot_general | solution.py:56
  84.9 0.0 copy-start.7
  84.9 4.6 %add_reduce_fusion.1 = (f32[256,256]{1,0:T(8,128)S(1)}, f32[8,256,256]{2,1,0:T(8,128)S(1)}) fusion(f32[8,256,256]{2,1,0:T(8,128)S(1)} %fusion.62, f32[8,256,256]{2,1,0:T(8,128)S(1)} %fusion.40, f32[8,256,256]{2,1,0:T(8,128)S(1)} %convolution_subtract_fusion), kind=kOutput, calls=%fused_computation.106 | convolution fusion | flops 1614217216 | bytes 8650752 | tf_op jit(solution)/shard_map/while/body/eval_jaxpr/myk,kx->myx/dot_general | solution.py:56
  89.6 0.5 maximum_multiply_fusion
  90.1 4.3 %fusion.57 = f32[8,256,256]{2,1,0:T(8,128)S(1)} fusion(f32[2,8,256,256]{3,2,1,0:T(8,128)S(1)} %maximum_multiply_fusion), kind=kOutput, calls=%fused_computation.112 | convolution fusion | flops 1611595776 | bytes 4194304 | tf_op jit(solution)/shard_map/while/body/eval_jaxpr/yk,mkx->myx/dot_general | solution.py:52
  94.4 4.3 %fusion.56 = f32[8,256,256]{2,1,0:T(8,128)S(1)} fusion(f32[2,8,256,256]{3,2,1,0:T(8,128)S(1)} %maximum_multiply_fusion), kind=kOutput, calls=%fused_computation.111 | convolution fusion | flops 1611595776 | bytes 4194304 | tf_op jit(solution)/shard_map/while/body/eval_jaxpr/yk,mkx->myx/dot_general | solution.py:52
  98.7 4.5 %fusion.61 = f32[8,256,256]{2,1,0:T(8,128)S(1)} fusion(f32[8,256,256]{2,1,0:T(8,128)S(1)} %fusion.56, f32[2,8,256,256]{3,2,1,0:T(8,128)S(1)} %maximum_multiply_fusion), kind=kOutput, calls=%fused_computation.116 | convolution fusion | flops 1612120064 | bytes 6291456 | tf_op jit(solution)/shard_map/while/body/eval_jaxpr/yk,mkx->myx/dot_general | solution.py:52
  103.2 4.3 %fusion.34 = f32[8,256,256]{2,1,0:T(8,128)S(1)} fusion(f32[8,256,256]{2,1,0:T(8,128)S(1)} %fusion.61), kind=kOutput, calls=%fused_computation.69 | convolution fusion | flops 1611595776 | bytes 4194304 | tf_op jit(solution)/shard_map/while/body/eval_jaxpr/myk,kx->myx/dot_general | solution.py:56
  107.5 4.3 %fusion.32 = f32[8,256,256]{2,1,0:T(8,128)S(1)} fusion(f32[8,256,256]{2,1,0:T(8,128)S(1)} %fusion.61), kind=kOutput, calls=%fused_computation.67 | convolution fusion | flops 1611595776 | bytes 4194304 | tf_op jit(solution)/shard_map/while/body/eval_jaxpr/myk,kx->myx/dot_general | solution.py:56
  111.8 4.7 %fusion.60 = f32[8,256,256]{2,1,0:T(8,128)S(1)} fusion(f32[8,256,256]{2,1,0:T(8,128)S(1)} %fusion.57, f32[2,8,256,256]{3,2,1,0:T(8,128)S(1)} %maximum_multiply_fusion), kind=kOutput, calls=%fused_computation.115 | convolution fusion | flops 1612120064 | bytes 6291456 | tf_op jit(solution)/shard_map/while/body/eval_jaxpr/yk,mkx->myx/dot_general | solution.py:52
  116.5 4.4 %fusion.68 = f32[8,256,256]{2,1,0:T(8,128)S(1)} fusion(f32[8,256,256]{2,1,0:T(8,128)S(1)} %fusion.34, f32[8,256,256]{2,1,0:T(8,128)S(1)} %fusion.60), kind=kOutput, calls=%fused_computation.119 | convolution fusion | flops 1612120064 | bytes 6291456 | tf_op jit(solution)/shard_map/while/body/eval_jaxpr/myk,kx->myx/dot_general | solution.py:56
  121.0 4.5 %fusion.71 = f32[8,256,256]{2,1,0:T(8,128)S(1)} fusion(f32[8,256,256]{2,1,0:T(8,128)S(1)} %fusion.32, f32[8,256,256]{2,1,0:T(8,128)S(1)} %fusion.60), kind=kOutput, calls=%fused_computation.120 | convolution fusion | flops 1612120064 | bytes 6291456 | tf_op jit(solution)/shard_map/while/body/eval_jaxpr/myk,kx->myx/dot_general | solution.py:56
  125.5 0.6 fusion.84
  126.0 0.4 pad_maximum_fusion.1
  126.4 3.1 fusion.11
  129.5 2.9 fusion.15
  132.4 5.0 %fusion.51 = (f32[1,8,256,256]{3,2,1,0:T(8,128)}, f32[8,256,256]{2,1,0:T(8,128)}, f32[8,256,256]{2,1,0:T(8,128)}, f32[1,8,256,256]{3,2,1,0:T(8,128)}, f32[1,8,256,256]{3,2,1,0:T(8,128)}) fusion(f32[2,8,256,256]{3,2,1,0:T(8,128)S(1)} %copy-done, f32[2,8,256,256]{3,2,1,0:T(8,128)S(1)} %fusion.15, f32[2,8,256,256]{3,2,1,0:T(8,128)S(1)} %fusion.11, ...), kind=kLoop, calls=%fused_computation.91 | loop fusion | flops 12058624 | bytes 31981568 | tf_op jit(solution)/shard_map/while/body/eval_jaxpr/stack | solution.py:48
  137.4 3.1 fusion.53
  140.6 0.3 maximum_reduce_fusion
  140.8 0.1 maximum_bitcast_fusion
  140.9 1.2 copy-done.3
  142.1 0.6 copy-done.4
  142.8 0.3 maximum_reduce_fusion.1
  143.0 0.1 maximum_bitcast_fusion.1
  143.1 1.3 pad_maximum_fusion.2
  144.4 0.2 broadcast_in_dim.15
  144.6 22.3 %dynamic_update_slice.4 = f32[2,3,384,384]{3,2,1,0:T(8,128)S(1)} dynamic-update-slice(f32[2,3,384,384]{3,2,1,0:T(8,128)S(1)} %broadcast_in_dim.15, f32[2,3,256,256]{3,2,1,0:T(8,128)} %pad_maximum_fusion.2, s32[]{:T(128)} %constant.149.clone.1, s32[]{:T(128)} %constant.149.clone.1, s32[]{:T(128)S(6)} %select_n.57, s32[]{:T(128)S(6)} %select_n.59) | dynamic-update-slice | bytes 3145732 | tf_op jit(solution)/shard_map/while/body/eval_jaxpr/dynamic_update_slice | solution.py:141
  166.9 1.8 copy-done.1
  168.7 0.0 all-reduce.6.cloned.1.call-update
  168.7 152.7 %all-reduce.6.cloned.1.call-done = f32[2,3,384,384]{3,2,1,0:T(8,128)} async-done(((f32[2,3,384,384]{3,2,1,0:T(8,128)}), f32[2,3,384,384]{3,2,1,0:T(8,128)}) %all-reduce.6.cloned.1.call-update) | async-done | bytes 3538960 | tf_op jit(solution)/shard_map/psum | solution.py:145
  321.4 1.5 slice.340
  322.9 1.4 collective-permute-start.2
  324.3 27.7 %collective-permute-done.2 = f32[2,3,384,128]{3,2,1,0:T(8,128)S(1)} collective-permute-done((f32[2,3,384,128]{3,2,1,0:T(8,128)S(1)}, f32[2,3,384,128]{3,2,1,0:T(8,128)S(1)}, u32[]{:S(2)}, u32[]{:S(2)}) %collective-permute-start.2) | collective-permute-done | bytes 1179680 | tf_op jit(solution)/shard_map/ppermute | solution.py:16
  352.0 0.1 fusion.74
  352.1 0.1 slice.343
  352.2 3.4 collective-permute-start.3
  355.6 0.2 slice.341
  355.7 16.0 %collective-permute-done.3 = f32[2,3,128,256]{3,2,1,0:T(8,128)S(1)} collective-permute-done((f32[2,3,128,256]{3,2,1,0:T(8,128)S(1)}, f32[2,3,128,256]{3,2,1,0:T(8,128)S(1)}, u32[]{:S(2)}, u32[]{:S(2)}) %collective-permute-start.3) | collective-permute-done | bytes 786464 | tf_op jit(solution)/shard_map/ppermute | solution.py:16
  371.8 0.1 fusion.78
  372.0 1.1 fusion.77
  (18 shorter events, 0.1 us)
Async XLA Ops:
  6.5 314.8 %all-reduce.6.cloned.1.call-start = ((), (), s32[]{:S(2)}) async-start(), calls=%async_computation | async-start | bytes 7077888 | tf_op jit(solution)/shard_map/psum | solution.py:145
  7.6 17.7 %copy-start.8 = (s32[1,1,1,2]{3,2,1,0:T(1,128)S(1)}, s32[1,1,1,2]{3,2,1,0:T(1,128)}, u32[]{:S(2)}) copy-start(s32[1,1,1,2]{3,2,1,0:T(1,128)} %param.12) | copy-start | bytes 28
  7.6 15.6 %collective-permute-start = (f32[2,2,128,256]{3,2,1,0:T(8,128)S(1)}, f32[2,2,128,256]{3,2,1,0:T(8,128)S(1)}, u32[]{:S(2)}, u32[]{:S(2)}) collective-permute-start(f32[2,2,128,256]{3,2,1,0:T(8,128)S(1)} %slice.282), channel_id=1, source_target_pairs={{2,0},{4,2},{6,4},{3,1},{5,3},{7,5},{10,8},{12,10},{14,12},{11,9},... | collective-permute-start | bytes 1572872 | tf_op jit(solution)/shard_map/ppermute | solution.py:16
  23.3 17.9 %collective-permute-start.1 = (f32[2,2,384,128]{3,2,1,0:T(8,128)S(1)}, f32[2,2,384,128]{3,2,1,0:T(8,128)S(1)}, u32[]{:S(2)}, u32[]{:S(2)}) collective-permute-start(f32[2,2,384,128]{3,2,1,0:T(8,128)S(1)} %slice.323), channel_id=1, source_target_pairs={{1,0},{3,2},{5,4},{7,6},{9,8},{11,10},{13,12},{15,14},{17,16},{19,... | collective-permute-start | bytes 2359304 | tf_op jit(solution)/shard_map/ppermute | solution.py:16
  41.8 2.2 copy-start
  84.9 4.7 %copy-start.7 = (f32[1,1,1,256,256]{4,3,2,1,0:T(8,128)S(1)}, f32[1,1,1,256,256]{4,3,2,1,0:T(8,128)}, u32[]{:S(2)}) copy-start(f32[1,1,1,256,256]{4,3,2,1,0:T(8,128)} %param.13) | copy-start | bytes 786436
  137.4 3.1 copy-start.5
  140.5 1.6 copy-start.3
  140.6 2.2 copy-start.4
  166.9 1.8 copy-start.1
  321.4 30.6 %copy-start.2 = (f32[2,3,384,384]{3,2,1,0:T(8,128)S(1)}, f32[2,3,384,384]{3,2,1,0:T(8,128)}, u32[]{:S(2)}) copy-start(f32[2,3,384,384]{3,2,1,0:T(8,128)} %all-reduce.6.cloned.1.call-done) | copy-start | bytes 10616836
  322.9 29.1 %slice-start = ((f32[2,3,384,384]{3,2,1,0:T(8,128)}), f32[2,3,384,256]{3,2,1,0:T(8,128)S(1)}, s32[]{:S(2)}) async-start(f32[2,3,384,384]{3,2,1,0:T(8,128)} %all-reduce.6.cloned.1.call-done), calls=%async_computation.1 | async-start | bytes 4718592 | tf_op jit(solution)/shard_map/slice | solution.py:105
  322.9 29.1 %collective-permute-start.2 = (f32[2,3,384,128]{3,2,1,0:T(8,128)S(1)}, f32[2,3,384,128]{3,2,1,0:T(8,128)S(1)}, u32[]{:S(2)}, u32[]{:S(2)}) collective-permute-start(f32[2,3,384,128]{3,2,1,0:T(8,128)S(1)} %slice.340), channel_id=1, source_target_pairs={{0,1},{2,3},{4,5},{6,7},{8,9},{10,11},{12,13},{14,15},{16,17},{18,... | collective-permute-start | bytes 3538952 | tf_op jit(solution)/shard_map/ppermute | solution.py:16
  352.2 19.6 %collective-permute-start.3 = (f32[2,3,128,256]{3,2,1,0:T(8,128)S(1)}, f32[2,3,128,256]{3,2,1,0:T(8,128)S(1)}, u32[]{:S(2)}, u32[]{:S(2)}) collective-permute-start(f32[2,3,128,256]{3,2,1,0:T(8,128)S(1)} %slice.343), channel_id=1, source_target_pairs={{0,2},{2,4},{4,6},{1,3},{3,5},{5,7},{8,10},{10,12},{12,14},{9,11},... | collective-permute-start | bytes 2359304 | tf_op jit(solution)/shard_map/ppermute | solution.py:16
  355.7 16.2 %copy-start.6 = (f32[2,2,256,256]{3,2,1,0:T(8,128)S(1)}, f32[2,2,256,256]{3,2,1,0:T(8,128)}, u32[]{:S(2)}) copy-start(f32[2,2,256,256]{3,2,1,0:T(8,128)} %param.10) | copy-start | bytes 3145732
Sparse Core Ops, SparseCore 0:
  168.8 152.4 all-reduce.5
where the time goes:
time: 385 us; the launch traced here: 380 us
  waiting for transfers between devices  219 us (57%)
  matrix products  72.3 us (19%)
  local copies, waits for them, and re-layouts  32.8 us (9%)
  other arithmetic  28.2 us (7%)
  between operations  18 us (5%)
  starting transfers between devices  9.31 us (2%)
    psum x1, waiting for transfers between devices, on_device(): totals = lax.psum(accumulated, 'scan')  153 us
    ppermute x4, waiting for transfers between devices, from_behind(): return lax.ppermute(array, axis, pairs)  66.8 us
    dot_general x8, matrix products, left_apply(): return jnp.einsum('yk,mkx->myx', table, field, precision=precise)  36.7 us
    dot_general x8, matrix products, right_apply(): return jnp.einsum('myk,kx->myx', field, table, precision=precise)  35.7 us
    dynamic_update_slice x1, local copies, waits for them, and re-layouts, visit(): lax.dynamic_update_slice(accumulated, updated, (0, 0, row_start, col_start))  22.3 us
    sub x4, other arithmetic, laplacian(): padded[:, :, :-2, 1:-1] + padded[:, :, 2:, 1:-1] + padded[:, :, 1:-1, :-2]  11.8 us
    ppermute x4, starting transfers between devices, from_behind(): return lax.ppermute(array, axis, pairs)  9.31 us
    another operation x4, other arithmetic, conj_times(): return jnp.stack([real_part, imag_part])  9.05 us
  transfers between devices with their start and end apart: 5, of which 5 were waited for; matrix products, arithmetic and copies ran while one was open for 1% of the time, Pallas kernels for 0%

commit v1 on v0

v1 whole, which is shorter than its diff:
```python
import functools
import math

import jax
import jax.numpy as jnp
import numpy as np
from jax import lax
from jax.experimental import pallas as pl
from jax.experimental.pallas import tpu as pltpu
from jax.sharding import PartitionSpec as P

fresnel_coef = 0.1
step_size = 4.0
SIDE = 256
HALF = 128
LAYERS = 2
SCANS = 16
STEPS = 32
f32 = jnp.float32
bf16 = jnp.bfloat16


def real_right(table):
    return np.block([[table.real, table.imag], [-table.imag, table.real]])


def real_left(table):
    return np.block([[table.real, -table.imag], [table.imag, table.real]])


def two_parts(table):
    high = table.astype(np.float32).astype(bf16)
    low = (table - high.astype(np.float64)).astype(np.float32).astype(bf16)
    return np.stack([high, low])


def make_tables():
    half = np.arange(HALF)
    col_even = np.exp(-2j * np.pi * np.outer(half, half) / HALF) / 16
    col_odd = np.exp(-2j * np.pi * np.outer(half, 2 * half + 1) / SIDE) / 16
    place = 16 * (half % 8) + half // 8
    row_even = np.exp(-2j * np.pi * np.outer(half, place) / HALF) / 16
    row_odd = np.exp(-2j * np.pi * np.outer(half, 2 * place + 1) / SIDE) / 16
    right = [col_even, col_odd, col_even.conj().T, col_odd.conj().T]
    left = [row_even, row_odd, row_even.conj().T, row_odd.conj().T]
    right = np.stack([two_parts(real_right(t)) for t in right])
    left = np.stack([two_parts(real_left(t)) for t in left])
    order = np.zeros((SIDE, SIDE), np.float32)
    order[2 * half, half] = 1.0
    order[2 * half + 1, half + HALF] = 1.0
    return right, left, order.astype(bf16)


def split(value):
    high = value.astype(bf16)
    return high, (value - high.astype(f32)).astype(bf16)


def mul(first, second):
    return jnp.dot(first, second, preferred_element_type=f32)


def right_dot(value, table, which):
    high, low = split(value)
    return (
        mul(high, table[which, 0]) + mul(low, table[which, 0]) + mul(high, table[which, 1])
    )


def left_dot(table, which, value):
    high, low = split(value)
    return (
        mul(table[which, 0], high) + mul(table[which, 0], low) + mul(table[which, 1], high)
    )


def neighbours(v):
    column = lax.broadcasted_iota(jnp.int32, v.shape, 2)
    sub = lax.broadcasted_iota(jnp.int32, (1, 8, SIDE), 1)
    left = jnp.where(column == 0, 0.0, pltpu.roll(v, 1, 2))
    right = jnp.where(column == SIDE - 1, 0.0, pltpu.roll(v, SIDE - 1, 2))
    first = jnp.where(sub == 0, 0.0, pltpu.roll(v[-1:], 1, 1))
    last = jnp.where(sub == 7, 0.0, pltpu.roll(v[:1], 7, 1))
    up = jnp.concatenate([first, v[:-1]], axis=0)
    down = jnp.concatenate([v[1:], last], axis=0)
    return (left + right) + (up + down)


def propagate(re, im, sign):
    damping = 0.5 * fresnel_coef**2
    turn = sign * fresnel_coef
    q_re = 4.0 * damping * re - turn * im - damping * neighbours(re)
    q_im = 4.0 * damping * im + turn * re - damping * neighbours(im)
    return (re - 4.0 * q_re) + neighbours(q_re), (im - 4.0 * q_im) + neighbours(q_im)


def load_rows(ref, lead):
    pick = lambda h, t: ref[lead + (h, pl.ds(t, 8, stride=STEPS), slice(None))]
    return jnp.stack(
        [jnp.concatenate([pick(0, t), pick(1, t)], axis=1) for t in range(STEPS)], axis=0
    )


def store_rows(ref, value):
    for h in range(2):
        for t in range(STEPS):
            ref[h, pl.ds(t, 8, stride=STEPS), :] = value[t, :, h * HALF : (h + 1) * HALF]


def probe_copies(probe_ref, probe, sems, m):
    return [
        pltpu.make_async_copy(
            probe_ref.at[p, m, :, pl.ds(h * HALF, HALF)], probe.at[p, m, h], sems.at[p, m, h]
        )
        for p in range(2)
        for h in range(2)
    ]


def wave_kernel(
    corner_ref,
    own_ref,
    below_ref,
    right_ref,
    diag_ref,
    probe_ref,
    measured_ref,
    col_tab,
    row_tab,
    order_ref,
    out_ref,
    light_ref,
    hold,
    trans,
    wave,
    far,
    misfit,
    total,
    probe_light,
    probe,
    sems,
):
    r, c = corner_ref[0], corner_ref[1]
    modes = probe_ref.shape[1]
    for m in range(modes):
        for copy in probe_copies(probe_ref, probe, sems, m):
            copy.start()
    rows = lax.broadcasted_iota(jnp.int32, (SIDE, SIDE), 0)
    cols = lax.broadcasted_iota(jnp.int32, (SIDE, SIDE), 1)
    top = rows[:HALF] < r
    near = cols[:, :HALF] < c
    back_r = lax.rem(SIDE - r, SIDE)
    back_c = lax.rem(SIDE - c, SIDE)
    for s in range(LAYERS):
        for p in range(2):
            left = jnp.where(near, right_ref[s, p], own_ref[s, p, :, :HALF])
            whole = jnp.concatenate([left, own_ref[s, p, :, HALF:]], axis=1)
            lower = jnp.concatenate(
                [
                    jnp.where(near[:HALF], diag_ref[s, p], below_ref[s, p, :, :HALF]),
                    below_ref[s, p, :, HALF:],
                ],
                axis=1,
            )
            whole = jnp.concatenate([jnp.where(top, lower, whole[:HALF]), whole[HALF:]], axis=0)
            whole = pltpu.roll(pltpu.roll(whole, back_c, 1), back_r, 0)
            hold[0] = whole[:, :HALF]
            hold[1] = whole[:, HALF:]
            view = load_rows(hold, ())
            trans[s, p] = view + 1.0 if p == 0 else view

    inten = measured_ref[...]
    high, low = split(inten)
    rest = (inten - high.astype(f32) - low.astype(f32)).astype(bf16)
    order = order_ref[...]
    misfit[...] = -(mul(high, order) + mul(low, order) + mul(rest, order))
    total[...] = jnp.zeros_like(total)
    probe_light[...] = jnp.zeros_like(probe_light)

    def forward(m, carry):
        for copy in probe_copies(probe_ref, probe, sems, m):
            copy.wait()
        p_re, p_im = load_rows(probe, (0, m)), load_rows(probe, (1, m))
        probe_light[...] += p_re * p_re + p_im * p_im
        t_re, t_im = trans[0, 0], trans[0, 1]
        w_re, w_im = propagate(p_re * t_re - p_im * t_im, p_re * t_im + p_im * t_re, 1.0)
        wave[0, m] = w_re
        wave[1, m] = w_im
        total[2] += w_re * w_re + w_im * w_im
        t_re, t_im = trans[1, 0], trans[1, 1]
        x_re = (w_re * t_re - w_im * t_im).reshape(SIDE, SIDE)
        x_im = (w_re * t_im + w_im * t_re).reshape(SIDE, SIDE)
        even = jnp.concatenate(
            [x_re[:, :HALF] + x_re[:, HALF:], x_im[:, :HALF] + x_im[:, HALF:]], axis=1
        )
        odd = jnp.concatenate(
            [x_re[:, :HALF] - x_re[:, HALF:], x_im[:, :HALF] - x_im[:, HALF:]], axis=1
        )
        even = right_dot(even, col_tab, 0)
        odd = right_dot(odd, col_tab, 1)
        y_re = jnp.concatenate([even[:, :HALF], odd[:, :HALF]], axis=1).reshape(16, 2, 8, SIDE)
        y_im = jnp.concatenate([even[:, HALF:], odd[:, HALF:]], axis=1).reshape(16, 2, 8, SIDE)
        pick = lambda e: jnp.concatenate([y_re[:, e], y_im[:, e]], axis=0).reshape(SIDE, SIDE)
        first = left_dot(row_tab, 0, pick(0))
        second = left_dot(row_tab, 1, pick(1))
        upper, lower = first + second, first - second
        far[m, 0] = upper
        far[m, 1] = lower
        misfit[:HALF] += upper[:HALF] * upper[:HALF] + upper[HALF:] * upper[HALF:]
        misfit[HALF:] += lower[:HALF] * lower[:HALF] + lower[HALF:] * lower[HALF:]
        return carry

    lax.fori_loop(0, modes, forward, 0)
    misfit[...] = 2.0 * misfit[...]

    def backward(m, carry):
        twice = lambda a: jnp.concatenate([a, a], axis=0)
        upper = twice(misfit[:HALF]) * far[m, 0]
        lower = twice(misfit[HALF:]) * far[m, 1]
        even = left_dot(row_tab, 2, upper + lower)
        odd = left_dot(row_tab, 3, upper - lower)
        join = lambda lanes: jnp.concatenate(
            [
                jnp.concatenate([even[:HALF, lanes], even[HALF:, lanes]], axis=1),
                jnp.concatenate([odd[:HALF, lanes], odd[HALF:, lanes]], axis=1),
            ],
            axis=0,
        )
        first = right_dot(join(slice(0, HALF)), col_tab, 2)
        second = right_dot(join(slice(HALF, SIDE)), col_tab, 3)
        plus, minus = first + second, first - second

        def weave(a):
            a = a.reshape(2, 16, 8, SIDE)
            return jnp.stack([a[0], a[1]], axis=1).reshape(STEPS, 8, SIDE)

        b_re = weave(jnp.concatenate([plus[:, :HALF], minus[:, :HALF]], axis=1))
        b_im = weave(jnp.concatenate([plus[:, HALF:], minus[:, HALF:]], axis=1))
        w_re, w_im = wave[0, m], wave[1, m]
        total[0] += w_re * b_re + w_im * b_im
        total[1] += w_re * b_im - w_im * b_re
        t_re, t_im = trans[1, 0], trans[1, 1]
        d_re, d_im = propagate(t_re * b_re + t_im * b_im, t_re * b_im - t_im * b_re, -1.0)
        p_re, p_im = load_rows(probe, (0, m)), load_rows(probe, (1, m))
        total[3] += p_re * d_re + p_im * d_im
        total[4] += p_re * d_im - p_im * d_re
        return carry

    lax.fori_loop(0, modes, backward, 0)

    for k in range(5):
        store_rows(hold, total[k])
        whole = jnp.concatenate([hold[0], hold[1]], axis=1)
        moved = pltpu.roll(pltpu.roll(whole, c, 1), r, 0).reshape(2, 16, 8, SIDE)
        out_ref[:, k, 0] = moved[0]
        out_ref[:, k, 1] = moved[1]
    store_rows(hold, probe_light[...])
    for h in range(2):
        for half in range(2):
            light_ref[half * SIDE : (half + 1) * SIDE, h * HALF : (h + 1) * HALF] = hold[h]


def run_wave(corner, own, below, right, diag, probe, measured):
    right_table, left_table, order = make_tables()
    modes = probe.shape[1]
    vmem = pl.BlockSpec(memory_space=pltpu.VMEM)
    field = (STEPS, 8, SIDE)
    return pl.pallas_call(
        wave_kernel,
        out_shape=(
            jax.ShapeDtypeStruct((SCANS, 5, 2, 8, SIDE), f32),
            jax.ShapeDtypeStruct((2 * SIDE, SIDE), f32),
        ),
        in_specs=[pl.BlockSpec(memory_space=pltpu.SMEM)]
        + [vmem] * 4
        + [pl.BlockSpec(memory_space=pl.ANY)]
        + [vmem] * 4,
        out_specs=(vmem, vmem),
        scratch_shapes=[
            pltpu.VMEM((2, SIDE, HALF), f32),
            pltpu.VMEM((LAYERS, 2) + field, f32),
            pltpu.VMEM((2, modes) + field, f32),
            pltpu.VMEM((modes, 2, SIDE, SIDE), f32),
            pltpu.VMEM((SIDE, SIDE), f32),
            pltpu.VMEM((5,) + field, f32),
            pltpu.VMEM(field, f32),
            pltpu.VMEM((2, modes, 2, SIDE, HALF), f32),
            pltpu.SemaphoreType.DMA((2, modes, 2)),
        ],
        compiler_params=pltpu.CompilerParams(vmem_limit_bytes=48 * 1024 * 1024),
        name="wave",
    )(
        corner,
        own,
        below,
        right,
        diag,
        probe,
        measured,
        jnp.asarray(right_table),
        jnp.asarray(left_table),
        jnp.asarray(order),
    )


def sum_kernel(me_ref, corners_ref, parts_ref, light_ref, own_ref, right_ref, below_ref, diag_ref):
    me = me_ref[0]
    own_ref[...] = jnp.zeros_like(own_ref)
    right_ref[...] = jnp.zeros_like(right_ref)
    below_ref[...] = jnp.zeros_like(below_ref)
    diag_ref[...] = jnp.zeros_like(diag_ref)
    sub = lax.broadcasted_iota(jnp.int32, (2, 8, SIDE), 1)
    side = lax.broadcasted_iota(jnp.int32, (2, 8, SIDE), 0)
    cols = lax.broadcasted_iota(jnp.int32, (2, 8, SIDE), 2)
    rows = HALF * side + 8 * me + sub
    for j in range(SCANS):
        r, c = corners_ref[j, 0], corners_ref[j, 1]
        lights = []
        for h in range(2):
            start = lax.rem(HALF * h + 8 * me + SIDE - r, SIDE)
            base = pl.multiple_of((start // 8) * 8, 8)
            block = light_ref[pl.ds(base, 16), :]
            block = pltpu.roll(block, lax.rem(16 - (start - base), 16), 0)[:8]
            lights.append(pltpu.roll(block, c, 1)[None])
        light = jnp.concatenate(lights, axis=0)
        inside_row, inside_col = rows >= r, cols >= c
        for k in range(6):
            value = parts_ref[j, k] if k < 5 else light
            here = jnp.where(inside_row, value, 0.0)
            there = (value - here)[0]
            own_ref[k] += jnp.where(inside_col, here, 0.0)
            right_ref[k] += jnp.where(inside_col, 0.0, here)[:, :, :HALF]
            below_ref[k] += jnp.where(inside_col[0], there, 0.0)
            diag_ref[k] += jnp.where(inside_col[0], 0.0, there)[:, :HALF]


def run_sum(me, corners, parts, light):
    smem = pl.BlockSpec(memory_space=pltpu.SMEM)
    vmem = pl.BlockSpec(memory_space=pltpu.VMEM)
    return pl.pallas_call(
        sum_kernel,
        out_shape=(
            jax.ShapeDtypeStruct((6, 2, 8, SIDE), f32),
            jax.ShapeDtypeStruct((6, 2, 8, HALF), f32),
            jax.ShapeDtypeStruct((6, 8, SIDE), f32),
            jax.ShapeDtypeStruct((6, 8, HALF), f32),
        ),
        in_specs=[smem, smem, vmem, vmem],
        out_specs=(vmem,) * 4,
        name="sum",
    )(me, corners, parts, light)


def update_kernel(me_ref, object_ref, own_ref, right_ref, below_ref, diag_ref, out_ref):
    me = me_ref[0]
    sums = []
    for k in range(6):
        near = own_ref[k, :, :, :HALF] + right_ref[k]
        whole = jnp.concatenate([near, own_ref[k, :, :, HALF:]], axis=2)
        low = jnp.concatenate(
            [below_ref[k, :, :HALF] + diag_ref[k], below_ref[k, :, HALF:]], axis=1
        )
        sums.append([whole[0] + low, whole[1]])
    for s in range(LAYERS):
        base = 3 * (1 - s)
        for h in range(2):
            scale = step_size / (sums[base + 2][h] + 1.0)
            start = pl.multiple_of(HALF * h + 8 * me, 8)
            for p in range(2):
                out_ref[s, p, h] = (
                    object_ref[s, p, pl.ds(start, 8), :] - scale * sums[base + p][h]
                )


def run_update(me, current, own, right, below, diag):
    smem = pl.BlockSpec(memory_space=pltpu.SMEM)
    vmem = pl.BlockSpec(memory_space=pltpu.VMEM)
    return pl.pallas_call(
        update_kernel,
        out_shape=jax.ShapeDtypeStruct((LAYERS, 2, 2, 8, SIDE), f32),
        in_specs=[smem] + [vmem] * 5,
        out_specs=vmem,
        name="update",
    )(me, current, own, right, below, diag)


def place_kernel(me_ref, *refs):
    blocks, out_ref = refs[:-1], refs[-1]
    me = me_ref[0]
    y, z, core = me // 4, lax.rem(me // 2, 2), lax.rem(me, 2)
    count = 0
    for ref in blocks:
        for b in range(ref.shape[0]):
            dc, dy, dz = count // 8, (count // 2) % 4, count % 2
            i = lax.rem(y + 4 - dy, 4) * 4 + lax.rem(z + dz, 2) * 2 + lax.rem(core + dc, 2)
            for h in range(2):
                start = pl.multiple_of(HALF * h + 8 * i, 8)
                out_ref[:, :, pl.ds(start, 8), :] = ref[b, :, :, h]
            count += 1


def run_place(me, blocks):
    vmem = pl.BlockSpec(memory_space=pltpu.VMEM)
    return pl.pallas_call(
        place_kernel,
        out_shape=jax.ShapeDtypeStruct((LAYERS, 2, SIDE, SIDE), f32),
        in_specs=[pl.BlockSpec(memory_space=pltpu.SMEM)] + [vmem] * len(blocks),
        out_specs=vmem,
        name="place",
    )(me, *blocks)


def shift(array, axis, by):
    count = lax.axis_size(axis)
    pairs = [(i, i + by) for i in range(count) if 0 <= i + by < count]
    return lax.ppermute(array, axis, pairs)


def shift_both(array, by):
    n_x, n_y = lax.axis_size("tx"), lax.axis_size("ty")
    pairs = [
        (a * n_y + b, (a + by) * n_y + b + by)
        for a in range(n_x)
        for b in range(n_y)
        if 0 <= a + by < n_x and 0 <= b + by < n_y
    ]
    return lax.ppermute(array, ("tx", "ty"), pairs)


def along_scan(array, dy, dz, dc):
    pairs = []
    for i in range(SCANS):
        y, z, core = i // 4, (i // 2) % 2, i % 2
        pairs.append((i, ((y + dy) % 4) * 4 + ((z + dz) % 2) * 2 + (core + dc) % 2))
    return lax.ppermute(array, "scan", pairs)


def on_device(object_slices, probe_modes, corners, measured):
    me = lax.axis_index("scan").astype(jnp.int32).reshape(1)
    corner = corners.reshape(2)
    below = shift(object_slices[:, :, :HALF, :], "tx", -1)
    right = shift(object_slices[:, :, :, :HALF], "ty", -1)
    diag = shift_both(object_slices[:, :, :HALF, :HALF], -1)
    told = jnp.broadcast_to(jnp.pad(corner, (0, 126))[None, None], (SCANS, 1, 128))
    all_corners = lax.all_to_all(told, "scan", 0, 0)[:, 0, :2]

    parts, light = run_wave(
        corner, object_slices, below, right, diag, probe_modes, measured.reshape(SIDE, SIDE)
    )
    parts = lax.all_to_all(parts, "scan", 0, 0)
    own, to_right, to_below, to_diag = run_sum(me, all_corners, parts, light)
    to_right = shift(to_right, "ty", 1)
    to_below = shift(to_below, "tx", 1)
    to_diag = shift_both(to_diag, 1)
    mine = run_update(me, object_slices, own, to_right, to_below, to_diag)[None]
    pair = jnp.concatenate([mine, along_scan(mine, 0, 1, 0)], axis=0)
    ring = [pair] + [along_scan(pair, dy, 0, 0) for dy in (1, 2, 3)]
    ring = jnp.concatenate(ring, axis=0)
    other = along_scan(ring, 0, 0, 1)
    return run_place(me, [ring, other])


def solution(mesh):
    placed = (
        P(None, None, "tx", "ty"),
        P(),
        P("tx", "ty", "scan", None),
        P("tx", "ty", "scan", None, None),
    )
    return jax.shard_map(
        on_device, mesh=mesh, in_specs=placed, out_specs=P(None, None, "tx", "ty"), check_vma=False
    )
```

time: 385 us -> 126 us (0.33)
  waiting for transfers between devices: 219 us -> 43.9 us
  matrix products: 72.3 us -> 0 us
  Pallas kernels: 0 us -> 37 us
  other arithmetic: 28.2 us -> 0.85 us
  starting transfers between devices: 9.31 us -> 32 us
  local copies, waits for them, and re-layouts: 32.8 us -> 10.3 us
  between operations: 18 us -> 0.19 us
    psum x1 -> x0, waiting for transfers between devices: 153 us -> none  [on_device(): totals = lax.psum(accumulated, 'scan')]
    dot_general x16 -> x0, matrix products: 72.3 us -> none  [the longest x8 36.7 us: left_apply(): return jnp.einsum('yk,mkx->myx', table, field, precision=precise)]
    ppermute x4 -> x11, waiting for transfers between devices: 66.8 us -> 23.1 us  [the longest x5 11.6 us: along_scan(): return lax.ppermute(array, 'scan', pairs)]
    pallas_call x0 -> x4, Pallas kernels: none -> 37 us  [the longest x1 30 us: run_wave(): pl.pallas_call(wave_kernel, out_shape=(jax.ShapeDtypeStruct((SCANS, 5, 2,...]
    dynamic_update_slice x1 -> x0, local copies, waits for them, and re-layouts: 22.3 us -> none  [visit(): lax.dynamic_update_slice(accumulated, updated, (0, 0, row_start, col_start))]
    all_to_all x0 -> x2, waiting for transfers between devices: none -> 20.8 us  [the longest x1 20.8 us: on_device(): parts = lax.all_to_all(parts, 'scan', 0, 0)]
    all_to_all x0 -> x2, starting transfers between devices: none -> 14.9 us  [the longest x1 7.52 us: on_device(): parts = lax.all_to_all(parts, 'scan', 0, 0)]
    sub x6 -> x0, other arithmetic: 13.5 us -> none  [the longest x4 11.8 us: laplacian(): padded[:, :, :-2, 1:-1] + padded[:, :, 2:, 1:-1] + padded[:, :, 1:-1, :-2]]
  transfers between devices with their start and end apart: 5 -> 13, of which waited for: 5 -> 8; matrix products, arithmetic and copies ran while one was open for 1% -> 2% of each run, Pallas kernels for 0% -> 24%
where the time goes in v1:
time: 126 us; the launch traced here: 124 us
  waiting for transfers between devices  43.9 us (35%)
  Pallas kernels  37 us (29%)
  starting transfers between devices  32 us (25%)
  local copies, waits for them, and re-layouts  10.3 us (8%)
    pallas_call x1, Pallas kernels, run_wave(): pl.pallas_call(wave_kernel, out_shape=(jax.ShapeDtypeStruct((SCANS, 5, 2,...  30 us
    all_to_all x1, waiting for transfers between devices, on_device(): parts = lax.all_to_all(parts, 'scan', 0, 0)  20.8 us
    ppermute x5, waiting for transfers between devices, along_scan(): return lax.ppermute(array, 'scan', pairs)  11.6 us
    ppermute x2, waiting for transfers between devices, shift_both(): return lax.ppermute(array, ('tx', 'ty'), pairs)  9.19 us
    ppermute x4, starting transfers between devices, shift(): return lax.ppermute(array, axis, pairs)  9.04 us
    all_to_all x1, starting transfers between devices, on_device(): parts = lax.all_to_all(parts, 'scan', 0, 0)  7.52 us
    all_to_all x1, starting transfers between devices, on_device(): all_corners = lax.all_to_all(told, 'scan', 0, 0)[:, 0, :2]  7.38 us
    unnamed x32, local copies, waits for them, and re-layouts  6.03 us
  transfers between devices with their start and end apart: 13, of which 8 were waited for; matrix products, arithmetic and copies ran while one was open for 2% of the time, Pallas kernels for 24%

profile of v1, /device:TPU:34, one launch (start us, length us, event | category | flops | bytes accessed | tf_op | source)
XLA Modules:
  0.0 124.3 jit_solution(7968128881268180926)
XLA Ops:
  0.0 0.0 copy-start
  0.0 0.0 copy-start.1
  0.0 0.0 copy-start.5
  0.0 0.0 copy-start.6
  0.0 0.0 copy-start.4
  0.0 2.0 %slice.13 = f32[2,2,128,256]{3,2,1,0:T(8,128)} slice(f32[2,2,256,256]{3,2,1,0:T(8,128)} %object_ref.1), slice={[0:2], [0:2], [0:128], [0:256]} | slice | bytes 1048576 | tf_op jit(solution)/shard_map/slice | solution.py:441
  2.1 2.4 %collective-permute-start = (f32[2,2,128,256]{3,2,1,0:T(8,128)}, f32[2,2,128,256]{3,2,1,0:T(8,128)S(1)}, u32[]{:S(2)}, u32[]{:S(2)}) collective-permute-start(f32[2,2,128,256]{3,2,1,0:T(8,128)} %slice.13), channel_id=1, source_target_pairs={{2,0},{4,2},{6,4},{3,1},{5,3},{7,5},{10,8},{12,10},{14,12},{11,9},... | collective-permute-start | bytes 1572872 | tf_op jit(solution)/shard_map/ppermute | solution.py:416
  4.5 0.0 copy-done
  4.5 0.9 slice.14
  5.4 1.9 %collective-permute-start.1 = (f32[2,2,256,128]{3,2,1,0:T(8,128)}, f32[2,2,256,128]{3,2,1,0:T(8,128)S(1)}, u32[]{:S(2)}, u32[]{:S(2)}) collective-permute-start(f32[2,2,256,128]{3,2,1,0:T(8,128)} %slice.14), channel_id=1, source_target_pairs={{1,0},{3,2},{5,4},{7,6},{9,8},{11,10},{13,12},{15,14},{17,16},{19,... | collective-permute-start | bytes 1572872 | tf_op jit(solution)/shard_map/ppermute | solution.py:416
  7.3 0.7 slice.15
  8.0 2.0 %collective-permute-start.2 = (f32[2,2,128,128]{3,2,1,0:T(8,128)}, f32[2,2,128,128]{3,2,1,0:T(8,128)}, u32[]{:S(2)}, u32[]{:S(2)}) collective-permute-start(f32[2,2,128,128]{3,2,1,0:T(8,128)} %slice.15), channel_id=1, source_target_pairs={{3,0},{5,2},{7,4},{11,8},{13,10},{15,12},{19,16},{21,18},{23,20},{... | collective-permute-start | bytes 786440 | tf_op jit(solution)/shard_map/ppermute | solution.py:427
  10.0 0.0 copy-done.6
  10.1 0.6 broadcast_in_dim.4
  10.7 7.4 %all-to-all-start = ((s32[16,1,128]{2,1,0:T(1,128)}), s32[16,1,128]{2,1,0:T(1,128)S(1)}, u32[]{:S(2)}, u32[]{:S(2)}) async-start(s32[16,1,128]{2,1,0:T(1,128)} %broadcast_in_dim.4), calls=%async_computation | async-start | bytes 16384 | tf_op jit(solution)/shard_map/all_to_all | solution.py:445
  18.0 3.7 %collective-permute-done.2.diag_ref = f32[2,2,128,128]{3,2,1,0:T(8,128)} collective-permute-done((f32[2,2,128,128]{3,2,1,0:T(8,128)}, f32[2,2,128,128]{3,2,1,0:T(8,128)}, u32[]{:S(2)}, u32[]{:S(2)}) %collective-permute-start.2) | collective-permute-done | bytes 262176 | tf_op jit(solution)/shard_map/ppermute | solution.py:427
  21.7 0.0 collective-permute-done.below_ref
  21.7 2.3 %collective-permute-done.1.right_ref = f32[2,2,256,128]{3,2,1,0:T(8,128)S(1)} collective-permute-done((f32[2,2,256,128]{3,2,1,0:T(8,128)}, f32[2,2,256,128]{3,2,1,0:T(8,128)S(1)}, u32[]{:S(2)}, u32[]{:S(2)}) %collective-permute-start.1) | collective-permute-done | bytes 524320 | tf_op jit(solution)/shard_map/ppermute | solution.py:416
  24.0 0.0 copy-done.1
  24.0 0.0 copy-done.5
  24.0 0.0 copy-done.4
  24.0 0.0 copy-start.2
  24.0 1.2 copy-done.2
  25.3 30.0 %wave.1 = (f32[16,5,2,8,256]{4,3,2,1,0:T(8,128)}, f32[512,256]{1,0:T(8,128)S(1)}) custom-call(s32[2]{0:T(128)S(1)} %bitcast.9, f32[2,2,256,256]{3,2,1,0:T(8,128)S(1)} %copy-done, f32[2,2,128,256]{3,2,1,0:T(8,128)S(1)} %collective-permute-done.below_ref, f32[2,2,256,128]{3,2,1,0:T(8,128)S(1)} %collective-permute-done.1.right_ref, ...), custom_call_target="tpu_custom_call" | custom-call | tf_op jit(solution)/shard_map/wave/pallas_call | solution.py:268
  55.3 0.0 copy-start.3
  55.3 0.8 copy-done.3
  56.1 0.0 all-to-all-done
  56.1 0.0 copy-start.12
  56.1 0.6 copy-done.12
  56.7 7.5 %all-to-all-start.1 = ((f32[16,5,2,8,256]{4,3,2,1,0:T(8,128)}), f32[16,5,2,8,256]{4,3,2,1,0:T(8,128)S(1)}, u32[]{:S(2)}, u32[]{:S(2)}) async-start(f32[16,5,2,8,256]{4,3,2,1,0:T(8,128)} %get-tuple-element.11), calls=%async_computation.1 | async-start | bytes 2621440 | tf_op jit(solution)/shard_map/all_to_all | solution.py:450
  64.2 20.8 %all-to-all-done.1.parts_ref = f32[16,5,2,8,256]{4,3,2,1,0:T(8,128)S(1)} async-done(((f32[16,5,2,8,256]{4,3,2,1,0:T(8,128)}), f32[16,5,2,8,256]{4,3,2,1,0:T(8,128)S(1)}, u32[]{:S(2)}, u32[]{:S(2)}) %all-to-all-start.1) | async-done | bytes 1310752 | tf_op jit(solution)/shard_map/all_to_all | solution.py:450
  85.0 0.0 copy-start.7
  85.0 1.1 copy-done.7
  86.1 2.7 %sum.1 = (f32[6,2,8,256]{3,2,1,0:T(8,128)}, f32[6,2,8,128]{3,2,1,0:T(8,128)}, f32[6,8,256]{2,1,0:T(8,128)}, f32[6,8,128]{2,1,0:T(8,128)}) custom-call(s32[1]{0:T(128)} %bitcast.me_ref, s32[16,2]{1,0:T(8,128)} %bitcast.12, f32[16,5,2,8,256]{4,3,2,1,0:T(8,128)} %copy-done.7, f32[512,256]{1,0:T(8,128)} %copy-done.3), custom_call_target="tpu_custom_call" | custom-call | tf_op jit(solution)/shard_map/sum/pallas_call | solution.py:340
  88.9 1.3 %collective-permute-start.3 = (f32[6,2,8,128]{3,2,1,0:T(8,128)}, f32[6,2,8,128]{3,2,1,0:T(8,128)S(1)}, u32[]{:S(2)}, u32[]{:S(2)}) collective-permute-start(f32[6,2,8,128]{3,2,1,0:T(8,128)} %get-tuple-element.14), channel_id=1, source_target_pairs={{0,1},{2,3},{4,5},{6,7},{8,9},{10,11},{12,13},{14,15},{16,17},{18,... | collective-permute-start | bytes 147464 | tf_op jit(solution)/shard_map/ppermute | solution.py:416
  90.1 3.4 %collective-permute-start.4 = (f32[6,8,256]{2,1,0:T(8,128)}, f32[6,8,256]{2,1,0:T(8,128)S(1)}, u32[]{:S(2)}, u32[]{:S(2)}) collective-permute-start(f32[6,8,256]{2,1,0:T(8,128)} %get-tuple-element.15), channel_id=1, source_target_pairs={{0,2},{2,4},{4,6},{1,3},{3,5},{5,7},{8,10},{10,12},{12,14},{9,11},... | collective-permute-start | bytes 147464 | tf_op jit(solution)/shard_map/ppermute | solution.py:416
  93.5 1.3 %collective-permute-start.5 = (f32[6,8,128]{2,1,0:T(8,128)}, f32[6,8,128]{2,1,0:T(8,128)S(1)}, u32[]{:S(2)}, u32[]{:S(2)}) collective-permute-start(f32[6,8,128]{2,1,0:T(8,128)} %get-tuple-element.16), channel_id=1, source_target_pairs={{0,3},{2,5},{4,7},{8,11},{10,13},{12,15},{16,19},{18,21},{20,23},{... | collective-permute-start | bytes 73736 | tf_op jit(solution)/shard_map/ppermute | solution.py:427
  94.8 5.5 %collective-permute-done.5.diag_ref = f32[6,8,128]{2,1,0:T(8,128)S(1)} collective-permute-done((f32[6,8,128]{2,1,0:T(8,128)}, f32[6,8,128]{2,1,0:T(8,128)S(1)}, u32[]{:S(2)}, u32[]{:S(2)}) %collective-permute-start.5) | collective-permute-done | bytes 24608 | tf_op jit(solution)/shard_map/ppermute | solution.py:427
  100.4 0.0 copy-start.13
  100.4 0.0 collective-permute-done.3.right_ref
  100.4 0.0 copy-start.10
  100.4 0.0 collective-permute-done.4.below_ref
  100.4 0.0 copy-start.11
  100.4 0.6 copy-done.13
  101.0 0.0 copy-done.10
  101.0 0.0 copy-done.11
  101.0 2.0 %update.1 = f32[2,2,2,8,256]{4,3,2,1,0:T(8,128)} custom-call(s32[1]{0:T(128)} %bitcast.me_ref, f32[2,2,256,256]{3,2,1,0:T(8,128)} %object_ref.1, f32[6,2,8,256]{3,2,1,0:T(8,128)} %get-tuple-element.13.own_ref, f32[6,2,8,128]{3,2,1,0:T(8,128)} %copy-done.10, f32[6,8,256]{2,1,0:T(8,128)} %copy-done.11, f32[6,8,128]{2,1,0:T(8,128)} %copy-done.13), custom_call_target="tpu_custom_call" | custom-call | tf_op jit(solution)/shard_map/update/pallas_call | solution.py:378
  103.0 0.7 collective-permute-start.6
  103.7 5.3 %collective-permute-done.6 = f32[1,2,2,2,8,256]{5,4,3,2,1,0:T(8,128)S(1)} collective-permute-done((f32[1,2,2,2,8,256]{5,4,3,2,1,0:T(8,128)}, f32[1,2,2,2,8,256]{5,4,3,2,1,0:T(8,128)S(1)}, u32[]{:S(2)}, u32[]{:S(2)}) %collective-permute-start.6) | collective-permute-done | bytes 65568 | tf_op jit(solution)/shard_map/ppermute | solution.py:435
  109.0 0.8 pad_maximum_fusion
  109.8 0.1 collective-permute-start.7
  109.9 0.8 constant_dynamic-update-slice_fusion.4
  110.8 2.4 %collective-permute-start.8 = (f32[2,2,2,2,8,256]{5,4,3,2,1,0:T(8,128)S(1)}, f32[2,2,2,2,8,256]{5,4,3,2,1,0:T(8,128)S(1)}, u32[]{:S(2)}, u32[]{:S(2)}) collective-permute-start(f32[2,2,2,2,8,256]{5,4,3,2,1,0:T(8,128)S(1)} %pad_maximum_fusion), channel_id=1, source_target_pairs={{0,64},{8,72},{16,80},{24,88},{32,96},{40,104},{48,112},{56,120},{... | collective-permute-start | bytes 393224 | tf_op jit(solution)/shard_map/ppermute | solution.py:435
  113.1 1.5 %collective-permute-start.9 = (f32[2,2,2,2,8,256]{5,4,3,2,1,0:T(8,128)S(1)}, f32[2,2,2,2,8,256]{5,4,3,2,1,0:T(8,128)S(1)}, u32[]{:S(2)}, u32[]{:S(2)}) collective-permute-start(f32[2,2,2,2,8,256]{5,4,3,2,1,0:T(8,128)S(1)} %pad_maximum_fusion), channel_id=1, source_target_pairs={{0,96},{8,104},{16,112},{24,120},{32,0},{40,8},{48,16},{56,24},{64... | collective-permute-start | bytes 393224 | tf_op jit(solution)/shard_map/ppermute | solution.py:435
  114.7 2.8 %collective-permute-done.7 = f32[2,2,2,2,8,256]{5,4,3,2,1,0:T(8,128)S(1)} collective-permute-done((f32[2,2,2,2,8,256]{5,4,3,2,1,0:T(8,128)S(1)}, f32[2,2,2,2,8,256]{5,4,3,2,1,0:T(8,128)S(1)}, u32[]{:S(2)}, u32[]{:S(2)}) %collective-permute-start.7) | collective-permute-done | bytes 131104 | tf_op jit(solution)/shard_map/ppermute | solution.py:435
  117.5 0.0 collective-permute-done.8
  117.5 1.7 %collective-permute-done.9 = f32[2,2,2,2,8,256]{5,4,3,2,1,0:T(8,128)S(1)} collective-permute-done((f32[2,2,2,2,8,256]{5,4,3,2,1,0:T(8,128)S(1)}, f32[2,2,2,2,8,256]{5,4,3,2,1,0:T(8,128)S(1)}, u32[]{:S(2)}, u32[]{:S(2)}) %collective-permute-start.9) | collective-permute-done | bytes 131104 | tf_op jit(solution)/shard_map/ppermute | solution.py:435
  119.2 0.0 copy-start.8
  119.2 0.1 collective-permute-start.10
  119.3 1.9 %collective-permute-done.10.refs_1_ = f32[8,2,2,2,8,256]{5,4,3,2,1,0:T(8,128)S(1)} collective-permute-done((f32[8,2,2,2,8,256]{5,4,3,2,1,0:T(8,128)S(1)}, f32[8,2,2,2,8,256]{5,4,3,2,1,0:T(8,128)S(1)}, u32[]{:S(2)}, u32[]{:S(2)}) %collective-permute-start.10) | collective-permute-done | bytes 524320 | tf_op jit(solution)/shard_map/ppermute | solution.py:435
  121.2 0.0 copy-done.8
  121.2 0.0 copy-start.9
  121.2 0.8 copy-done.9
  122.0 2.3 %place.1 = f32[2,2,256,256]{3,2,1,0:T(8,128)} custom-call(s32[1]{0:T(128)} %bitcast.me_ref, f32[8,2,2,2,8,256]{5,4,3,2,1,0:T(8,128)} %copy-done.8, f32[8,2,2,2,8,256]{5,4,3,2,1,0:T(8,128)} %copy-done.9), custom_call_target="tpu_custom_call" | custom-call | tf_op jit(solution)/shard_map/place/pallas_call | solution.py:404
  (5 shorter events, 0.0 us)
Async XLA Ops:
  0.0 4.5 %copy-start = (f32[2,2,256,256]{3,2,1,0:T(8,128)S(1)}, f32[2,2,256,256]{3,2,1,0:T(8,128)}, u32[]{:S(2)}) copy-start(f32[2,2,256,256]{3,2,1,0:T(8,128)} %object_ref.1) | copy-start | bytes 3145732
  0.0 24.0 %copy-start.1 = (bf16[4,2,256,256]{3,2,1,0:T(8,128)(2,1)S(1)}, bf16[4,2,256,256]{3,2,1,0:T(8,128)(2,1)}, u32[]{:S(2)}) copy-start(bf16[4,2,256,256]{3,2,1,0:T(8,128)(2,1)} %constant.14.clone.col_tab) | copy-start | bytes 3145732
  0.0 24.0 %copy-start.5 = (bf16[256,256]{1,0:T(8,128)(2,1)S(1)}, bf16[256,256]{1,0:T(8,128)(2,1)}, u32[]{:S(2)}) copy-start(bf16[256,256]{1,0:T(8,128)(2,1)} %constant.16.clone.order_ref) | copy-start | bytes 393220
  0.0 10.0 %copy-start.6 = (s32[1,1,1,2]{3,2,1,0:T(1,128)S(1)}, s32[1,1,1,2]{3,2,1,0:T(1,128)}, u32[]{:S(2)}) copy-start(s32[1,1,1,2]{3,2,1,0:T(1,128)} %param.9) | copy-start | bytes 28
  0.0 24.0 %copy-start.4 = (f32[1,1,1,256,256]{4,3,2,1,0:T(8,128)S(1)}, f32[1,1,1,256,256]{4,3,2,1,0:T(8,128)}, u32[]{:S(2)}) copy-start(f32[1,1,1,256,256]{4,3,2,1,0:T(8,128)} %param.10) | copy-start | bytes 786436
  2.1 19.6 %collective-permute-start = (f32[2,2,128,256]{3,2,1,0:T(8,128)}, f32[2,2,128,256]{3,2,1,0:T(8,128)S(1)}, u32[]{:S(2)}, u32[]{:S(2)}) collective-permute-start(f32[2,2,128,256]{3,2,1,0:T(8,128)} %slice.13), channel_id=1, source_target_pairs={{2,0},{4,2},{6,4},{3,1},{5,3},{7,5},{10,8},{12,10},{14,12},{11,9},... | collective-permute-start | bytes 1572872 | tf_op jit(solution)/shard_map/ppermute | solution.py:416
  5.4 18.7 %collective-permute-start.1 = (f32[2,2,256,128]{3,2,1,0:T(8,128)}, f32[2,2,256,128]{3,2,1,0:T(8,128)S(1)}, u32[]{:S(2)}, u32[]{:S(2)}) collective-permute-start(f32[2,2,256,128]{3,2,1,0:T(8,128)} %slice.14), channel_id=1, source_target_pairs={{1,0},{3,2},{5,4},{7,6},{9,8},{11,10},{13,12},{15,14},{17,16},{19,... | collective-permute-start | bytes 1572872 | tf_op jit(solution)/shard_map/ppermute | solution.py:416
  8.0 13.7 %collective-permute-start.2 = (f32[2,2,128,128]{3,2,1,0:T(8,128)}, f32[2,2,128,128]{3,2,1,0:T(8,128)}, u32[]{:S(2)}, u32[]{:S(2)}) collective-permute-start(f32[2,2,128,128]{3,2,1,0:T(8,128)} %slice.15), channel_id=1, source_target_pairs={{3,0},{5,2},{7,4},{11,8},{13,10},{15,12},{19,16},{21,18},{23,20},{... | collective-permute-start | bytes 786440 | tf_op jit(solution)/shard_map/ppermute | solution.py:427
  10.7 45.5 %all-to-all-start = ((s32[16,1,128]{2,1,0:T(1,128)}), s32[16,1,128]{2,1,0:T(1,128)S(1)}, u32[]{:S(2)}, u32[]{:S(2)}) async-start(s32[16,1,128]{2,1,0:T(1,128)} %broadcast_in_dim.4), calls=%async_computation | async-start | bytes 16384 | tf_op jit(solution)/shard_map/all_to_all | solution.py:445
  24.0 1.2 copy-start.2
  55.3 0.8 copy-start.3
  56.1 0.6 copy-start.12
  56.7 28.3 %all-to-all-start.1 = ((f32[16,5,2,8,256]{4,3,2,1,0:T(8,128)}), f32[16,5,2,8,256]{4,3,2,1,0:T(8,128)S(1)}, u32[]{:S(2)}, u32[]{:S(2)}) async-start(f32[16,5,2,8,256]{4,3,2,1,0:T(8,128)} %get-tuple-element.11), calls=%async_computation.1 | async-start | bytes 2621440 | tf_op jit(solution)/shard_map/all_to_all | solution.py:450
  85.0 1.1 copy-start.7
  88.9 11.5 %collective-permute-start.3 = (f32[6,2,8,128]{3,2,1,0:T(8,128)}, f32[6,2,8,128]{3,2,1,0:T(8,128)S(1)}, u32[]{:S(2)}, u32[]{:S(2)}) collective-permute-start(f32[6,2,8,128]{3,2,1,0:T(8,128)} %get-tuple-element.14), channel_id=1, source_target_pairs={{0,1},{2,3},{4,5},{6,7},{8,9},{10,11},{12,13},{14,15},{16,17},{18,... | collective-permute-start | bytes 147464 | tf_op jit(solution)/shard_map/ppermute | solution.py:416
  90.1 10.2 %collective-permute-start.4 = (f32[6,8,256]{2,1,0:T(8,128)}, f32[6,8,256]{2,1,0:T(8,128)S(1)}, u32[]{:S(2)}, u32[]{:S(2)}) collective-permute-start(f32[6,8,256]{2,1,0:T(8,128)} %get-tuple-element.15), channel_id=1, source_target_pairs={{0,2},{2,4},{4,6},{1,3},{3,5},{5,7},{8,10},{10,12},{12,14},{9,11},... | collective-permute-start | bytes 147464 | tf_op jit(solution)/shard_map/ppermute | solution.py:416
  93.5 6.8 %collective-permute-start.5 = (f32[6,8,128]{2,1,0:T(8,128)}, f32[6,8,128]{2,1,0:T(8,128)S(1)}, u32[]{:S(2)}, u32[]{:S(2)}) collective-permute-start(f32[6,8,128]{2,1,0:T(8,128)} %get-tuple-element.16), channel_id=1, source_target_pairs={{0,3},{2,5},{4,7},{8,11},{10,13},{12,15},{16,19},{18,21},{20,23},{... | collective-permute-start | bytes 73736 | tf_op jit(solution)/shard_map/ppermute | solution.py:427
  100.4 0.6 copy-start.13
  100.4 0.6 copy-start.10
  100.4 0.6 copy-start.11
  103.0 6.0 %collective-permute-start.6 = (f32[1,2,2,2,8,256]{5,4,3,2,1,0:T(8,128)}, f32[1,2,2,2,8,256]{5,4,3,2,1,0:T(8,128)S(1)}, u32[]{:S(2)}, u32[]{:S(2)}) collective-permute-start(f32[1,2,2,2,8,256]{5,4,3,2,1,0:T(8,128)} %bitcast.10), channel_id=1, source_target_pairs={{0,16},{8,24},{16,0},{24,8},{32,48},{40,56},{48,32},{56,40},{64,80... | collective-permute-start | bytes 196616 | tf_op jit(solution)/shard_map/ppermute | solution.py:435
  109.8 7.7 %collective-permute-start.7 = (f32[2,2,2,2,8,256]{5,4,3,2,1,0:T(8,128)S(1)}, f32[2,2,2,2,8,256]{5,4,3,2,1,0:T(8,128)S(1)}, u32[]{:S(2)}, u32[]{:S(2)}) collective-permute-start(f32[2,2,2,2,8,256]{5,4,3,2,1,0:T(8,128)S(1)} %pad_maximum_fusion), channel_id=1, source_target_pairs={{0,32},{8,40},{16,48},{24,56},{32,64},{40,72},{48,80},{56,88},{64,... | collective-permute-start | bytes 393224 | tf_op jit(solution)/shard_map/ppermute | solution.py:435
  110.8 6.7 %collective-permute-start.8 = (f32[2,2,2,2,8,256]{5,4,3,2,1,0:T(8,128)S(1)}, f32[2,2,2,2,8,256]{5,4,3,2,1,0:T(8,128)S(1)}, u32[]{:S(2)}, u32[]{:S(2)}) collective-permute-start(f32[2,2,2,2,8,256]{5,4,3,2,1,0:T(8,128)S(1)} %pad_maximum_fusion), channel_id=1, source_target_pairs={{0,64},{8,72},{16,80},{24,88},{32,96},{40,104},{48,112},{56,120},{... | collective-permute-start | bytes 393224 | tf_op jit(solution)/shard_map/ppermute | solution.py:435
  113.1 6.0 %collective-permute-start.9 = (f32[2,2,2,2,8,256]{5,4,3,2,1,0:T(8,128)S(1)}, f32[2,2,2,2,8,256]{5,4,3,2,1,0:T(8,128)S(1)}, u32[]{:S(2)}, u32[]{:S(2)}) collective-permute-start(f32[2,2,2,2,8,256]{5,4,3,2,1,0:T(8,128)S(1)} %pad_maximum_fusion), channel_id=1, source_target_pairs={{0,96},{8,104},{16,112},{24,120},{32,0},{40,8},{48,16},{56,24},{64... | collective-permute-start | bytes 393224 | tf_op jit(solution)/shard_map/ppermute | solution.py:435
  119.2 2.0 %copy-start.8 = (f32[8,2,2,2,8,256]{5,4,3,2,1,0:T(8,128)}, f32[8,2,2,2,8,256]{5,4,3,2,1,0:T(8,128)S(1)}, u32[]{:S(2)}) copy-start(f32[8,2,2,2,8,256]{5,4,3,2,1,0:T(8,128)S(1)} %constant_dynamic-update-slice_fusion.refs_0_) | copy-start | bytes 1572868
  119.2 2.0 %collective-permute-start.10 = (f32[8,2,2,2,8,256]{5,4,3,2,1,0:T(8,128)S(1)}, f32[8,2,2,2,8,256]{5,4,3,2,1,0:T(8,128)S(1)}, u32[]{:S(2)}, u32[]{:S(2)}) collective-permute-start(f32[8,2,2,2,8,256]{5,4,3,2,1,0:T(8,128)S(1)} %constant_dynamic-update-slice_fusion.refs_0_), channel_id=1, source_target_pairs={{0,8},{8,0},{16,24},{24,16},{32,40},{40,32},{48,56},{56,48},{64,72... | collective-permute-start | bytes 1572872 | tf_op jit(solution)/shard_map/ppermute | solution.py:435
  121.2 0.8 copy-start.9

commit v2 on v1

v2 whole, which is shorter than its diff:
```python
import functools
import math

import jax
import jax.numpy as jnp
import numpy as np
from jax import lax
from jax.experimental import pallas as pl
from jax.experimental.pallas import tpu as pltpu
from jax.sharding import PartitionSpec as P

fresnel_coef = 0.1
step_size = 4.0
SIDE = 256
HALF = 128
LAYERS = 2
SCANS = 16
ROWS = 32
PAD = 8
f32 = jnp.float32
bf16 = jnp.bfloat16


def real_right(table):
    return np.block([[table.real, table.imag], [-table.imag, table.real]])


def real_left(table):
    return np.block([[table.real, -table.imag], [table.imag, table.real]])


def stacked(table, axis):
    high = table.astype(np.float32).astype(bf16)
    low = (table - high.astype(np.float64)).astype(np.float32).astype(bf16)
    return np.concatenate([high, high, low], axis=axis)


def make_tables():
    half = np.arange(HALF)
    col_even = np.exp(-2j * np.pi * np.outer(half, half) / HALF) / 16
    col_odd = np.exp(-2j * np.pi * np.outer(half, 2 * half + 1) / SIDE) / 16
    row_even, row_odd = col_even.T, col_odd.T
    right = [col_even, col_odd, col_even.conj().T, col_odd.conj().T]
    left = [row_even, row_odd, row_even.conj().T, row_odd.conj().T]
    right = np.stack([stacked(real_right(t), 0) for t in right])
    left = np.stack([stacked(real_left(t), 1) for t in left])
    order = np.zeros((SIDE, SIDE), np.float32)
    order[2 * half, half] = 1.0
    order[2 * half + 1, half + HALF] = 1.0
    return right, left, order.astype(bf16)


def split(value):
    high = value.astype(bf16)
    return high, (value - high.astype(f32)).astype(bf16)


def mul(first, second):
    return jnp.dot(first, second, preferred_element_type=f32)


def put(ref, lead, rows, value):
    high, low = split(value)
    ref[lead + (0, rows)] = high
    ref[lead + (1, rows)] = low


def right_dot(ref, side, table, which):
    high, low = ref[side, 0], ref[side, 1]
    return mul(jnp.concatenate([high, low, high], axis=1), table[which])


def left_dot(table, which, ref, side):
    high, low = ref[side, 0], ref[side, 1]
    return mul(table[which], jnp.concatenate([high, low, high], axis=0))


def neighbours(ref, p, start):
    rows = lambda by: pl.ds(start + PAD + by, ROWS)
    low, high = ref[p, 0, rows(0)], ref[p, 1, rows(0)]
    lane = lax.broadcasted_iota(jnp.int32, low.shape, 1)
    first, last = lane == 0, lane == HALF - 1
    low_up, high_up = pltpu.roll(low, 1, 1), pltpu.roll(high, 1, 1)
    low_down, high_down = pltpu.roll(low, HALF - 1, 1), pltpu.roll(high, HALF - 1, 1)
    low_sum = jnp.where(first, 0.0, low_up) + jnp.where(last, high_down, low_down)
    high_sum = jnp.where(first, low_up, high_up) + jnp.where(last, 0.0, high_down)
    return (
        low_sum + (ref[p, 0, rows(-1)] + ref[p, 0, rows(1)]),
        high_sum + (ref[p, 1, rows(-1)] + ref[p, 1, rows(1)]),
    )


damping = 0.5 * fresnel_coef**2


def turn_rows(source, target, start, sign):
    turn = sign * fresnel_coef
    rows = pl.ds(start + PAD, ROWS)
    near_re, near_im = neighbours(source, 0, start), neighbours(source, 1, start)
    for h in range(2):
        re, im = source[0, h, rows], source[1, h, rows]
        target[0, h, rows] = 4.0 * damping * re - turn * im - damping * near_re[h]
        target[1, h, rows] = 4.0 * damping * im + turn * re - damping * near_im[h]


def end_rows(source, target, start):
    rows = pl.ds(start + PAD, ROWS)
    near = [neighbours(target, p, start) for p in range(2)]
    return [
        [source[p, h, rows] - 4.0 * target[p, h, rows] + near[p][h] for p in range(2)]
        for h in range(2)
    ]


def probe_copies(probe_ref, probe, sems, m):
    return [
        pltpu.make_async_copy(
            probe_ref.at[p, m, :, pl.ds(h * HALF, HALF)], probe.at[p, m, h], sems.at[p, m, h]
        )
        for p in range(2)
        for h in range(2)
    ]


def arrange(value, order, axis):
    high, low = split(value)
    rest = (value - high.astype(f32) - low.astype(f32)).astype(bf16)
    if axis == 1:
        return mul(high, order) + mul(low, order) + mul(rest, order)
    turned = order.T
    return mul(turned, high) + mul(turned, low) + mul(turned, rest)


def wave_kernel(
    corner_ref,
    below_ref,
    right_ref,
    diag_ref,
    other_below_ref,
    other_right_ref,
    other_diag_ref,
    own_far,
    probe_ref,
    measured_far,
    col_far,
    row_far,
    order_far,
    out_ref,
    own_ref,
    measured_ref,
    col_tab,
    row_tab,
    order_ref,
    hold,
    trans,
    wave,
    far,
    misfit,
    total,
    probe,
    sems,
    more_sems,
    field,
    turned,
    across,
    along,
):
    r, c = corner_ref[0], corner_ref[1]
    modes = probe_ref.shape[1]
    own_copy = pltpu.make_async_copy(own_far, own_ref, more_sems.at[0])
    later = [
        pltpu.make_async_copy(source, target, more_sems.at[n + 1])
        for n, (source, target) in enumerate(
            [
                (order_far, order_ref),
                (measured_far, measured_ref),
                (col_far, col_tab),
                (row_far, row_tab),
            ]
        )
    ]
    own_copy.start()
    for copy in probe_copies(probe_ref, probe, sems, 0):
        copy.start()
    for copy in later:
        copy.start()
    for m in range(1, modes):
        for copy in probe_copies(probe_ref, probe, sems, m):
            copy.start()
    rows = lax.broadcasted_iota(jnp.int32, (SIDE, SIDE), 0)
    cols = lax.broadcasted_iota(jnp.int32, (SIDE, SIDE), 1)
    top = rows[:HALF] < r
    near = cols[:, :HALF] < c
    back_c = lax.rem(SIDE - c, SIDE)
    own_copy.wait()
    for s in range(LAYERS):
        for p in range(2):
            held = corner_ref[2] == p
            right = jnp.where(held, right_ref[s], other_right_ref[s])
            below = jnp.where(held, below_ref[s], other_below_ref[s])
            diag = jnp.where(held, diag_ref[s], other_diag_ref[s])
            left = jnp.where(near, right, own_ref[s, p, :, :HALF])
            whole = jnp.concatenate([left, own_ref[s, p, :, HALF:]], axis=1)
            lower = jnp.concatenate(
                [jnp.where(near[:HALF], diag, below[:, :HALF]), below[:, HALF:]], axis=1
            )
            whole = jnp.concatenate([jnp.where(top, lower, whole[:HALF]), whole[HALF:]], axis=0)
            whole = pltpu.roll(whole, back_c, 1)
            for half in range(2):
                hold[0, half * SIDE : (half + 1) * SIDE] = whole[:, :HALF]
                hold[1, half * SIDE : (half + 1) * SIDE] = whole[:, HALF:]
            for h in range(2):
                view = hold[h, pl.ds(r, SIDE)]
                trans[s, p, h] = view + 1.0 if p == 0 else view

    for copy in later:
        copy.wait()
    order = order_ref[...]
    misfit[...] = -arrange(arrange(measured_ref[...], order, 1), order, 0)
    total[...] = jnp.zeros_like(total)
    field[...] = jnp.zeros_like(field)
    turned[...] = jnp.zeros_like(turned)
    starts = range(0, SIDE, ROWS)

    def forward(m, carry):
        for copy in probe_copies(probe_ref, probe, sems, m):
            copy.wait()
        for start in starts:
            rows, inner = pl.ds(start, ROWS), pl.ds(start + PAD, ROWS)
            for h in range(2):
                p_re, p_im = probe[0, m, h, rows], probe[1, m, h, rows]
                t_re, t_im = trans[0, 0, h, rows], trans[0, 1, h, rows]
                field[0, h, inner] = p_re * t_re - p_im * t_im
                field[1, h, inner] = p_re * t_im + p_im * t_re
        for start in starts:
            turn_rows(field, turned, start, 1.0)
        for start in starts:
            rows = pl.ds(start, ROWS)
            x = []
            for h, (w_re, w_im) in enumerate(end_rows(field, turned, start)):
                wave[0, m, h, rows] = w_re
                wave[1, m, h, rows] = w_im
                total[2, h, rows] += w_re * w_re + w_im * w_im
                t_re, t_im = trans[1, 0, h, rows], trans[1, 1, h, rows]
                x.append(
                    jnp.concatenate([w_re * t_re - w_im * t_im, w_re * t_im + w_im * t_re], axis=1)
                )
            put(across, (0,), rows, x[0] + x[1])
            put(across, (1,), rows, x[0] - x[1])
        even = right_dot(across, 0, col_tab, 0)
        odd = right_dot(across, 1, col_tab, 1)
        for start in range(0, HALF, ROWS):
            for q in range(2):
                lanes = slice(HALF * q, HALF * (q + 1))
                above, under = [
                    jnp.concatenate([even[part, lanes], odd[part, lanes]], axis=1)
                    for part in (slice(start, start + ROWS), slice(start + HALF, start + HALF + ROWS))
                ]
                rows = pl.ds(HALF * q + start, ROWS)
                put(along, (0,), rows, above + under)
                put(along, (1,), rows, above - under)
        for e in range(2):
            found = left_dot(row_tab, e, along, e)
            far[m, e] = found
            misfit[pl.ds(HALF * e, HALF)] += found[:HALF] * found[:HALF] + found[HALF:] * found[HALF:]
        return carry

    lax.fori_loop(0, modes, forward, 0)
    misfit[...] = 2.0 * misfit[...]

    def backward(m, carry):
        for e in range(2):
            for start in range(0, HALF, ROWS):
                scale = misfit[pl.ds(HALF * e + start, ROWS)]
                for q in range(2):
                    rows = pl.ds(HALF * q + start, ROWS)
                    put(along, (e,), rows, scale * far[m, e, rows])
        even = left_dot(row_tab, 2, along, 0)
        odd = left_dot(row_tab, 3, along, 1)
        for start in range(0, HALF, ROWS):
            re, im = slice(start, start + ROWS), slice(HALF + start, HALF + start + ROWS)
            for n in range(2):
                f_re = even[re] + odd[re] if n == 0 else even[re] - odd[re]
                f_im = even[im] + odd[im] if n == 0 else even[im] - odd[im]
                rows = pl.ds(HALF * n + start, ROWS)
                for q in range(2):
                    lanes = slice(HALF * q, HALF * (q + 1))
                    put(
                        across,
                        (q,),
                        rows,
                        jnp.concatenate([f_re[:, lanes], f_im[:, lanes]], axis=1),
                    )
        first = right_dot(across, 0, col_tab, 2)
        second = right_dot(across, 1, col_tab, 3)
        for start in starts:
            rows, inner = pl.ds(start, ROWS), pl.ds(start + PAD, ROWS)
            part = slice(start, start + ROWS)
            for h in range(2):
                both = first[part] + second[part] if h == 0 else first[part] - second[part]
                b_re, b_im = both[:, :HALF], both[:, HALF:]
                w_re, w_im = wave[0, m, h, rows], wave[1, m, h, rows]
                total[0, h, rows] += w_re * b_re + w_im * b_im
                total[1, h, rows] += w_re * b_im - w_im * b_re
                t_re, t_im = trans[1, 0, h, rows], trans[1, 1, h, rows]
                field[0, h, inner] = t_re * b_re + t_im * b_im
                field[1, h, inner] = t_re * b_im - t_im * b_re
        for start in starts:
            turn_rows(field, turned, start, -1.0)
        for start in starts:
            rows = pl.ds(start, ROWS)
            for h, (d_re, d_im) in enumerate(end_rows(field, turned, start)):
                p_re, p_im = probe[0, m, h, rows], probe[1, m, h, rows]
                total[3, h, rows] += p_re * d_re + p_im * d_im
                total[4, h, rows] += p_re * d_im - p_im * d_re
        return carry

    lax.fori_loop(0, modes, backward, 0)

    for k in range(5):
        for h in range(2):
            hold[h, :SIDE] = total[k, h]
            hold[h, SIDE:] = total[k, h]
        for n in range(SIDE // 8):
            rows = pl.ds(SIDE - r + 8 * n, 8)
            block = jnp.concatenate([hold[0, rows], hold[1, rows]], axis=1)
            out_ref[n % 16, 2 * k + n // 16] = pltpu.roll(block, c, 1)
    lane = lax.broadcasted_iota(jnp.int32, (8, SIDE), 1)
    mark = jnp.where(lane == 0, r, c).astype(f32)
    for i in range(SCANS):
        out_ref[i, 10] = mark


def glow_kernel(probe_ref, light_ref):
    @pl.when(pl.program_id(0) == 0)
    def _():
        light_ref[...] = jnp.zeros_like(light_ref)

    light = probe_ref[0, 0] * probe_ref[0, 0] + probe_ref[1, 0] * probe_ref[1, 0]
    light_ref[:SIDE] += light
    light_ref[SIDE:] += light


def run_glow(probe):
    modes = probe.shape[1]
    return pl.pallas_call(
        glow_kernel,
        grid=(modes,),
        out_shape=jax.ShapeDtypeStruct((2 * SIDE, SIDE), f32),
        in_specs=[pl.BlockSpec((2, 1, SIDE, SIDE), lambda m: (0, m, 0, 0))],
        out_specs=pl.BlockSpec((2 * SIDE, SIDE), lambda m: (0, 0)),
        compiler_params=pltpu.CompilerParams(vmem_limit_bytes=60 * 1024 * 1024),
        cost_estimate=pl.CostEstimate(
            flops=4 * modes * SIDE * SIDE, bytes_accessed=8 * modes * SIDE * SIDE, transcendentals=0
        ),
        name="glow",
    )(probe)


def cut_kernel(me_ref, object_ref, below_ref, right_ref, diag_ref, sems):
    core = lax.rem(me_ref[0], 2)
    copies = []
    for s in range(LAYERS):
        plane = object_ref.at[s, core]
        near = pl.ds(0, HALF)
        for n, (source, target) in enumerate(
            [
                (plane.at[near, :], below_ref.at[s]),
                (plane.at[:, near], right_ref.at[s]),
                (plane.at[near, near], diag_ref.at[s]),
            ]
        ):
            copies.append(pltpu.make_async_copy(source, target, sems.at[s, n]))
    for copy in copies:
        copy.start()
    for copy in copies:
        copy.wait()


def run_cut(me, current):
    vmem = pl.BlockSpec(memory_space=pltpu.VMEM)
    return pl.pallas_call(
        cut_kernel,
        out_shape=(
            jax.ShapeDtypeStruct((LAYERS, HALF, SIDE), f32),
            jax.ShapeDtypeStruct((LAYERS, SIDE, HALF), f32),
            jax.ShapeDtypeStruct((LAYERS, HALF, HALF), f32),
        ),
        in_specs=[pl.BlockSpec(memory_space=pltpu.SMEM), pl.BlockSpec(memory_space=pl.ANY)],
        out_specs=(vmem,) * 3,
        scratch_shapes=[pltpu.SemaphoreType.DMA((LAYERS, 3))],
        compiler_params=pltpu.CompilerParams(vmem_limit_bytes=60 * 1024 * 1024),
        name="cut",
    )(me, current)


def run_wave(corner, own, rims, probe, measured):
    right_table, left_table, order = make_tables()
    modes = probe.shape[1]
    vmem = pl.BlockSpec(memory_space=pltpu.VMEM)
    field = (2, SIDE, HALF)
    wide = (2, 2, SIDE + 2 * PAD, HALF)
    return pl.pallas_call(
        wave_kernel,
        out_shape=jax.ShapeDtypeStruct((SCANS, 11, 8, SIDE), f32),
        in_specs=[pl.BlockSpec(memory_space=pltpu.SMEM)]
        + [vmem] * 6
        + [pl.BlockSpec(memory_space=pl.ANY)] * 6,
        out_specs=vmem,
        scratch_shapes=[
            pltpu.VMEM((LAYERS, 2, SIDE, SIDE), f32),
            pltpu.VMEM((SIDE, SIDE), f32),
            pltpu.VMEM((4, 3 * SIDE, SIDE), bf16),
            pltpu.VMEM((4, SIDE, 3 * SIDE), bf16),
            pltpu.VMEM((SIDE, SIDE), bf16),
            pltpu.VMEM((2, 2 * SIDE, HALF), f32),
            pltpu.VMEM((LAYERS, 2) + field, f32),
            pltpu.VMEM((2, modes) + field, f32),
            pltpu.VMEM((modes, 2, SIDE, SIDE), f32),
            pltpu.VMEM((SIDE, SIDE), f32),
            pltpu.VMEM((5,) + field, f32),
            pltpu.VMEM((2, modes, 2, SIDE, HALF), f32),
            pltpu.SemaphoreType.DMA((2, modes, 2)),
            pltpu.SemaphoreType.DMA((5,)),
            pltpu.VMEM(wide, f32),
            pltpu.VMEM(wide, f32),
            pltpu.VMEM((2, 2, SIDE, SIDE), bf16),
            pltpu.VMEM((2, 2, SIDE, SIDE), bf16),
        ],
        compiler_params=pltpu.CompilerParams(vmem_limit_bytes=60 * 1024 * 1024),
        name="wave",
    )(
        corner,
        *rims,
        own,
        probe,
        measured,
        jnp.asarray(right_table),
        jnp.asarray(left_table),
        jnp.asarray(order),
    )


def sum_kernel(
    me_ref, parts_ref, light_ref, own_ref, right_ref, below_ref, diag_ref, marks_ref, sem
):
    me = me_ref[0]
    copy = pltpu.make_async_copy(parts_ref.at[:, 10, :, pl.ds(0, HALF)], marks_ref, sem)
    copy.start()
    own_ref[...] = jnp.zeros_like(own_ref)
    right_ref[...] = jnp.zeros_like(right_ref)
    below_ref[...] = jnp.zeros_like(below_ref)
    diag_ref[...] = jnp.zeros_like(diag_ref)
    sub = lax.broadcasted_iota(jnp.int32, (2, 8, SIDE), 1)
    side = lax.broadcasted_iota(jnp.int32, (2, 8, SIDE), 0)
    cols = lax.broadcasted_iota(jnp.int32, (2, 8, SIDE), 2)
    rows = HALF * side + 8 * me + sub
    copy.wait()
    for j in range(SCANS):
        r = marks_ref[j, 0, 0].astype(jnp.int32)
        c = marks_ref[j, 0, 1].astype(jnp.int32)
        lights = []
        for h in range(2):
            start = lax.rem(HALF * h + 8 * me + SIDE - r, SIDE)
            base = pl.multiple_of((start // 8) * 8, 8)
            block = light_ref[pl.ds(base, 16), :]
            block = pltpu.roll(block, lax.rem(16 - (start - base), 16), 0)[:8]
            lights.append(pltpu.roll(block, c, 1)[None])
        light = jnp.concatenate(lights, axis=0)
        inside_row, inside_col = rows >= r, cols >= c
        for k in range(6):
            value = parts_ref[j, 2 * k : 2 * k + 2] if k < 5 else light
            here = jnp.where(inside_row, value, 0.0)
            there = (value - here)[0]
            own_ref[k] += jnp.where(inside_col, here, 0.0)
            right_ref[k] += jnp.where(inside_col, 0.0, here)[:, :, :HALF]
            below_ref[k] += jnp.where(inside_col[0], there, 0.0)
            diag_ref[k] += jnp.where(inside_col[0], 0.0, there)[:, :HALF]


def run_sum(me, parts, light):
    smem = pl.BlockSpec(memory_space=pltpu.SMEM)
    vmem = pl.BlockSpec(memory_space=pltpu.VMEM)
    return pl.pallas_call(
        sum_kernel,
        out_shape=(
            jax.ShapeDtypeStruct((6, 2, 8, SIDE), f32),
            jax.ShapeDtypeStruct((6, 2, 8, HALF), f32),
            jax.ShapeDtypeStruct((6, 8, SIDE), f32),
            jax.ShapeDtypeStruct((6, 8, HALF), f32),
        ),
        in_specs=[smem, vmem, vmem],
        out_specs=(vmem,) * 4,
        scratch_shapes=[pltpu.SMEM((SCANS, 8, HALF), f32), pltpu.SemaphoreType.DMA],
        compiler_params=pltpu.CompilerParams(vmem_limit_bytes=8 * 1024 * 1024),
        name="sum",
    )(me, parts, light)


def update_kernel(me_ref, object_ref, own_ref, right_ref, below_ref, diag_ref, out_ref):
    me = me_ref[0]
    sums = []
    for k in range(6):
        near = own_ref[k, :, :, :HALF] + right_ref[k]
        whole = jnp.concatenate([near, own_ref[k, :, :, HALF:]], axis=2)
        low = jnp.concatenate(
            [below_ref[k, :, :HALF] + diag_ref[k], below_ref[k, :, HALF:]], axis=1
        )
        sums.append([whole[0] + low, whole[1]])
    for s in range(LAYERS):
        base = 3 * (1 - s)
        for h in range(2):
            scale = step_size / (sums[base + 2][h] + 1.0)
            start = pl.multiple_of(HALF * h + 8 * me, 8)
            for p in range(2):
                out_ref[s, p, h] = (
                    object_ref[s, p, pl.ds(start, 8), :] - scale * sums[base + p][h]
                )


def run_update(me, current, own, right, below, diag):
    smem = pl.BlockSpec(memory_space=pltpu.SMEM)
    vmem = pl.BlockSpec(memory_space=pltpu.VMEM)
    return pl.pallas_call(
        update_kernel,
        out_shape=jax.ShapeDtypeStruct((LAYERS, 2, 2, 8, SIDE), f32),
        in_specs=[smem] + [vmem] * 5,
        out_specs=vmem,
        compiler_params=pltpu.CompilerParams(vmem_limit_bytes=4 * 1024 * 1024),
        name="update",
    )(me, current, own, right, below, diag)


def place_kernel(me_ref, *refs):
    blocks, out_ref = refs[:-1], refs[-1]
    me = me_ref[0]
    y, z, core = me // 4, lax.rem(me // 2, 2), lax.rem(me, 2)
    count = 0
    for ref in blocks:
        for b in range(ref.shape[0]):
            dc, dy, dz = count // 8, (count // 2) % 4, count % 2
            i = lax.rem(y + 4 - dy, 4) * 4 + lax.rem(z + dz, 2) * 2 + lax.rem(core + dc, 2)
            for h in range(2):
                start = pl.multiple_of(HALF * h + 8 * i, 8)
                out_ref[:, :, pl.ds(start, 8), :] = ref[b, :, :, h]
            count += 1


def run_place(me, blocks):
    vmem = pl.BlockSpec(memory_space=pltpu.VMEM)
    return pl.pallas_call(
        place_kernel,
        out_shape=jax.ShapeDtypeStruct((LAYERS, 2, SIDE, SIDE), f32),
        in_specs=[pl.BlockSpec(memory_space=pltpu.SMEM)] + [vmem] * len(blocks),
        out_specs=vmem,
        compiler_params=pltpu.CompilerParams(vmem_limit_bytes=8 * 1024 * 1024),
        name="place",
    )(me, *blocks)


def shift(array, axis, by):
    count = lax.axis_size(axis)
    pairs = [(i, i + by) for i in range(count) if 0 <= i + by < count]
    return lax.ppermute(array, axis, pairs)


def shift_both(array, by):
    n_x, n_y = lax.axis_size("tx"), lax.axis_size("ty")
    pairs = [
        (a * n_y + b, (a + by) * n_y + b + by)
        for a in range(n_x)
        for b in range(n_y)
        if 0 <= a + by < n_x and 0 <= b + by < n_y
    ]
    return lax.ppermute(array, ("tx", "ty"), pairs)


def along_scan(array, dy, dz, dc):
    pairs = []
    for i in range(SCANS):
        y, z, core = i // 4, (i // 2) % 2, i % 2
        pairs.append((i, ((y + dy) % 4) * 4 + ((z + dz) % 2) * 2 + (core + dc) % 2))
    return lax.ppermute(array, "scan", pairs)


def on_device(object_slices, probe_modes, corners, measured):
    me = lax.axis_index("scan").astype(jnp.int32).reshape(1)
    corner = corners.reshape(2)
    rims = run_cut(me, object_slices)
    rims = (shift(rims[0], "tx", -1), shift(rims[1], "ty", -1), shift_both(rims[2], -1))
    light = run_glow(probe_modes)
    others = tuple(along_scan(rim, 0, 0, 1) for rim in rims)

    parts = run_wave(
        jnp.concatenate([corner, me % 2]),
        object_slices,
        rims + others,
        probe_modes,
        measured.reshape(SIDE, SIDE),
    )
    parts = lax.all_to_all(parts, "scan", 0, 0)
    own, to_right, to_below, to_diag = run_sum(me, parts, light)
    to_right = shift(to_right, "ty", 1)
    to_below = shift(to_below, "tx", 1)
    to_diag = shift_both(to_diag, 1)
    mine = run_update(me, object_slices, own, to_right, to_below, to_diag)[None]
    pair = jnp.concatenate([mine, along_scan(mine, 0, 1, 0)], axis=0)
    ring = [pair] + [along_scan(pair, dy, 0, 0) for dy in (1, 2, 3)]
    ring = jnp.concatenate(ring, axis=0)
    other = along_scan(ring, 0, 0, 1)
    return run_place(me, [ring, other])


def solution(mesh):
    placed = (
        P(None, None, "tx", "ty"),
        P(),
        P("tx", "ty", "scan", None),
        P("tx", "ty", "scan", None, None),
    )
    return jax.shard_map(
        on_device, mesh=mesh, in_specs=placed, out_specs=P(None, None, "tx", "ty"), check_vma=False
    )
```

time: 126 us -> 109 us (0.87)
  local copies, waits for them, and re-layouts: 10.3 us -> 1.87 us
  starting transfers between devices: 32 us -> 24.6 us
  waiting for transfers between devices: 43.9 us -> 40.3 us
  Pallas kernels: 37 us -> 39.7 us
    all_to_all x1 -> x0, starting transfers between devices: 7.38 us -> none  [on_device(): all_corners = lax.all_to_all(told, 'scan', 0, 0)[:, 0, :2]]
    pallas_call x1 -> x3, Pallas kernels: 30 us -> 36.3 us  [the longest x1 28.7 us: run_wave(): pl.pallas_call(wave_kernel, out_shape=jax.ShapeDtypeStruct((SCANS, 11, 8,...]
    ppermute x4, waiting for transfers between devices: 2.33 us -> 6.95 us  [shift(): return lax.ppermute(array, axis, pairs)]
    unnamed x32 -> x20, local copies, waits for them, and re-layouts: 6.03 us -> 1.86 us
    all_to_all x1, waiting for transfers between devices: 20.8 us -> 16.6 us  [on_device(): parts = lax.all_to_all(parts, 'scan', 0, 0)]
    ppermute x2, waiting for transfers between devices: 9.19 us -> 5.32 us  [shift_both(): return lax.ppermute(array, ('tx', 'ty'), pairs)]
    slice x3 -> x0, local copies, waits for them, and re-layouts: 3.62 us -> none  [the longest x1 2.02 us: on_device(): below = shift(object_slices[:, :, :HALF, :], 'tx', -1)]
    pallas_call x1, Pallas kernels: 1.96 us -> 0.03 us  [run_update(): pl.pallas_call(update_kernel, out_shape=jax.ShapeDtypeStruct((LAYERS, 2,...]
  transfers between devices with their start and end apart: 13 -> 15, of which waited for: 8 -> 8; matrix products, arithmetic and copies ran while one was open for 2% -> 1% of each run, Pallas kernels for 24% -> 5%
where the time goes in v2:
time: 109 us; the launch traced here: 108 us
  waiting for transfers between devices  40.3 us (37%)
  Pallas kernels  39.7 us (36%)
  starting transfers between devices  24.6 us (23%)
  local copies, waits for them, and re-layouts  1.87 us (2%)
  other arithmetic  1.27 us (1%)
    pallas_call x1, Pallas kernels, run_wave(): pl.pallas_call(wave_kernel, out_shape=jax.ShapeDtypeStruct((SCANS, 11, 8,...  28.7 us
    all_to_all x1, waiting for transfers between devices, on_device(): parts = lax.all_to_all(parts, 'scan', 0, 0)  16.6 us
    ppermute x8, waiting for transfers between devices, along_scan(): return lax.ppermute(array, 'scan', pairs)  11.3 us
    ppermute x4, starting transfers between devices, shift(): return lax.ppermute(array, axis, pairs)  9.05 us
    all_to_all x1, starting transfers between devices, on_device(): parts = lax.all_to_all(parts, 'scan', 0, 0)  7.51 us
    ppermute x4, waiting for transfers between devices, shift(): return lax.ppermute(array, axis, pairs)  6.95 us
    pallas_call x1, Pallas kernels, run_glow(): pl.pallas_call(glow_kernel, grid=(modes,), out_shape=jax.ShapeDtypeStruct...  5.55 us
    ppermute x8, starting transfers between devices, along_scan(): return lax.ppermute(array, 'scan', pairs)  5.47 us
  transfers between devices with their start and end apart: 15, of which 8 were waited for; matrix products, arithmetic and copies ran while one was open for 1% of the time, Pallas kernels for 5%

profile of v2, /device:TPU:34, one launch (start us, length us, event | category | flops | bytes accessed | tf_op | source)
XLA Modules:
  0.0 107.9 jit_solution(6377055892850325985)
XLA Ops:
  0.0 2.0 %cut.1 = (f32[2,128,256]{2,1,0:T(8,128)}, f32[2,256,128]{2,1,0:T(8,128)}, f32[2,128,128]{2,1,0:T(8,128)}) custom-call(s32[1]{0:T(128)} %bitcast.me_ref, f32[2,2,256,256]{3,2,1,0:T(8,128)} %object_ref.3), custom_call_target="tpu_custom_call" | custom-call | tf_op jit(solution)/shard_map/cut/pallas_call | solution.py:382
  2.0 2.4 %collective-permute-start = (f32[2,128,256]{2,1,0:T(8,128)}, f32[2,128,256]{2,1,0:T(8,128)S(1)}, u32[]{:S(2)}, u32[]{:S(2)}) collective-permute-start(f32[2,128,256]{2,1,0:T(8,128)} %get-tuple-element.12), channel_id=1, source_target_pairs={{2,0},{4,2},{6,4},{3,1},{5,3},{7,5},{10,8},{12,10},{14,12},{11,9},... | collective-permute-start | bytes 786440 | tf_op jit(solution)/shard_map/ppermute | solution.py:564
  4.5 1.9 %collective-permute-start.1 = (f32[2,256,128]{2,1,0:T(8,128)}, f32[2,256,128]{2,1,0:T(8,128)S(1)}, u32[]{:S(2)}, u32[]{:S(2)}) collective-permute-start(f32[2,256,128]{2,1,0:T(8,128)} %get-tuple-element.13), channel_id=1, source_target_pairs={{1,0},{3,2},{5,4},{7,6},{9,8},{11,10},{13,12},{15,14},{17,16},{19,... | collective-permute-start | bytes 786440 | tf_op jit(solution)/shard_map/ppermute | solution.py:564
  6.4 1.3 %collective-permute-start.2 = (f32[2,128,128]{2,1,0:T(8,128)}, f32[2,128,128]{2,1,0:T(8,128)S(1)}, u32[]{:S(2)}, u32[]{:S(2)}) collective-permute-start(f32[2,128,128]{2,1,0:T(8,128)} %get-tuple-element.14), channel_id=1, source_target_pairs={{3,0},{5,2},{7,4},{11,8},{13,10},{15,12},{19,16},{21,18},{23,20},{... | collective-permute-start | bytes 393224 | tf_op jit(solution)/shard_map/ppermute | solution.py:575
  7.7 5.6 %collective-permute-done.below_ref = f32[2,128,256]{2,1,0:T(8,128)S(1)} collective-permute-done((f32[2,128,256]{2,1,0:T(8,128)}, f32[2,128,256]{2,1,0:T(8,128)S(1)}, u32[]{:S(2)}, u32[]{:S(2)}) %collective-permute-start) | collective-permute-done | bytes 262176 | tf_op jit(solution)/shard_map/ppermute | solution.py:564
  13.3 0.0 copy-start.2
  13.3 0.0 collective-permute-start.3
  13.3 1.3 %collective-permute-done.1.right_ref = f32[2,256,128]{2,1,0:T(8,128)S(1)} collective-permute-done((f32[2,256,128]{2,1,0:T(8,128)}, f32[2,256,128]{2,1,0:T(8,128)S(1)}, u32[]{:S(2)}, u32[]{:S(2)}) %collective-permute-start.1) | collective-permute-done | bytes 262176 | tf_op jit(solution)/shard_map/ppermute | solution.py:564
  14.7 0.0 copy-start.3
  14.7 0.0 collective-permute-start.4
  14.7 0.0 collective-permute-done.2.diag_ref
  14.7 0.0 copy-start.6
  14.7 0.5 collective-permute-start.5
  15.2 1.3 %pad_add_fusion.corner_ref = s32[3]{0:T(128)} fusion(s32[1]{0:T(128)S(6)} %select_n.7, s32[2]{0:T(128)} %bitcast.8), kind=kLoop, calls=%fused_computation.6 | loop fusion | flops 3 | bytes 24 | tf_op jit(solution)/shard_map/concatenate | solution.py:595
  16.5 0.0 collective-permute-done.5.other_diag_ref
  16.5 0.0 copy-start.7
  16.5 0.0 collective-permute-done.3.other_below_ref
  16.5 0.0 copy-start.4
  16.5 0.0 collective-permute-done.4.other_right_ref
  16.5 0.0 copy-start.5
  16.5 0.0 copy-done.2
  16.5 0.0 copy-done.3
  16.5 0.0 copy-done.6
  16.5 0.6 copy-done.7
  17.1 0.1 copy-done.4
  17.2 0.1 copy-done.5
  17.3 28.7 %wave.1 = f32[16,11,8,256]{3,2,1,0:T(8,128)} custom-call(s32[3]{0:T(128)} %pad_add_fusion.corner_ref, f32[2,128,256]{2,1,0:T(8,128)} %copy-done.2, f32[2,256,128]{2,1,0:T(8,128)} %copy-done.3, f32[2,128,128]{2,1,0:T(8,128)} %copy-done.6, f32[2,128,256]{2,1,0:T(8,128)} %copy-done.4, f32[2,256,128]{2,1,0:T(8,128)} %copy-done.5, f32[2,128,128]{2,1,0:T(8,128)} %copy-done.7, ...), custom_call_target="tpu_custom_call" | custom-call | tf_op jit(solution)/shard_map/wave/pallas_call | solution.py:403
  46.0 7.5 %all-to-all-start = ((f32[16,11,8,256]{3,2,1,0:T(8,128)}), f32[16,11,8,256]{3,2,1,0:T(8,128)S(1)}, u32[]{:S(2)}, u32[]{:S(2)}) async-start(f32[16,11,8,256]{3,2,1,0:T(8,128)} %wave.1), calls=%async_computation | async-start | bytes 2883584 | tf_op jit(solution)/shard_map/all_to_all | solution.py:601
  53.6 5.5 %glow.1.light_ref = f32[512,256]{1,0:T(8,128)} custom-call(f32[2,8,256,256]{3,2,1,0:T(8,128)} %probe_ref.3), custom_call_target="tpu_custom_call" | custom-call | flops 2097152 | bytes 4194304 | tf_op jit(solution)/shard_map/glow/pallas_call | solution.py:346
  59.1 0.0 copy-start
  59.1 16.6 %all-to-all-done.parts_ref = f32[16,11,8,256]{3,2,1,0:T(8,128)S(1)} async-done(((f32[16,11,8,256]{3,2,1,0:T(8,128)}), f32[16,11,8,256]{3,2,1,0:T(8,128)S(1)}, u32[]{:S(2)}, u32[]{:S(2)}) %all-to-all-start) | async-done | bytes 1441824 | tf_op jit(solution)/shard_map/all_to_all | solution.py:601
  75.7 0.0 copy-start.1
  75.7 1.0 copy-done.1
  76.8 2.3 %sum.1 = (f32[6,2,8,256]{3,2,1,0:T(8,128)S(1)}, f32[6,2,8,128]{3,2,1,0:T(8,128)S(1)}, f32[6,8,256]{2,1,0:T(8,128)S(1)}, f32[6,8,128]{2,1,0:T(8,128)S(1)}) custom-call(s32[1]{0:T(128)} %bitcast.me_ref, f32[16,11,8,256]{3,2,1,0:T(8,128)S(1)} %all-to-all-done.parts_ref, f32[512,256]{1,0:T(8,128)S(1)} %copy-done.1), custom_call_target="tpu_custom_call" | custom-call | tf_op jit(solution)/shard_map/sum/pallas_call | solution.py:484
  79.1 1.3 %collective-permute-start.6 = (f32[6,2,8,128]{3,2,1,0:T(8,128)S(1)}, f32[6,2,8,128]{3,2,1,0:T(8,128)S(1)}, u32[]{:S(2)}, u32[]{:S(2)}) collective-permute-start(f32[6,2,8,128]{3,2,1,0:T(8,128)S(1)} %get-tuple-element.16), channel_id=1, source_target_pairs={{0,1},{2,3},{4,5},{6,7},{8,9},{10,11},{12,13},{14,15},{16,17},{18,... | collective-permute-start | bytes 147464 | tf_op jit(solution)/shard_map/ppermute | solution.py:564
  80.4 3.4 %collective-permute-start.7 = (f32[6,8,256]{2,1,0:T(8,128)S(1)}, f32[6,8,256]{2,1,0:T(8,128)S(1)}, u32[]{:S(2)}, u32[]{:S(2)}) collective-permute-start(f32[6,8,256]{2,1,0:T(8,128)S(1)} %get-tuple-element.17), channel_id=1, source_target_pairs={{0,2},{2,4},{4,6},{1,3},{3,5},{5,7},{8,10},{10,12},{12,14},{9,11},... | collective-permute-start | bytes 147464 | tf_op jit(solution)/shard_map/ppermute | solution.py:564
  83.8 1.3 %collective-permute-start.8 = (f32[6,8,128]{2,1,0:T(8,128)S(1)}, f32[6,8,128]{2,1,0:T(8,128)S(1)}, u32[]{:S(2)}, u32[]{:S(2)}) collective-permute-start(f32[6,8,128]{2,1,0:T(8,128)S(1)} %get-tuple-element.18), channel_id=1, source_target_pairs={{0,3},{2,5},{4,7},{8,11},{10,13},{12,15},{16,19},{18,21},{20,23},{... | collective-permute-start | bytes 73736 | tf_op jit(solution)/shard_map/ppermute | solution.py:575
  85.1 5.3 %collective-permute-done.8.diag_ref = f32[6,8,128]{2,1,0:T(8,128)S(1)} collective-permute-done((f32[6,8,128]{2,1,0:T(8,128)S(1)}, f32[6,8,128]{2,1,0:T(8,128)S(1)}, u32[]{:S(2)}, u32[]{:S(2)}) %collective-permute-start.8) | collective-permute-done | bytes 24608 | tf_op jit(solution)/shard_map/ppermute | solution.py:575
  90.4 0.0 collective-permute-done.6.right_ref
  90.4 0.0 collective-permute-done.7.below_ref
  90.4 0.0 copy-done
  90.5 1.0 collective-permute-start.9
  91.4 4.9 %collective-permute-done.9 = f32[1,2,2,2,8,256]{5,4,3,2,1,0:T(8,128)S(1)} collective-permute-done((f32[1,2,2,2,8,256]{5,4,3,2,1,0:T(8,128)S(1)}, f32[1,2,2,2,8,256]{5,4,3,2,1,0:T(8,128)S(1)}, u32[]{:S(2)}, u32[]{:S(2)}) %collective-permute-start.9) | collective-permute-done | bytes 65568 | tf_op jit(solution)/shard_map/ppermute | solution.py:583
  96.3 0.2 collective-permute-start.10
  96.6 2.3 %collective-permute-start.11 = (f32[2,2,2,2,8,256]{5,4,3,2,1,0:T(8,128)S(1)}, f32[2,2,2,2,8,256]{5,4,3,2,1,0:T(8,128)S(1)}, u32[]{:S(2)}, u32[]{:S(2)}) collective-permute-start(f32[2,2,2,2,8,256]{5,4,3,2,1,0:T(8,128)S(1)} %pad_maximum_fusion), channel_id=1, source_target_pairs={{0,64},{8,72},{16,80},{24,88},{32,96},{40,104},{48,112},{56,120},{... | collective-permute-start | bytes 393224 | tf_op jit(solution)/shard_map/ppermute | solution.py:583
  98.9 1.3 %collective-permute-start.12 = (f32[2,2,2,2,8,256]{5,4,3,2,1,0:T(8,128)S(1)}, f32[2,2,2,2,8,256]{5,4,3,2,1,0:T(8,128)S(1)}, u32[]{:S(2)}, u32[]{:S(2)}) collective-permute-start(f32[2,2,2,2,8,256]{5,4,3,2,1,0:T(8,128)S(1)} %pad_maximum_fusion), channel_id=1, source_target_pairs={{0,96},{8,104},{16,112},{24,120},{32,0},{40,8},{48,16},{56,24},{64... | collective-permute-start | bytes 393224 | tf_op jit(solution)/shard_map/ppermute | solution.py:583
  100.2 3.7 %collective-permute-done.10 = f32[2,2,2,2,8,256]{5,4,3,2,1,0:T(8,128)S(1)} collective-permute-done((f32[2,2,2,2,8,256]{5,4,3,2,1,0:T(8,128)S(1)}, f32[2,2,2,2,8,256]{5,4,3,2,1,0:T(8,128)S(1)}, u32[]{:S(2)}, u32[]{:S(2)}) %collective-permute-start.10) | collective-permute-done | bytes 131104 | tf_op jit(solution)/shard_map/ppermute | solution.py:583
  104.0 0.0 collective-permute-done.11
  104.0 0.8 collective-permute-done.12
  104.8 0.1 collective-permute-start.13
  104.9 1.9 %collective-permute-done.13.refs_1_ = f32[8,2,2,2,8,256]{5,4,3,2,1,0:T(8,128)S(1)} collective-permute-done((f32[8,2,2,2,8,256]{5,4,3,2,1,0:T(8,128)S(1)}, f32[8,2,2,2,8,256]{5,4,3,2,1,0:T(8,128)S(1)}, u32[]{:S(2)}, u32[]{:S(2)}) %collective-permute-start.13) | collective-permute-done | bytes 524320 | tf_op jit(solution)/shard_map/ppermute | solution.py:583
  106.8 1.1 place.1
  (7 shorter events, 0.1 us)
Async XLA Ops:
  2.0 11.3 %collective-permute-start = (f32[2,128,256]{2,1,0:T(8,128)}, f32[2,128,256]{2,1,0:T(8,128)S(1)}, u32[]{:S(2)}, u32[]{:S(2)}) collective-permute-start(f32[2,128,256]{2,1,0:T(8,128)} %get-tuple-element.12), channel_id=1, source_target_pairs={{2,0},{4,2},{6,4},{3,1},{5,3},{7,5},{10,8},{12,10},{14,12},{11,9},... | collective-permute-start | bytes 786440 | tf_op jit(solution)/shard_map/ppermute | solution.py:564
  4.5 10.2 %collective-permute-start.1 = (f32[2,256,128]{2,1,0:T(8,128)}, f32[2,256,128]{2,1,0:T(8,128)S(1)}, u32[]{:S(2)}, u32[]{:S(2)}) collective-permute-start(f32[2,256,128]{2,1,0:T(8,128)} %get-tuple-element.13), channel_id=1, source_target_pairs={{1,0},{3,2},{5,4},{7,6},{9,8},{11,10},{13,12},{15,14},{17,16},{19,... | collective-permute-start | bytes 786440 | tf_op jit(solution)/shard_map/ppermute | solution.py:564
  6.4 8.3 %collective-permute-start.2 = (f32[2,128,128]{2,1,0:T(8,128)}, f32[2,128,128]{2,1,0:T(8,128)S(1)}, u32[]{:S(2)}, u32[]{:S(2)}) collective-permute-start(f32[2,128,128]{2,1,0:T(8,128)} %get-tuple-element.14), channel_id=1, source_target_pairs={{3,0},{5,2},{7,4},{11,8},{13,10},{15,12},{19,16},{21,18},{23,20},{... | collective-permute-start | bytes 393224 | tf_op jit(solution)/shard_map/ppermute | solution.py:575
  13.3 3.2 %copy-start.2 = (f32[2,128,256]{2,1,0:T(8,128)}, f32[2,128,256]{2,1,0:T(8,128)S(1)}, u32[]{:S(2)}) copy-start(f32[2,128,256]{2,1,0:T(8,128)S(1)} %collective-permute-done.below_ref) | copy-start | bytes 786436
  13.3 3.1 %collective-permute-start.3 = (f32[2,128,256]{2,1,0:T(8,128)S(1)}, f32[2,128,256]{2,1,0:T(8,128)S(1)}, u32[]{:S(2)}, u32[]{:S(2)}) collective-permute-start(f32[2,128,256]{2,1,0:T(8,128)S(1)} %collective-permute-done.below_ref), channel_id=1, source_target_pairs={{0,8},{8,0},{16,24},{24,16},{32,40},{40,32},{48,56},{56,48},{64,72... | collective-permute-start | bytes 786440 | tf_op jit(solution)/shard_map/ppermute | solution.py:583
  14.7 1.8 %copy-start.3 = (f32[2,256,128]{2,1,0:T(8,128)}, f32[2,256,128]{2,1,0:T(8,128)S(1)}, u32[]{:S(2)}) copy-start(f32[2,256,128]{2,1,0:T(8,128)S(1)} %collective-permute-done.1.right_ref) | copy-start | bytes 786436
  14.7 1.8 %collective-permute-start.4 = (f32[2,256,128]{2,1,0:T(8,128)S(1)}, f32[2,256,128]{2,1,0:T(8,128)S(1)}, u32[]{:S(2)}, u32[]{:S(2)}) collective-permute-start(f32[2,256,128]{2,1,0:T(8,128)S(1)} %collective-permute-done.1.right_ref), channel_id=1, source_target_pairs={{0,8},{8,0},{16,24},{24,16},{32,40},{40,32},{48,56},{56,48},{64,72... | collective-permute-start | bytes 786440 | tf_op jit(solution)/shard_map/ppermute | solution.py:583
  14.7 1.8 %copy-start.6 = (f32[2,128,128]{2,1,0:T(8,128)}, f32[2,128,128]{2,1,0:T(8,128)S(1)}, u32[]{:S(2)}) copy-start(f32[2,128,128]{2,1,0:T(8,128)S(1)} %collective-permute-done.2.diag_ref) | copy-start | bytes 393220
  14.7 1.8 %collective-permute-start.5 = (f32[2,128,128]{2,1,0:T(8,128)S(1)}, f32[2,128,128]{2,1,0:T(8,128)S(1)}, u32[]{:S(2)}, u32[]{:S(2)}) collective-permute-start(f32[2,128,128]{2,1,0:T(8,128)S(1)} %collective-permute-done.2.diag_ref), channel_id=1, source_target_pairs={{0,8},{8,0},{16,24},{24,16},{32,40},{40,32},{48,56},{56,48},{64,72... | collective-permute-start | bytes 393224 | tf_op jit(solution)/shard_map/ppermute | solution.py:583
  16.5 0.7 copy-start.7
  16.5 0.8 copy-start.4
  16.5 0.8 copy-start.5
  46.0 29.7 %all-to-all-start = ((f32[16,11,8,256]{3,2,1,0:T(8,128)}), f32[16,11,8,256]{3,2,1,0:T(8,128)S(1)}, u32[]{:S(2)}, u32[]{:S(2)}) async-start(f32[16,11,8,256]{3,2,1,0:T(8,128)} %wave.1), calls=%async_computation | async-start | bytes 2883584 | tf_op jit(solution)/shard_map/all_to_all | solution.py:601
  59.1 31.3 %copy-start = (f32[2,2,256,256]{3,2,1,0:T(8,128)S(1)}, f32[2,2,256,256]{3,2,1,0:T(8,128)}, u32[]{:S(2)}) copy-start(f32[2,2,256,256]{3,2,1,0:T(8,128)} %object_ref.3) | copy-start | bytes 3145732
  75.7 1.0 copy-start.1
  79.1 11.3 %collective-permute-start.6 = (f32[6,2,8,128]{3,2,1,0:T(8,128)S(1)}, f32[6,2,8,128]{3,2,1,0:T(8,128)S(1)}, u32[]{:S(2)}, u32[]{:S(2)}) collective-permute-start(f32[6,2,8,128]{3,2,1,0:T(8,128)S(1)} %get-tuple-element.16), channel_id=1, source_target_pairs={{0,1},{2,3},{4,5},{6,7},{8,9},{10,11},{12,13},{14,15},{16,17},{18,... | collective-permute-start | bytes 147464 | tf_op jit(solution)/shard_map/ppermute | solution.py:564
  80.4 10.0 %collective-permute-start.7 = (f32[6,8,256]{2,1,0:T(8,128)S(1)}, f32[6,8,256]{2,1,0:T(8,128)S(1)}, u32[]{:S(2)}, u32[]{:S(2)}) collective-permute-start(f32[6,8,256]{2,1,0:T(8,128)S(1)} %get-tuple-element.17), channel_id=1, source_target_pairs={{0,2},{2,4},{4,6},{1,3},{3,5},{5,7},{8,10},{10,12},{12,14},{9,11},... | collective-permute-start | bytes 147464 | tf_op jit(solution)/shard_map/ppermute | solution.py:564
  83.8 6.6 %collective-permute-start.8 = (f32[6,8,128]{2,1,0:T(8,128)S(1)}, f32[6,8,128]{2,1,0:T(8,128)S(1)}, u32[]{:S(2)}, u32[]{:S(2)}) collective-permute-start(f32[6,8,128]{2,1,0:T(8,128)S(1)} %get-tuple-element.18), channel_id=1, source_target_pairs={{0,3},{2,5},{4,7},{8,11},{10,13},{12,15},{16,19},{18,21},{20,23},{... | collective-permute-start | bytes 73736 | tf_op jit(solution)/shard_map/ppermute | solution.py:575
  90.5 5.8 %collective-permute-start.9 = (f32[1,2,2,2,8,256]{5,4,3,2,1,0:T(8,128)S(1)}, f32[1,2,2,2,8,256]{5,4,3,2,1,0:T(8,128)S(1)}, u32[]{:S(2)}, u32[]{:S(2)}) collective-permute-start(f32[1,2,2,2,8,256]{5,4,3,2,1,0:T(8,128)S(1)} %bitcast.5), channel_id=1, source_target_pairs={{0,16},{8,24},{16,0},{24,8},{32,48},{40,56},{48,32},{56,40},{64,80... | collective-permute-start | bytes 196616 | tf_op jit(solution)/shard_map/ppermute | solution.py:583
  96.3 7.7 %collective-permute-start.10 = (f32[2,2,2,2,8,256]{5,4,3,2,1,0:T(8,128)S(1)}, f32[2,2,2,2,8,256]{5,4,3,2,1,0:T(8,128)S(1)}, u32[]{:S(2)}, u32[]{:S(2)}) collective-permute-start(f32[2,2,2,2,8,256]{5,4,3,2,1,0:T(8,128)S(1)} %pad_maximum_fusion), channel_id=1, source_target_pairs={{0,32},{8,40},{16,48},{24,56},{32,64},{40,72},{48,80},{56,88},{64,... | collective-permute-start | bytes 393224 | tf_op jit(solution)/shard_map/ppermute | solution.py:583
  96.6 7.4 %collective-permute-start.11 = (f32[2,2,2,2,8,256]{5,4,3,2,1,0:T(8,128)S(1)}, f32[2,2,2,2,8,256]{5,4,3,2,1,0:T(8,128)S(1)}, u32[]{:S(2)}, u32[]{:S(2)}) collective-permute-start(f32[2,2,2,2,8,256]{5,4,3,2,1,0:T(8,128)S(1)} %pad_maximum_fusion), channel_id=1, source_target_pairs={{0,64},{8,72},{16,80},{24,88},{32,96},{40,104},{48,112},{56,120},{... | collective-permute-start | bytes 393224 | tf_op jit(solution)/shard_map/ppermute | solution.py:583
  98.9 5.9 %collective-permute-start.12 = (f32[2,2,2,2,8,256]{5,4,3,2,1,0:T(8,128)S(1)}, f32[2,2,2,2,8,256]{5,4,3,2,1,0:T(8,128)S(1)}, u32[]{:S(2)}, u32[]{:S(2)}) collective-permute-start(f32[2,2,2,2,8,256]{5,4,3,2,1,0:T(8,128)S(1)} %pad_maximum_fusion), channel_id=1, source_target_pairs={{0,96},{8,104},{16,112},{24,120},{32,0},{40,8},{48,16},{56,24},{64... | collective-permute-start | bytes 393224 | tf_op jit(solution)/shard_map/ppermute | solution.py:583
  104.8 2.0 %collective-permute-start.13 = (f32[8,2,2,2,8,256]{5,4,3,2,1,0:T(8,128)S(1)}, f32[8,2,2,2,8,256]{5,4,3,2,1,0:T(8,128)S(1)}, u32[]{:S(2)}, u32[]{:S(2)}) collective-permute-start(f32[8,2,2,2,8,256]{5,4,3,2,1,0:T(8,128)S(1)} %constant_dynamic-update-slice_fusion.refs_0_), channel_id=1, source_target_pairs={{0,8},{8,0},{16,24},{24,16},{32,40},{40,32},{48,56},{56,48},{64,72... | collective-permute-start | bytes 1572872 | tf_op jit(solution)/shard_map/ppermute | solution.py:583

commit v3 on v2

--- a/solution.py
+++ b/solution.py
@@ -44,10 +44,7 @@
     left = [row_even, row_odd, row_even.conj().T, row_odd.conj().T]
     right = np.stack([stacked(real_right(t), 0) for t in right])
     left = np.stack([stacked(real_left(t), 1) for t in left])
-    order = np.zeros((SIDE, SIDE), np.float32)
-    order[2 * half, half] = 1.0
-    order[2 * half + 1, half + HALF] = 1.0
-    return right, left, order.astype(bf16)
+    return right, left
 
 
 def split(value):
@@ -122,17 +119,9 @@
     ]
 
 
-def arrange(value, order, axis):
-    high, low = split(value)
-    rest = (value - high.astype(f32) - low.astype(f32)).astype(bf16)
-    if axis == 1:
-        return mul(high, order) + mul(low, order) + mul(rest, order)
-    turned = order.T
-    return mul(turned, high) + mul(turned, low) + mul(turned, rest)
-
-
 def wave_kernel(
     corner_ref,
+    me_ref,
     below_ref,
     right_ref,
     diag_ref,
@@ -144,13 +133,11 @@
     measured_far,
     col_far,
     row_far,
-    order_far,
     out_ref,
     own_ref,
     measured_ref,
     col_tab,
     row_tab,
-    order_ref,
     hold,
     trans,
     wave,
@@ -162,9 +149,12 @@
     more_sems,
     field,
     turned,
-    across,
-    along,
+    across_0,
+    across_1,
+    along_0,
+    along_1,
 ):
+    across, along = (across_0, across_1), (along_0, along_1)
     r, c = corner_ref[0], corner_ref[1]
     modes = probe_ref.shape[1]
     own_copy = pltpu.make_async_copy(own_far, own_ref, more_sems.at[0])
@@ -172,10 +162,9 @@
         pltpu.make_async_copy(source, target, more_sems.at[n + 1])
         for n, (source, target) in enumerate(
             [
-                (order_far, order_ref),
-                (measured_far, measured_ref),
                 (col_far, col_tab),
                 (row_far, row_tab),
+                (measured_far, measured_ref),
             ]
         )
     ]
@@ -195,7 +184,7 @@
     own_copy.wait()
     for s in range(LAYERS):
         for p in range(2):
-            held = corner_ref[2] == p
+            held = lax.rem(me_ref[0], 2) == p
             right = jnp.where(held, right_ref[s], other_right_ref[s])
             below = jnp.where(held, below_ref[s], other_below_ref[s])
             diag = jnp.where(held, diag_ref[s], other_diag_ref[s])
@@ -213,42 +202,45 @@
                 view = hold[h, pl.ds(r, SIDE)]
                 trans[s, p, h] = view + 1.0 if p == 0 else view
 
-    for copy in later:
-        copy.wait()
-    order = order_ref[...]
-    misfit[...] = -arrange(arrange(measured_ref[...], order, 1), order, 0)
+    misfit[...] = jnp.zeros_like(misfit)
     total[...] = jnp.zeros_like(total)
     field[...] = jnp.zeros_like(field)
     turned[...] = jnp.zeros_like(turned)
+    far[modes] = jnp.zeros_like(far[modes])
     starts = range(0, SIDE, ROWS)
 
-    def forward(m, carry):
-        for copy in probe_copies(probe_ref, probe, sems, m):
-            copy.wait()
+    def enter(m, side):
+        held = jnp.minimum(m, modes - 1)
         for start in starts:
             rows, inner = pl.ds(start, ROWS), pl.ds(start + PAD, ROWS)
             for h in range(2):
-                p_re, p_im = probe[0, m, h, rows], probe[1, m, h, rows]
+                p_re, p_im = probe[0, held, h, rows], probe[1, held, h, rows]
                 t_re, t_im = trans[0, 0, h, rows], trans[0, 1, h, rows]
-                field[0, h, inner] = p_re * t_re - p_im * t_im
-                field[1, h, inner] = p_re * t_im + p_im * t_re
+                field[side, 0, h, inner] = p_re * t_re - p_im * t_im
+                field[side, 1, h, inner] = p_re * t_im + p_im * t_re
+            yield
         for start in starts:
-            turn_rows(field, turned, start, 1.0)
+            turn_rows(field.at[side], turned, start, 1.0)
+            yield
         for start in starts:
             rows = pl.ds(start, ROWS)
             x = []
-            for h, (w_re, w_im) in enumerate(end_rows(field, turned, start)):
+            for h, (w_re, w_im) in enumerate(end_rows(field.at[side], turned, start)):
                 wave[0, m, h, rows] = w_re
                 wave[1, m, h, rows] = w_im
-                total[2, h, rows] += w_re * w_re + w_im * w_im
                 t_re, t_im = trans[1, 0, h, rows], trans[1, 1, h, rows]
                 x.append(
                     jnp.concatenate([w_re * t_re - w_im * t_im, w_re * t_im + w_im * t_re], axis=1)
                 )
-            put(across, (0,), rows, x[0] + x[1])
-            put(across, (1,), rows, x[0] - x[1])
-        even = right_dot(across, 0, col_tab, 0)
-        odd = right_dot(across, 1, col_tab, 1)
+            put(across[side], (0,), rows, x[0] + x[1])
+            put(across[side], (1,), rows, x[0] - x[1])
+            yield
+
+    def transform(m, side):
+        even = right_dot(across[side], 0, col_tab, 0)
+        yield
+        odd = right_dot(across[side], 1, col_tab, 1)
+        yield
         for start in range(0, HALF, ROWS):
             for q in range(2):
                 lanes = slice(HALF * q, HALF * (q + 1))
@@ -257,26 +249,57 @@
                     for part in (slice(start, start + ROWS), slice(start + HALF, start + HALF + ROWS))
                 ]
                 rows = pl.ds(HALF * q + start, ROWS)
-                put(along, (0,), rows, above + under)
-                put(along, (1,), rows, above - under)
+                put(along[side], (0,), rows, above + under)
+                put(along[side], (1,), rows, above - under)
+            yield
         for e in range(2):
-            found = left_dot(row_tab, e, along, e)
-            far[m, e] = found
-            misfit[pl.ds(HALF * e, HALF)] += found[:HALF] * found[:HALF] + found[HALF:] * found[HALF:]
+            found = left_dot(row_tab, e, along[side], e)
+            yield
+            for start in range(0, HALF, ROWS):
+                re, im = found[start : start + ROWS], found[HALF + start : HALF + start + ROWS]
+                far[m, e, pl.ds(start, ROWS)] = re
+                far[m, e, pl.ds(HALF + start, ROWS)] = im
+                misfit[pl.ds(HALF * e + start, ROWS)] += re * re + im * im
+                yield
+        for start in starts:
+            rows = pl.ds(start, ROWS)
+            for h in range(2):
+                w_re, w_im = wave[0, m, h, rows], wave[1, m, h, rows]
+                total[2, h, rows] += w_re * w_re + w_im * w_im
+            yield
+
+    def beside(*parts):
+        live = list(parts)
+        while live:
+            live = [part for part in live if next(part, live) is not live]
+
+    for m in range(modes):
+        for copy in probe_copies(probe_ref, probe, sems, m):
+            copy.wait()
+    beside(enter(0, 0))
+    for copy in later:
+        copy.wait()
+
+    def forward(j, carry):
+        beside(transform(2 * j, 0), enter(2 * j + 1, 1))
+        beside(transform(2 * j + 1, 1), enter(2 * j + 2, 0))
         return carry
 
-    lax.fori_loop(0, modes, forward, 0)
-    misfit[...] = 2.0 * misfit[...]
-
-    def backward(m, carry):
+    lax.fori_loop(0, modes // 2, forward, 0)
+    misfit[...] = 2.0 * (misfit[...] - measured_ref[...])
+
+    def restore(m, side):
         for e in range(2):
             for start in range(0, HALF, ROWS):
                 scale = misfit[pl.ds(HALF * e + start, ROWS)]
                 for q in range(2):
                     rows = pl.ds(HALF * q + start, ROWS)
-                    put(along, (e,), rows, scale * far[m, e, rows])
-        even = left_dot(row_tab, 2, along, 0)
-        odd = left_dot(row_tab, 3, along, 1)
+                    put(along[side], (e,), rows, scale * far[m, e, rows])
+                yield
+        even = left_dot(row_tab, 2, along[side], 0)
+        yield
+        odd = left_dot(row_tab, 3, along[side], 1)
+        yield
         for start in range(0, HALF, ROWS):
             re, im = slice(start, start + ROWS), slice(HALF + start, HALF + start + ROWS)
             for n in range(2):
@@ -286,13 +309,16 @@
                 for q in range(2):
                     lanes = slice(HALF * q, HALF * (q + 1))
                     put(
-                        across,
+                        across[side],
                         (q,),
                         rows,
                         jnp.concatenate([f_re[:, lanes], f_im[:, lanes]], axis=1),
                     )
-        first = right_dot(across, 0, col_tab, 2)
-        second = right_dot(across, 1, col_tab, 3)
+            yield
+        first = right_dot(across[side], 0, col_tab, 2)
+        yield
+        second = right_dot(across[side], 1, col_tab, 3)
+        yield
         for start in starts:
             rows, inner = pl.ds(start, ROWS), pl.ds(start + PAD, ROWS)
             part = slice(start, start + ROWS)
@@ -303,19 +329,30 @@
                 total[0, h, rows] += w_re * b_re + w_im * b_im
                 total[1, h, rows] += w_re * b_im - w_im * b_re
                 t_re, t_im = trans[1, 0, h, rows], trans[1, 1, h, rows]
-                field[0, h, inner] = t_re * b_re + t_im * b_im
-                field[1, h, inner] = t_re * b_im - t_im * b_re
+                field[side, 0, h, inner] = t_re * b_re + t_im * b_im
+                field[side, 1, h, inner] = t_re * b_im - t_im * b_re
+            yield
+
+    def leave(m, side):
         for start in starts:
-            turn_rows(field, turned, start, -1.0)
+            turn_rows(field.at[side], turned, start, -1.0)
+            yield
         for start in starts:
             rows = pl.ds(start, ROWS)
-            for h, (d_re, d_im) in enumerate(end_rows(field, turned, start)):
+            for h, (d_re, d_im) in enumerate(end_rows(field.at[side], turned, start)):
                 p_re, p_im = probe[0, m, h, rows], probe[1, m, h, rows]
                 total[3, h, rows] += p_re * d_re + p_im * d_im
                 total[4, h, rows] += p_re * d_im - p_im * d_re
+            yield
+
+    beside(restore(0, 0))
+
+    def backward(j, carry):
+        beside(restore(2 * j + 1, 1), leave(2 * j, 0))
+        beside(restore(2 * j + 2, 0), leave(2 * j + 1, 1))
         return carry
 
-    lax.fori_loop(0, modes, backward, 0)
+    lax.fori_loop(0, modes // 2, backward, 0)
 
     for k in range(5):
         for h in range(2):
@@ -331,30 +368,53 @@
         out_ref[i, 10] = mark
 
 
-def glow_kernel(probe_ref, light_ref):
+def glow_kernel(probe_ref, measured_ref, light_ref, expected_ref):
     @pl.when(pl.program_id(0) == 0)
     def _():
         light_ref[...] = jnp.zeros_like(light_ref)
+        row = lax.broadcasted_iota(jnp.int32, (SIDE, SIDE), 0)
+        col = lax.broadcasted_iota(jnp.int32, (SIDE, SIDE), 1)
+        place = lambda k: jnp.where(k < HALF, 2 * k, 2 * (k - HALF) + 1)
+        by_col = (row == place(col)).astype(f32).astype(bf16)
+        by_row = (col == place(row)).astype(f32).astype(bf16)
+        value = measured_ref[...]
+        for left in (False, True):
+            high, low = split(value)
+            rest = (value - high.astype(f32) - low.astype(f32)).astype(bf16)
+            if left:
+                value = mul(by_row, high) + mul(by_row, low) + mul(by_row, rest)
+            else:
+                value = mul(high, by_col) + mul(low, by_col) + mul(rest, by_col)
+        expected_ref[...] = value
 
     light = probe_ref[0, 0] * probe_ref[0, 0] + probe_ref[1, 0] * probe_ref[1, 0]
     light_ref[:SIDE] += light
     light_ref[SIDE:] += light
 
 
-def run_glow(probe):
+def run_glow(probe, measured):
     modes = probe.shape[1]
     return pl.pallas_call(
         glow_kernel,
         grid=(modes,),
-        out_shape=jax.ShapeDtypeStruct((2 * SIDE, SIDE), f32),
-        in_specs=[pl.BlockSpec((2, 1, SIDE, SIDE), lambda m: (0, m, 0, 0))],
-        out_specs=pl.BlockSpec((2 * SIDE, SIDE), lambda m: (0, 0)),
+        out_shape=(
+            jax.ShapeDtypeStruct((2 * SIDE, SIDE), f32),
+            jax.ShapeDtypeStruct((SIDE, SIDE), f32),
+        ),
+        in_specs=[
+            pl.BlockSpec((2, 1, SIDE, SIDE), lambda m: (0, m, 0, 0)),
+            pl.BlockSpec((SIDE, SIDE), lambda m: (0, 0)),
+        ],
+        out_specs=(
+            pl.BlockSpec((2 * SIDE, SIDE), lambda m: (0, 0)),
+            pl.BlockSpec((SIDE, SIDE), lambda m: (0, 0)),
+        ),
         compiler_params=pltpu.CompilerParams(vmem_limit_bytes=60 * 1024 * 1024),
         cost_estimate=pl.CostEstimate(
             flops=4 * modes * SIDE * SIDE, bytes_accessed=8 * modes * SIDE * SIDE, transcendentals=0
         ),
         name="glow",
-    )(probe)
+    )(probe, measured)
 
 
 def cut_kernel(me_ref, object_ref, below_ref, right_ref, diag_ref, sems):
@@ -394,8 +454,8 @@
     )(me, current)
 
 
-def run_wave(corner, own, rims, probe, measured):
-    right_table, left_table, order = make_tables()
+def run_wave(corner, me, own, rims, probe, measured):
+    right_table, left_table = make_tables()
     modes = probe.shape[1]
     vmem = pl.BlockSpec(memory_space=pltpu.VMEM)
     field = (2, SIDE, HALF)
@@ -403,27 +463,28 @@
     return pl.pallas_call(
         wave_kernel,
         out_shape=jax.ShapeDtypeStruct((SCANS, 11, 8, SIDE), f32),
-        in_specs=[pl.BlockSpec(memory_space=pltpu.SMEM)]
+        in_specs=[pl.BlockSpec(memory_space=pltpu.SMEM)] * 2
         + [vmem] * 6
-        + [pl.BlockSpec(memory_space=pl.ANY)] * 6,
+        + [pl.BlockSpec(memory_space=pl.ANY)] * 5,
         out_specs=vmem,
         scratch_shapes=[
             pltpu.VMEM((LAYERS, 2, SIDE, SIDE), f32),
             pltpu.VMEM((SIDE, SIDE), f32),
             pltpu.VMEM((4, 3 * SIDE, SIDE), bf16),
             pltpu.VMEM((4, SIDE, 3 * SIDE), bf16),
-            pltpu.VMEM((SIDE, SIDE), bf16),
             pltpu.VMEM((2, 2 * SIDE, HALF), f32),
             pltpu.VMEM((LAYERS, 2) + field, f32),
-            pltpu.VMEM((2, modes) + field, f32),
-            pltpu.VMEM((modes, 2, SIDE, SIDE), f32),
+            pltpu.VMEM((2, modes + 1) + field, f32),
+            pltpu.VMEM((modes + 1, 2, SIDE, SIDE), f32),
             pltpu.VMEM((SIDE, SIDE), f32),
             pltpu.VMEM((5,) + field, f32),
             pltpu.VMEM((2, modes, 2, SIDE, HALF), f32),
             pltpu.SemaphoreType.DMA((2, modes, 2)),
-            pltpu.SemaphoreType.DMA((5,)),
+            pltpu.SemaphoreType.DMA((4,)),
+            pltpu.VMEM((2,) + wide, f32),
             pltpu.VMEM(wide, f32),
-            pltpu.VMEM(wide, f32),
+            pltpu.VMEM((2, 2, SIDE, SIDE), bf16),
+            pltpu.VMEM((2, 2, SIDE, SIDE), bf16),
             pltpu.VMEM((2, 2, SIDE, SIDE), bf16),
             pltpu.VMEM((2, 2, SIDE, SIDE), bf16),
         ],
@@ -431,13 +492,13 @@
         name="wave",
     )(
         corner,
+        me,
         *rims,
         own,
         probe,
         measured,
         jnp.asarray(right_table),
         jnp.asarray(left_table),
-        jnp.asarray(order),
     )
 
 
@@ -588,15 +649,17 @@
     corner = corners.reshape(2)
     rims = run_cut(me, object_slices)
     rims = (shift(rims[0], "tx", -1), shift(rims[1], "ty", -1), shift_both(rims[2], -1))
-    light = run_glow(probe_modes)
+    light, expected = run_glow(probe_modes, measured.reshape(SIDE, SIDE))
+    rims, light, expected = lax.optimization_barrier((rims, light, expected))
     others = tuple(along_scan(rim, 0, 0, 1) for rim in rims)
 
     parts = run_wave(
-        jnp.concatenate([corner, me % 2]),
+        corner,
+        me,
         object_slices,
         rims + others,
         probe_modes,
-        measured.reshape(SIDE, SIDE),
+        expected,
     )
     parts = lax.all_to_all(parts, "scan", 0, 0)
     own, to_right, to_below, to_diag = run_sum(me, parts, light)

time: 109 us -> 104 us (0.954)
  blocking collectives: 0 us -> 29.6 us
  waiting for transfers between devices: 40.3 us -> 21 us
  starting transfers between devices: 24.6 us -> 16.3 us
  Pallas kernels: 39.7 us -> 34.8 us
  other arithmetic: 1.27 us -> 0.01 us
    all_to_all x0 -> x1, blocking collectives: none -> 29.6 us  [on_device(): parts = lax.all_to_all(parts, 'scan', 0, 0)]
    all_to_all x1 -> x0, waiting for transfers between devices: 16.6 us -> none  [on_device(): parts = lax.all_to_all(parts, 'scan', 0, 0)]
    all_to_all x1 -> x0, starting transfers between devices: 7.51 us -> none  [on_device(): parts = lax.all_to_all(parts, 'scan', 0, 0)]
    ppermute x4, waiting for transfers between devices: 6.95 us -> 0.59 us  [shift(): return lax.ppermute(array, axis, pairs)]
    pallas_call x1, Pallas kernels: 28.7 us -> 23 us  [run_wave(): pl.pallas_call(wave_kernel, out_shape=jax.ShapeDtypeStruct((SCANS, 11, 8,...]
    ppermute x8, waiting for transfers between devices: 11.3 us -> 15.1 us  [along_scan(): return lax.ppermute(array, 'scan', pairs)]
    concatenate x1 -> x0, other arithmetic: 1.26 us -> none  [on_device(): jnp.concatenate([corner, me % 2])]
  transfers between devices with their start and end apart: 15 -> 14, of which waited for: 8 -> 7; matrix products, arithmetic and copies ran while one was open for 1% -> 0% of each run, Pallas kernels for 5% -> 6%
where the time goes in v3:
time: 104 us; the launch traced here: 103 us
  Pallas kernels  34.8 us (33%)
  blocking collectives  29.6 us (28%)
  waiting for transfers between devices  21 us (20%)
  starting transfers between devices  16.3 us (16%)
    all_to_all x1, blocking collectives, on_device(): parts = lax.all_to_all(parts, 'scan', 0, 0)  29.6 us
    pallas_call x1, Pallas kernels, run_wave(): pl.pallas_call(wave_kernel, out_shape=jax.ShapeDtypeStruct((SCANS, 11, 8,...  23 us
    ppermute x8, waiting for transfers between devices, along_scan(): return lax.ppermute(array, 'scan', pairs)  15.1 us
    ppermute x4, starting transfers between devices, shift(): return lax.ppermute(array, axis, pairs)  9.07 us
    pallas_call x1, Pallas kernels, run_glow(): pl.pallas_call(glow_kernel, grid=(modes,), out_shape=(jax.ShapeDtypeStruc...  6.34 us
    ppermute x2, waiting for transfers between devices, shift_both(): return lax.ppermute(array, ('tx', 'ty'), pairs)  5.32 us
    ppermute x8, starting transfers between devices, along_scan(): return lax.ppermute(array, 'scan', pairs)  4.59 us
    ppermute x2, starting transfers between devices, shift_both(): return lax.ppermute(array, ('tx', 'ty'), pairs)  2.59 us
  transfers between devices with their start and end apart: 14, of which 7 were waited for; matrix products, arithmetic and copies ran while one was open for 0% of the time, Pallas kernels for 6%

profile of v3, /device:TPU:34, one launch (start us, length us, event | category | flops | bytes accessed | tf_op | source)
XLA Modules:
  0.0 102.7 jit_solution(16860180692243866012)
XLA Ops:
  0.0 2.1 %cut.1 = (f32[2,128,256]{2,1,0:T(8,128)}, f32[2,256,128]{2,1,0:T(8,128)}, f32[2,128,128]{2,1,0:T(8,128)}) custom-call(s32[1]{0:T(128)} %bitcast.me_ref, f32[2,2,256,256]{3,2,1,0:T(8,128)} %object_ref.3), custom_call_target="tpu_custom_call" | custom-call | tf_op jit(solution)/shard_map/cut/pallas_call | solution.py:442
  2.1 2.4 %collective-permute-start = (f32[2,128,256]{2,1,0:T(8,128)}, f32[2,128,256]{2,1,0:T(8,128)S(1)}, u32[]{:S(2)}, u32[]{:S(2)}) collective-permute-start(f32[2,128,256]{2,1,0:T(8,128)} %get-tuple-element.19), channel_id=1, source_target_pairs={{2,0},{4,2},{6,4},{3,1},{5,3},{7,5},{10,8},{12,10},{14,12},{11,9},... | collective-permute-start | bytes 786440 | tf_op jit(solution)/shard_map/ppermute | solution.py:625
  4.5 1.9 %collective-permute-start.1 = (f32[2,256,128]{2,1,0:T(8,128)}, f32[2,256,128]{2,1,0:T(8,128)S(1)}, u32[]{:S(2)}, u32[]{:S(2)}) collective-permute-start(f32[2,256,128]{2,1,0:T(8,128)} %get-tuple-element.20), channel_id=1, source_target_pairs={{1,0},{3,2},{5,4},{7,6},{9,8},{11,10},{13,12},{15,14},{17,16},{19,... | collective-permute-start | bytes 786440 | tf_op jit(solution)/shard_map/ppermute | solution.py:625
  6.5 1.3 %collective-permute-start.2 = (f32[2,128,128]{2,1,0:T(8,128)}, f32[2,128,128]{2,1,0:T(8,128)S(1)}, u32[]{:S(2)}, u32[]{:S(2)}) collective-permute-start(f32[2,128,128]{2,1,0:T(8,128)} %get-tuple-element.21), channel_id=1, source_target_pairs={{3,0},{5,2},{7,4},{11,8},{13,10},{15,12},{19,16},{21,18},{23,20},{... | collective-permute-start | bytes 393224 | tf_op jit(solution)/shard_map/ppermute | solution.py:636
  7.8 6.3 %glow.1 = (f32[512,256]{1,0:T(8,128)}, f32[256,256]{1,0:T(8,128)}) custom-call(f32[2,8,256,256]{3,2,1,0:T(8,128)} %probe_ref.3, f32[256,256]{1,0:T(8,128)} %bitcast.7), custom_call_target="tpu_custom_call" | custom-call | flops 2097152 | bytes 4194304 | tf_op jit(solution)/shard_map/glow/pallas_call | solution.py:397
  14.1 0.0 collective-permute-done.2.diag_ref
  14.1 0.0 copy-start.6
  14.1 0.0 collective-permute-done.below_ref
  14.1 0.0 copy-start.2
  14.2 0.6 collective-permute-done.1.right_ref
  14.7 0.0 copy-start.3
  14.7 0.0 collective-permute-start.3
  14.7 0.5 collective-permute-start.4
  15.2 0.0 collective-permute-start.5
  15.3 1.6 %collective-permute-done.5.other_diag_ref = f32[2,128,128]{2,1,0:T(8,128)S(1)} collective-permute-done((f32[2,128,128]{2,1,0:T(8,128)S(1)}, f32[2,128,128]{2,1,0:T(8,128)S(1)}, u32[]{:S(2)}, u32[]{:S(2)}) %collective-permute-start.5) | collective-permute-done | bytes 131104 | tf_op jit(solution)/shard_map/ppermute | solution.py:644
  16.8 0.0 copy-start.7
  16.8 0.0 collective-permute-done.3.other_below_ref
  16.8 0.0 copy-start.4
  16.8 0.0 collective-permute-done.4.other_right_ref
  16.8 0.0 copy-start.5
  16.9 0.0 copy-done.6
  16.9 0.0 copy-done.2
  16.9 0.0 copy-done.3
  16.9 0.6 copy-done.7
  17.5 0.1 copy-done.4
  17.6 0.1 copy-done.5
  17.7 23.0 %wave.1 = f32[16,11,8,256]{3,2,1,0:T(8,128)} custom-call(s32[2]{0:T(128)} %bitcast.8, s32[1]{0:T(128)} %bitcast.me_ref, f32[2,128,256]{2,1,0:T(8,128)} %copy-done.2, f32[2,256,128]{2,1,0:T(8,128)} %copy-done.3, f32[2,128,128]{2,1,0:T(8,128)} %copy-done.6, f32[2,128,256]{2,1,0:T(8,128)} %copy-done.4, f32[2,256,128]{2,1,0:T(8,128)} %copy-done.5, ...), custom_call_target="tpu_custom_call" | custom-call | tf_op jit(solution)/shard_map/wave/pallas_call | solution.py:463
  40.7 0.0 copy-start.1
  40.7 29.6 %all_to_all.5.parts_ref = f32[16,11,8,256]{3,2,1,0:T(8,128)S(1)} all-to-all(f32[16,11,8,256]{3,2,1,0:T(8,128)} %wave.1), channel_id=1, replica_groups=mesh['scan'=16,'tx'=4,'ty'=2] {'scan'}, dimensions={0} | all-to-all | bytes 2883584 | tf_op jit(solution)/shard_map/all_to_all | solution.py:664
  70.3 0.0 copy-done.1
  70.3 0.0 copy-start
  70.3 2.3 %sum.1 = (f32[6,2,8,256]{3,2,1,0:T(8,128)S(1)}, f32[6,2,8,128]{3,2,1,0:T(8,128)S(1)}, f32[6,8,256]{2,1,0:T(8,128)S(1)}, f32[6,8,128]{2,1,0:T(8,128)S(1)}) custom-call(s32[1]{0:T(128)} %bitcast.me_ref, f32[16,11,8,256]{3,2,1,0:T(8,128)S(1)} %all_to_all.5.parts_ref, f32[512,256]{1,0:T(8,128)S(1)} %copy-done.1), custom_call_target="tpu_custom_call" | custom-call | tf_op jit(solution)/shard_map/sum/pallas_call | solution.py:545
  72.6 1.3 %collective-permute-start.6 = (f32[6,2,8,128]{3,2,1,0:T(8,128)S(1)}, f32[6,2,8,128]{3,2,1,0:T(8,128)S(1)}, u32[]{:S(2)}, u32[]{:S(2)}) collective-permute-start(f32[6,2,8,128]{3,2,1,0:T(8,128)S(1)} %get-tuple-element.30), channel_id=1, source_target_pairs={{0,1},{2,3},{4,5},{6,7},{8,9},{10,11},{12,13},{14,15},{16,17},{18,... | collective-permute-start | bytes 147464 | tf_op jit(solution)/shard_map/ppermute | solution.py:625
  73.9 3.4 %collective-permute-start.7 = (f32[6,8,256]{2,1,0:T(8,128)S(1)}, f32[6,8,256]{2,1,0:T(8,128)S(1)}, u32[]{:S(2)}, u32[]{:S(2)}) collective-permute-start(f32[6,8,256]{2,1,0:T(8,128)S(1)} %get-tuple-element.31), channel_id=1, source_target_pairs={{0,2},{2,4},{4,6},{1,3},{3,5},{5,7},{8,10},{10,12},{12,14},{9,11},... | collective-permute-start | bytes 147464 | tf_op jit(solution)/shard_map/ppermute | solution.py:625
  77.3 1.3 %collective-permute-start.8 = (f32[6,8,128]{2,1,0:T(8,128)S(1)}, f32[6,8,128]{2,1,0:T(8,128)S(1)}, u32[]{:S(2)}, u32[]{:S(2)}) collective-permute-start(f32[6,8,128]{2,1,0:T(8,128)S(1)} %get-tuple-element.32), channel_id=1, source_target_pairs={{0,3},{2,5},{4,7},{8,11},{10,13},{12,15},{16,19},{18,21},{20,23},{... | collective-permute-start | bytes 73736 | tf_op jit(solution)/shard_map/ppermute | solution.py:636
  78.6 5.3 %collective-permute-done.8.diag_ref = f32[6,8,128]{2,1,0:T(8,128)S(1)} collective-permute-done((f32[6,8,128]{2,1,0:T(8,128)S(1)}, f32[6,8,128]{2,1,0:T(8,128)S(1)}, u32[]{:S(2)}, u32[]{:S(2)}) %collective-permute-start.8) | collective-permute-done | bytes 24608 | tf_op jit(solution)/shard_map/ppermute | solution.py:636
  83.9 0.0 collective-permute-done.6.right_ref
  83.9 0.0 collective-permute-done.7.below_ref
  83.9 0.0 copy-done
  84.0 0.7 collective-permute-start.9
  84.7 5.1 %collective-permute-done.9 = f32[1,2,2,2,8,256]{5,4,3,2,1,0:T(8,128)S(1)} collective-permute-done((f32[1,2,2,2,8,256]{5,4,3,2,1,0:T(8,128)S(1)}, f32[1,2,2,2,8,256]{5,4,3,2,1,0:T(8,128)S(1)}, u32[]{:S(2)}, u32[]{:S(2)}) %collective-permute-start.9) | collective-permute-done | bytes 65568 | tf_op jit(solution)/shard_map/ppermute | solution.py:644
  89.8 0.1 collective-permute-start.10
  89.9 3.2 %collective-permute-start.12 = (f32[2,2,2,2,8,256]{5,4,3,2,1,0:T(8,128)S(1)}, f32[2,2,2,2,8,256]{5,4,3,2,1,0:T(8,128)S(1)}, u32[]{:S(2)}, u32[]{:S(2)}) collective-permute-start(f32[2,2,2,2,8,256]{5,4,3,2,1,0:T(8,128)S(1)} %pad_maximum_fusion), channel_id=1, source_target_pairs={{0,96},{8,104},{16,112},{24,120},{32,0},{40,8},{48,16},{56,24},{64... | collective-permute-start | bytes 393224 | tf_op jit(solution)/shard_map/ppermute | solution.py:644
  93.2 0.0 collective-permute-start.11
  93.2 4.0 %collective-permute-done.10 = f32[2,2,2,2,8,256]{5,4,3,2,1,0:T(8,128)S(1)} collective-permute-done((f32[2,2,2,2,8,256]{5,4,3,2,1,0:T(8,128)S(1)}, f32[2,2,2,2,8,256]{5,4,3,2,1,0:T(8,128)S(1)}, u32[]{:S(2)}, u32[]{:S(2)}) %collective-permute-start.10) | collective-permute-done | bytes 131104 | tf_op jit(solution)/shard_map/ppermute | solution.py:644
  97.2 2.5 %collective-permute-done.11 = f32[2,2,2,2,8,256]{5,4,3,2,1,0:T(8,128)S(1)} collective-permute-done((f32[2,2,2,2,8,256]{5,4,3,2,1,0:T(8,128)S(1)}, f32[2,2,2,2,8,256]{5,4,3,2,1,0:T(8,128)S(1)}, u32[]{:S(2)}, u32[]{:S(2)}) %collective-permute-start.11) | collective-permute-done | bytes 131104 | tf_op jit(solution)/shard_map/ppermute | solution.py:644
  99.6 0.0 collective-permute-done.12
  99.7 0.1 collective-permute-start.13
  99.8 1.9 %collective-permute-done.13.refs_1_ = f32[8,2,2,2,8,256]{5,4,3,2,1,0:T(8,128)S(1)} collective-permute-done((f32[8,2,2,2,8,256]{5,4,3,2,1,0:T(8,128)S(1)}, f32[8,2,2,2,8,256]{5,4,3,2,1,0:T(8,128)S(1)}, u32[]{:S(2)}, u32[]{:S(2)}) %collective-permute-start.13) | collective-permute-done | bytes 524320 | tf_op jit(solution)/shard_map/ppermute | solution.py:644
  101.7 1.1 %place.1 = f32[2,2,256,256]{3,2,1,0:T(8,128)} custom-call(s32[1]{0:T(128)} %bitcast.me_ref, f32[8,2,2,2,8,256]{5,4,3,2,1,0:T(8,128)S(1)} %constant_dynamic-update-slice_fusion.refs_0_, f32[8,2,2,2,8,256]{5,4,3,2,1,0:T(8,128)S(1)} %collective-permute-done.13.refs_1_), custom_call_target="tpu_custom_call" | custom-call | tf_op jit(solution)/shard_map/place/pallas_call | solution.py:612
  (7 shorter events, 0.1 us)
Async XLA Ops:
  2.1 12.1 %collective-permute-start = (f32[2,128,256]{2,1,0:T(8,128)}, f32[2,128,256]{2,1,0:T(8,128)S(1)}, u32[]{:S(2)}, u32[]{:S(2)}) collective-permute-start(f32[2,128,256]{2,1,0:T(8,128)} %get-tuple-element.19), channel_id=1, source_target_pairs={{2,0},{4,2},{6,4},{3,1},{5,3},{7,5},{10,8},{12,10},{14,12},{11,9},... | collective-permute-start | bytes 786440 | tf_op jit(solution)/shard_map/ppermute | solution.py:625
  4.5 10.2 %collective-permute-start.1 = (f32[2,256,128]{2,1,0:T(8,128)}, f32[2,256,128]{2,1,0:T(8,128)S(1)}, u32[]{:S(2)}, u32[]{:S(2)}) collective-permute-start(f32[2,256,128]{2,1,0:T(8,128)} %get-tuple-element.20), channel_id=1, source_target_pairs={{1,0},{3,2},{5,4},{7,6},{9,8},{11,10},{13,12},{15,14},{17,16},{19,... | collective-permute-start | bytes 786440 | tf_op jit(solution)/shard_map/ppermute | solution.py:625
  6.5 7.6 %collective-permute-start.2 = (f32[2,128,128]{2,1,0:T(8,128)}, f32[2,128,128]{2,1,0:T(8,128)S(1)}, u32[]{:S(2)}, u32[]{:S(2)}) collective-permute-start(f32[2,128,128]{2,1,0:T(8,128)} %get-tuple-element.21), channel_id=1, source_target_pairs={{3,0},{5,2},{7,4},{11,8},{13,10},{15,12},{19,16},{21,18},{23,20},{... | collective-permute-start | bytes 393224 | tf_op jit(solution)/shard_map/ppermute | solution.py:636
  14.1 2.7 %copy-start.6 = (f32[2,128,128]{2,1,0:T(8,128)}, f32[2,128,128]{2,1,0:T(8,128)S(1)}, u32[]{:S(2)}) copy-start(f32[2,128,128]{2,1,0:T(8,128)S(1)} %collective-permute-done.2.diag_ref) | copy-start | bytes 393220
  14.1 2.7 %copy-start.2 = (f32[2,128,256]{2,1,0:T(8,128)}, f32[2,128,256]{2,1,0:T(8,128)S(1)}, u32[]{:S(2)}) copy-start(f32[2,128,256]{2,1,0:T(8,128)S(1)} %collective-permute-done.below_ref) | copy-start | bytes 786436
  14.7 2.1 %copy-start.3 = (f32[2,256,128]{2,1,0:T(8,128)}, f32[2,256,128]{2,1,0:T(8,128)S(1)}, u32[]{:S(2)}) copy-start(f32[2,256,128]{2,1,0:T(8,128)S(1)} %collective-permute-done.1.right_ref) | copy-start | bytes 786436
  14.7 2.1 %collective-permute-start.3 = (f32[2,128,256]{2,1,0:T(8,128)S(1)}, f32[2,128,256]{2,1,0:T(8,128)S(1)}, u32[]{:S(2)}, u32[]{:S(2)}) collective-permute-start(f32[2,128,256]{2,1,0:T(8,128)S(1)} %collective-permute-done.below_ref), channel_id=1, source_target_pairs={{0,8},{8,0},{16,24},{24,16},{32,40},{40,32},{48,56},{56,48},{64,72... | collective-permute-start | bytes 786440 | tf_op jit(solution)/shard_map/ppermute | solution.py:644
  14.7 2.1 %collective-permute-start.4 = (f32[2,256,128]{2,1,0:T(8,128)S(1)}, f32[2,256,128]{2,1,0:T(8,128)S(1)}, u32[]{:S(2)}, u32[]{:S(2)}) collective-permute-start(f32[2,256,128]{2,1,0:T(8,128)S(1)} %collective-permute-done.1.right_ref), channel_id=1, source_target_pairs={{0,8},{8,0},{16,24},{24,16},{32,40},{40,32},{48,56},{56,48},{64,72... | collective-permute-start | bytes 786440 | tf_op jit(solution)/shard_map/ppermute | solution.py:644
  15.2 1.6 %collective-permute-start.5 = (f32[2,128,128]{2,1,0:T(8,128)S(1)}, f32[2,128,128]{2,1,0:T(8,128)S(1)}, u32[]{:S(2)}, u32[]{:S(2)}) collective-permute-start(f32[2,128,128]{2,1,0:T(8,128)S(1)} %collective-permute-done.2.diag_ref), channel_id=1, source_target_pairs={{0,8},{8,0},{16,24},{24,16},{32,40},{40,32},{48,56},{56,48},{64,72... | collective-permute-start | bytes 393224 | tf_op jit(solution)/shard_map/ppermute | solution.py:644
  16.8 0.6 copy-start.7
  16.8 0.7 copy-start.4
  16.8 0.9 copy-start.5
  40.7 29.6 %copy-start.1 = (f32[512,256]{1,0:T(8,128)S(1)}, f32[512,256]{1,0:T(8,128)}, u32[]{:S(2)}) copy-start(f32[512,256]{1,0:T(8,128)} %get-tuple-element.28.light_ref) | copy-start | bytes 1572868
  70.3 13.7 %copy-start = (f32[2,2,256,256]{3,2,1,0:T(8,128)S(1)}, f32[2,2,256,256]{3,2,1,0:T(8,128)}, u32[]{:S(2)}) copy-start(f32[2,2,256,256]{3,2,1,0:T(8,128)} %object_ref.3) | copy-start | bytes 3145732
  72.6 11.3 %collective-permute-start.6 = (f32[6,2,8,128]{3,2,1,0:T(8,128)S(1)}, f32[6,2,8,128]{3,2,1,0:T(8,128)S(1)}, u32[]{:S(2)}, u32[]{:S(2)}) collective-permute-start(f32[6,2,8,128]{3,2,1,0:T(8,128)S(1)} %get-tuple-element.30), channel_id=1, source_target_pairs={{0,1},{2,3},{4,5},{6,7},{8,9},{10,11},{12,13},{14,15},{16,17},{18,... | collective-permute-start | bytes 147464 | tf_op jit(solution)/shard_map/ppermute | solution.py:625
  73.9 10.0 %collective-permute-start.7 = (f32[6,8,256]{2,1,0:T(8,128)S(1)}, f32[6,8,256]{2,1,0:T(8,128)S(1)}, u32[]{:S(2)}, u32[]{:S(2)}) collective-permute-start(f32[6,8,256]{2,1,0:T(8,128)S(1)} %get-tuple-element.31), channel_id=1, source_target_pairs={{0,2},{2,4},{4,6},{1,3},{3,5},{5,7},{8,10},{10,12},{12,14},{9,11},... | collective-permute-start | bytes 147464 | tf_op jit(solution)/shard_map/ppermute | solution.py:625
  77.3 6.6 %collective-permute-start.8 = (f32[6,8,128]{2,1,0:T(8,128)S(1)}, f32[6,8,128]{2,1,0:T(8,128)S(1)}, u32[]{:S(2)}, u32[]{:S(2)}) collective-permute-start(f32[6,8,128]{2,1,0:T(8,128)S(1)} %get-tuple-element.32), channel_id=1, source_target_pairs={{0,3},{2,5},{4,7},{8,11},{10,13},{12,15},{16,19},{18,21},{20,23},{... | collective-permute-start | bytes 73736 | tf_op jit(solution)/shard_map/ppermute | solution.py:636
  84.0 5.8 %collective-permute-start.9 = (f32[1,2,2,2,8,256]{5,4,3,2,1,0:T(8,128)S(1)}, f32[1,2,2,2,8,256]{5,4,3,2,1,0:T(8,128)S(1)}, u32[]{:S(2)}, u32[]{:S(2)}) collective-permute-start(f32[1,2,2,2,8,256]{5,4,3,2,1,0:T(8,128)S(1)} %bitcast.5), channel_id=1, source_target_pairs={{0,16},{8,24},{16,0},{24,8},{32,48},{40,56},{48,32},{56,40},{64,80... | collective-permute-start | bytes 196616 | tf_op jit(solution)/shard_map/ppermute | solution.py:644
  89.8 7.3 %collective-permute-start.10 = (f32[2,2,2,2,8,256]{5,4,3,2,1,0:T(8,128)S(1)}, f32[2,2,2,2,8,256]{5,4,3,2,1,0:T(8,128)S(1)}, u32[]{:S(2)}, u32[]{:S(2)}) collective-permute-start(f32[2,2,2,2,8,256]{5,4,3,2,1,0:T(8,128)S(1)} %pad_maximum_fusion), channel_id=1, source_target_pairs={{0,32},{8,40},{16,48},{24,56},{32,64},{40,72},{48,80},{56,88},{64,... | collective-permute-start | bytes 393224 | tf_op jit(solution)/shard_map/ppermute | solution.py:644
  89.9 9.7 %collective-permute-start.12 = (f32[2,2,2,2,8,256]{5,4,3,2,1,0:T(8,128)S(1)}, f32[2,2,2,2,8,256]{5,4,3,2,1,0:T(8,128)S(1)}, u32[]{:S(2)}, u32[]{:S(2)}) collective-permute-start(f32[2,2,2,2,8,256]{5,4,3,2,1,0:T(8,128)S(1)} %pad_maximum_fusion), channel_id=1, source_target_pairs={{0,96},{8,104},{16,112},{24,120},{32,0},{40,8},{48,16},{56,24},{64... | collective-permute-start | bytes 393224 | tf_op jit(solution)/shard_map/ppermute | solution.py:644
  93.2 6.5 %collective-permute-start.11 = (f32[2,2,2,2,8,256]{5,4,3,2,1,0:T(8,128)S(1)}, f32[2,2,2,2,8,256]{5,4,3,2,1,0:T(8,128)S(1)}, u32[]{:S(2)}, u32[]{:S(2)}) collective-permute-start(f32[2,2,2,2,8,256]{5,4,3,2,1,0:T(8,128)S(1)} %pad_maximum_fusion), channel_id=1, source_target_pairs={{0,64},{8,72},{16,80},{24,88},{32,96},{40,104},{48,112},{56,120},{... | collective-permute-start | bytes 393224 | tf_op jit(solution)/shard_map/ppermute | solution.py:644
  99.7 2.0 %collective-permute-start.13 = (f32[8,2,2,2,8,256]{5,4,3,2,1,0:T(8,128)S(1)}, f32[8,2,2,2,8,256]{5,4,3,2,1,0:T(8,128)S(1)}, u32[]{:S(2)}, u32[]{:S(2)}) collective-permute-start(f32[8,2,2,2,8,256]{5,4,3,2,1,0:T(8,128)S(1)} %constant_dynamic-update-slice_fusion.refs_0_), channel_id=1, source_target_pairs={{0,8},{8,0},{16,24},{24,16},{32,40},{40,32},{48,56},{56,48},{64,72... | collective-permute-start | bytes 1572872 | tf_op jit(solution)/shard_map/ppermute | solution.py:644

commit v4 on v3

--- a/solution.py
+++ b/solution.py
@@ -109,27 +109,17 @@
     ]
 
 
-def probe_copies(probe_ref, probe, sems, m):
-    return [
-        pltpu.make_async_copy(
-            probe_ref.at[p, m, :, pl.ds(h * HALF, HALF)], probe.at[p, m, h], sems.at[p, m, h]
-        )
-        for p in range(2)
-        for h in range(2)
-    ]
-
-
 def wave_kernel(
     corner_ref,
     me_ref,
-    below_ref,
-    right_ref,
-    diag_ref,
-    other_below_ref,
-    other_right_ref,
-    other_diag_ref,
+    below_far,
+    right_far,
+    diag_far,
+    other_below_far,
+    other_right_far,
+    other_diag_far,
     own_far,
-    probe_ref,
+    probe,
     measured_far,
     col_far,
     row_far,
@@ -144,8 +134,6 @@
     far,
     misfit,
     total,
-    probe,
-    sems,
     more_sems,
     field,
     turned,
@@ -153,10 +141,14 @@
     across_1,
     along_0,
     along_1,
+    below_ref,
+    right_ref,
+    diag_ref,
+    rim_sems,
 ):
     across, along = (across_0, across_1), (along_0, along_1)
     r, c = corner_ref[0], corner_ref[1]
-    modes = probe_ref.shape[1]
+    modes = probe.shape[1]
     own_copy = pltpu.make_async_copy(own_far, own_ref, more_sems.at[0])
     later = [
         pltpu.make_async_copy(source, target, more_sems.at[n + 1])
@@ -168,26 +160,32 @@
             ]
         )
     ]
+    core = lax.rem(me_ref[0], 2)
+    rim_copies = [
+        pltpu.make_async_copy(
+            source, target.at[lax.rem(core + side, 2)], rim_sems.at[side, n]
+        )
+        for side, sources in enumerate(
+            [(below_far, right_far, diag_far), (other_below_far, other_right_far, other_diag_far)]
+        )
+        for n, (source, target) in enumerate(zip(sources, (below_ref, right_ref, diag_ref)))
+    ]
     own_copy.start()
-    for copy in probe_copies(probe_ref, probe, sems, 0):
+    for copy in rim_copies:
         copy.start()
     for copy in later:
         copy.start()
-    for m in range(1, modes):
-        for copy in probe_copies(probe_ref, probe, sems, m):
-            copy.start()
     rows = lax.broadcasted_iota(jnp.int32, (SIDE, SIDE), 0)
     cols = lax.broadcasted_iota(jnp.int32, (SIDE, SIDE), 1)
     top = rows[:HALF] < r
     near = cols[:, :HALF] < c
     back_c = lax.rem(SIDE - c, SIDE)
     own_copy.wait()
+    for copy in rim_copies:
+        copy.wait()
     for s in range(LAYERS):
         for p in range(2):
-            held = lax.rem(me_ref[0], 2) == p
-            right = jnp.where(held, right_ref[s], other_right_ref[s])
-            below = jnp.where(held, below_ref[s], other_below_ref[s])
-            diag = jnp.where(held, diag_ref[s], other_diag_ref[s])
+            right, below, diag = right_ref[p, s], below_ref[p, s], diag_ref[p, s]
             left = jnp.where(near, right, own_ref[s, p, :, :HALF])
             whole = jnp.concatenate([left, own_ref[s, p, :, HALF:]], axis=1)
             lower = jnp.concatenate(
@@ -273,9 +271,6 @@
         while live:
             live = [part for part in live if next(part, live) is not live]
 
-    for m in range(modes):
-        for copy in probe_copies(probe_ref, probe, sems, m):
-            copy.wait()
     beside(enter(0, 0))
     for copy in later:
         copy.wait()
@@ -368,7 +363,7 @@
         out_ref[i, 10] = mark
 
 
-def glow_kernel(probe_ref, measured_ref, light_ref, expected_ref):
+def glow_kernel(probe_ref, measured_ref, light_ref, expected_ref, halves_ref):
     @pl.when(pl.program_id(0) == 0)
     def _():
         light_ref[...] = jnp.zeros_like(light_ref)
@@ -387,6 +382,9 @@
                 value = mul(high, by_col) + mul(low, by_col) + mul(rest, by_col)
         expected_ref[...] = value
 
+    for p in range(2):
+        for h in range(2):
+            halves_ref[p, 0, h] = probe_ref[p, 0, :, h * HALF : (h + 1) * HALF]
     light = probe_ref[0, 0] * probe_ref[0, 0] + probe_ref[1, 0] * probe_ref[1, 0]
     light_ref[:SIDE] += light
     light_ref[SIDE:] += light
@@ -400,6 +398,7 @@
         out_shape=(
             jax.ShapeDtypeStruct((2 * SIDE, SIDE), f32),
             jax.ShapeDtypeStruct((SIDE, SIDE), f32),
+            jax.ShapeDtypeStruct((2, modes, 2, SIDE, HALF), f32),
         ),
         in_specs=[
             pl.BlockSpec((2, 1, SIDE, SIDE), lambda m: (0, m, 0, 0)),
@@ -408,8 +407,9 @@
         out_specs=(
             pl.BlockSpec((2 * SIDE, SIDE), lambda m: (0, 0)),
             pl.BlockSpec((SIDE, SIDE), lambda m: (0, 0)),
+            pl.BlockSpec((2, 1, 2, SIDE, HALF), lambda m: (0, m, 0, 0, 0)),
         ),
-        compiler_params=pltpu.CompilerParams(vmem_limit_bytes=60 * 1024 * 1024),
+        compiler_params=pltpu.CompilerParams(vmem_limit_bytes=10 * 1024 * 1024),
         cost_estimate=pl.CostEstimate(
             flops=4 * modes * SIDE * SIDE, bytes_accessed=8 * modes * SIDE * SIDE, transcendentals=0
         ),
@@ -438,7 +438,7 @@
 
 
 def run_cut(me, current):
-    vmem = pl.BlockSpec(memory_space=pltpu.VMEM)
+    far = pl.BlockSpec(memory_space=pl.ANY)
     return pl.pallas_call(
         cut_kernel,
         out_shape=(
@@ -446,10 +446,10 @@
             jax.ShapeDtypeStruct((LAYERS, SIDE, HALF), f32),
             jax.ShapeDtypeStruct((LAYERS, HALF, HALF), f32),
         ),
-        in_specs=[pl.BlockSpec(memory_space=pltpu.SMEM), pl.BlockSpec(memory_space=pl.ANY)],
-        out_specs=(vmem,) * 3,
+        in_specs=[pl.BlockSpec(memory_space=pltpu.SMEM), far],
+        out_specs=(pl.BlockSpec(memory_space=pltpu.VMEM),) * 3,
         scratch_shapes=[pltpu.SemaphoreType.DMA((LAYERS, 3))],
-        compiler_params=pltpu.CompilerParams(vmem_limit_bytes=60 * 1024 * 1024),
+        compiler_params=pltpu.CompilerParams(vmem_limit_bytes=4 * 1024 * 1024),
         name="cut",
     )(me, current)
 
@@ -464,8 +464,9 @@
         wave_kernel,
         out_shape=jax.ShapeDtypeStruct((SCANS, 11, 8, SIDE), f32),
         in_specs=[pl.BlockSpec(memory_space=pltpu.SMEM)] * 2
-        + [vmem] * 6
-        + [pl.BlockSpec(memory_space=pl.ANY)] * 5,
+        + [pl.BlockSpec(memory_space=pl.ANY)] * 7
+        + [vmem]
+        + [pl.BlockSpec(memory_space=pl.ANY)] * 3,
         out_specs=vmem,
         scratch_shapes=[
             pltpu.VMEM((LAYERS, 2, SIDE, SIDE), f32),
@@ -478,8 +479,6 @@
             pltpu.VMEM((modes + 1, 2, SIDE, SIDE), f32),
             pltpu.VMEM((SIDE, SIDE), f32),
             pltpu.VMEM((5,) + field, f32),
-            pltpu.VMEM((2, modes, 2, SIDE, HALF), f32),
-            pltpu.SemaphoreType.DMA((2, modes, 2)),
             pltpu.SemaphoreType.DMA((4,)),
             pltpu.VMEM((2,) + wide, f32),
             pltpu.VMEM(wide, f32),
@@ -487,8 +486,12 @@
             pltpu.VMEM((2, 2, SIDE, SIDE), bf16),
             pltpu.VMEM((2, 2, SIDE, SIDE), bf16),
             pltpu.VMEM((2, 2, SIDE, SIDE), bf16),
+            pltpu.VMEM((2, LAYERS, HALF, SIDE), f32),
+            pltpu.VMEM((2, LAYERS, SIDE, HALF), f32),
+            pltpu.VMEM((2, LAYERS, HALF, HALF), f32),
+            pltpu.SemaphoreType.DMA((2, 3)),
         ],
-        compiler_params=pltpu.CompilerParams(vmem_limit_bytes=60 * 1024 * 1024),
+        compiler_params=pltpu.CompilerParams(vmem_limit_bytes=36 * 1024 * 1024),
         name="wave",
     )(
         corner,
@@ -649,8 +652,8 @@
     corner = corners.reshape(2)
     rims = run_cut(me, object_slices)
     rims = (shift(rims[0], "tx", -1), shift(rims[1], "ty", -1), shift_both(rims[2], -1))
-    light, expected = run_glow(probe_modes, measured.reshape(SIDE, SIDE))
-    rims, light, expected = lax.optimization_barrier((rims, light, expected))
+    light, expected, halves = run_glow(probe_modes, measured.reshape(SIDE, SIDE))
+    rims, light, expected, halves = lax.optimization_barrier((rims, light, expected, halves))
     others = tuple(along_scan(rim, 0, 0, 1) for rim in rims)
 
     parts = run_wave(
@@ -658,7 +661,7 @@
         me,
         object_slices,
         rims + others,
-        probe_modes,
+        halves,
         expected,
     )
     parts = lax.all_to_all(parts, "scan", 0, 0)

time: 104 us -> 98.2 us (0.944)
  Pallas kernels: 34.8 us -> 25.3 us
  local copies, waits for them, and re-layouts: 0.88 us -> 4.42 us
    pallas_call x1, Pallas kernels: 6.34 us -> 2.17 us  [run_glow(): pl.pallas_call(glow_kernel, grid=(modes,), out_shape=(jax.ShapeDtypeStruc...]
    pallas_call x1, Pallas kernels: 23 us -> 19.3 us  [run_wave(): pl.pallas_call(wave_kernel, out_shape=jax.ShapeDtypeStruct((SCANS, 11, 8,...]
    unnamed x20 -> x18, local copies, waits for them, and re-layouts: 0.87 us -> 4.4 us
    pallas_call x1, Pallas kernels: 2.07 us -> 0.4 us  [run_cut(): pl.pallas_call(cut_kernel, out_shape=(jax.ShapeDtypeStruct((LAYERS, HALF,...]
  transfers between devices with their start and end apart: 14 -> 14, of which waited for: 7 -> 7; matrix products, arithmetic and copies ran while one was open for 0% -> 0% of each run, Pallas kernels for 6% -> 2%
where the time goes in v4:
time: 98.2 us; the launch traced here: 97.1 us
  blocking collectives  29.2 us (30%)
  Pallas kernels  25.3 us (26%)
  waiting for transfers between devices  21.7 us (22%)
  starting transfers between devices  16.3 us (17%)
  local copies, waits for them, and re-layouts  4.42 us (5%)
    all_to_all x1, blocking collectives, on_device(): parts = lax.all_to_all(parts, 'scan', 0, 0)  29.2 us
    pallas_call x1, Pallas kernels, run_wave(): pl.pallas_call(wave_kernel, out_shape=jax.ShapeDtypeStruct((SCANS, 11, 8,...  19.3 us
    ppermute x8, waiting for transfers between devices, along_scan(): return lax.ppermute(array, 'scan', pairs)  15.1 us
    ppermute x4, starting transfers between devices, shift(): return lax.ppermute(array, axis, pairs)  9.1 us
    ppermute x2, waiting for transfers between devices, shift_both(): return lax.ppermute(array, ('tx', 'ty'), pairs)  5.32 us
    ppermute x8, starting transfers between devices, along_scan(): return lax.ppermute(array, 'scan', pairs)  4.59 us
    unnamed x18, local copies, waits for them, and re-layouts  4.4 us
    ppermute x2, starting transfers between devices, shift_both(): return lax.ppermute(array, ('tx', 'ty'), pairs)  2.59 us
  transfers between devices with their start and end apart: 14, of which 7 were waited for; matrix products, arithmetic and copies ran while one was open for 0% of the time, Pallas kernels for 2%

profile of v4, /device:TPU:34, one launch (start us, length us, event | category | flops | bytes accessed | tf_op | source)
XLA Modules:
  0.0 97.1 jit_solution(9640399999567290053)
XLA Ops:
  0.0 0.0 copy-start
  0.0 1.2 %copy-done = f32[2,2,256,256]{3,2,1,0:T(8,128)S(1)} copy-done((f32[2,2,256,256]{3,2,1,0:T(8,128)S(1)}, f32[2,2,256,256]{3,2,1,0:T(8,128)}, u32[]{:S(2)}) %copy-start) | copy-done | bytes 1048600
  1.2 0.4 cut.1
  1.6 2.4 %collective-permute-start = (f32[2,128,256]{2,1,0:T(8,128)S(1)}, f32[2,128,256]{2,1,0:T(8,128)S(1)}, u32[]{:S(2)}, u32[]{:S(2)}) collective-permute-start(f32[2,128,256]{2,1,0:T(8,128)S(1)} %get-tuple-element.21), channel_id=1, source_target_pairs={{2,0},{4,2},{6,4},{3,1},{5,3},{7,5},{10,8},{12,10},{14,12},{11,9},... | collective-permute-start | bytes 786440 | tf_op jit(solution)/shard_map/ppermute | solution.py:628
  4.1 1.9 %collective-permute-start.1 = (f32[2,256,128]{2,1,0:T(8,128)S(1)}, f32[2,256,128]{2,1,0:T(8,128)S(1)}, u32[]{:S(2)}, u32[]{:S(2)}) collective-permute-start(f32[2,256,128]{2,1,0:T(8,128)S(1)} %get-tuple-element.22), channel_id=1, source_target_pairs={{1,0},{3,2},{5,4},{7,6},{9,8},{11,10},{13,12},{15,14},{17,16},{19,... | collective-permute-start | bytes 786440 | tf_op jit(solution)/shard_map/ppermute | solution.py:628
  6.0 1.3 %collective-permute-start.2 = (f32[2,128,128]{2,1,0:T(8,128)S(1)}, f32[2,128,128]{2,1,0:T(8,128)S(1)}, u32[]{:S(2)}, u32[]{:S(2)}) collective-permute-start(f32[2,128,128]{2,1,0:T(8,128)S(1)} %get-tuple-element.23), channel_id=1, source_target_pairs={{3,0},{5,2},{7,4},{11,8},{13,10},{15,12},{19,16},{21,18},{23,20},{... | collective-permute-start | bytes 393224 | tf_op jit(solution)/shard_map/ppermute | solution.py:639
  7.3 0.0 copy-start.2
  7.4 2.2 %copy-done.2 = f32[2,8,256,256]{3,2,1,0:T(8,128)S(1)} copy-done((f32[2,8,256,256]{3,2,1,0:T(8,128)S(1)}, f32[2,8,256,256]{3,2,1,0:T(8,128)}, u32[]{:S(2)}) %copy-start.2) | copy-done | bytes 4194328
  9.5 0.0 copy-start.5
  9.5 0.9 copy-done.5
  10.5 0.0 copy-start.1
  10.5 0.0 copy-start.3
  10.5 0.0 copy-start.4
  10.5 0.0 copy-start.6
  10.5 2.2 %glow.1 = (f32[512,256]{1,0:T(8,128)S(1)}, f32[256,256]{1,0:T(8,128)S(1)}, f32[2,8,2,256,128]{4,3,2,1,0:T(8,128)S(1)}) custom-call(f32[2,8,256,256]{3,2,1,0:T(8,128)S(1)} %copy-done.2, f32[256,256]{1,0:T(8,128)S(1)} %bitcast.7), custom_call_target="tpu_custom_call" | custom-call | flops 2097152 | bytes 4194304 | tf_op jit(solution)/shard_map/glow/pallas_call | solution.py:395
  12.7 0.0 collective-permute-done.2.diag_far
  12.7 0.0 collective-permute-done.below_far
  12.7 1.2 %collective-permute-done.1.right_far = f32[2,256,128]{2,1,0:T(8,128)S(1)} collective-permute-done((f32[2,256,128]{2,1,0:T(8,128)S(1)}, f32[2,256,128]{2,1,0:T(8,128)S(1)}, u32[]{:S(2)}, u32[]{:S(2)}) %collective-permute-start.1) | collective-permute-done | bytes 262176 | tf_op jit(solution)/shard_map/ppermute | solution.py:628
  14.0 0.0 collective-permute-start.3
  14.0 0.5 collective-permute-start.4
  14.5 0.0 collective-permute-start.5
  14.5 1.6 %collective-permute-done.5.other_diag_far = f32[2,128,128]{2,1,0:T(8,128)S(1)} collective-permute-done((f32[2,128,128]{2,1,0:T(8,128)S(1)}, f32[2,128,128]{2,1,0:T(8,128)S(1)}, u32[]{:S(2)}, u32[]{:S(2)}) %collective-permute-start.5) | collective-permute-done | bytes 131104 | tf_op jit(solution)/shard_map/ppermute | solution.py:647
  16.1 0.0 collective-permute-done.3.other_below_far
  16.1 0.0 collective-permute-done.4.other_right_far
  16.1 0.0 copy-done.1
  16.1 0.0 copy-done.3
  16.1 0.0 copy-done.4
  16.1 0.0 copy-done.6
  16.1 19.3 %wave.1 = f32[16,11,8,256]{3,2,1,0:T(8,128)S(1)} custom-call(s32[2]{0:T(128)S(1)} %bitcast.8, s32[1]{0:T(128)} %bitcast.me_ref, f32[2,128,256]{2,1,0:T(8,128)S(1)} %collective-permute-done.below_far, f32[2,256,128]{2,1,0:T(8,128)S(1)} %collective-permute-done.1.right_far, f32[2,128,128]{2,1,0:T(8,128)S(1)} %collective-permute-done.2.diag_far, ...), custom_call_target="tpu_custom_call" | custom-call | tf_op jit(solution)/shard_map/wave/pallas_call | solution.py:463
  35.5 29.2 %all_to_all.5.parts_ref = f32[16,11,8,256]{3,2,1,0:T(8,128)S(1)} all-to-all(f32[16,11,8,256]{3,2,1,0:T(8,128)S(1)} %wave.1), channel_id=1, replica_groups=mesh['scan'=16,'tx'=4,'ty'=2] {'scan'}, dimensions={0} | all-to-all | bytes 2883584 | tf_op jit(solution)/shard_map/all_to_all | solution.py:667
  64.7 2.3 %sum.1 = (f32[6,2,8,256]{3,2,1,0:T(8,128)S(1)}, f32[6,2,8,128]{3,2,1,0:T(8,128)S(1)}, f32[6,8,256]{2,1,0:T(8,128)S(1)}, f32[6,8,128]{2,1,0:T(8,128)S(1)}) custom-call(s32[1]{0:T(128)} %bitcast.me_ref, f32[16,11,8,256]{3,2,1,0:T(8,128)S(1)} %all_to_all.5.parts_ref, f32[512,256]{1,0:T(8,128)S(1)} %get-tuple-element.32.light_ref), custom_call_target="tpu_custom_call" | custom-call | tf_op jit(solution)/shard_map/sum/pallas_call | solution.py:548
  67.0 1.3 %collective-permute-start.6 = (f32[6,2,8,128]{3,2,1,0:T(8,128)S(1)}, f32[6,2,8,128]{3,2,1,0:T(8,128)S(1)}, u32[]{:S(2)}, u32[]{:S(2)}) collective-permute-start(f32[6,2,8,128]{3,2,1,0:T(8,128)S(1)} %get-tuple-element.34), channel_id=1, source_target_pairs={{0,1},{2,3},{4,5},{6,7},{8,9},{10,11},{12,13},{14,15},{16,17},{18,... | collective-permute-start | bytes 147464 | tf_op jit(solution)/shard_map/ppermute | solution.py:628
  68.3 3.4 %collective-permute-start.7 = (f32[6,8,256]{2,1,0:T(8,128)S(1)}, f32[6,8,256]{2,1,0:T(8,128)S(1)}, u32[]{:S(2)}, u32[]{:S(2)}) collective-permute-start(f32[6,8,256]{2,1,0:T(8,128)S(1)} %get-tuple-element.35), channel_id=1, source_target_pairs={{0,2},{2,4},{4,6},{1,3},{3,5},{5,7},{8,10},{10,12},{12,14},{9,11},... | collective-permute-start | bytes 147464 | tf_op jit(solution)/shard_map/ppermute | solution.py:628
  71.7 1.3 %collective-permute-start.8 = (f32[6,8,128]{2,1,0:T(8,128)S(1)}, f32[6,8,128]{2,1,0:T(8,128)S(1)}, u32[]{:S(2)}, u32[]{:S(2)}) collective-permute-start(f32[6,8,128]{2,1,0:T(8,128)S(1)} %get-tuple-element.36), channel_id=1, source_target_pairs={{0,3},{2,5},{4,7},{8,11},{10,13},{12,15},{16,19},{18,21},{20,23},{... | collective-permute-start | bytes 73736 | tf_op jit(solution)/shard_map/ppermute | solution.py:639
  73.0 5.3 %collective-permute-done.8.diag_ref = f32[6,8,128]{2,1,0:T(8,128)S(1)} collective-permute-done((f32[6,8,128]{2,1,0:T(8,128)S(1)}, f32[6,8,128]{2,1,0:T(8,128)S(1)}, u32[]{:S(2)}, u32[]{:S(2)}) %collective-permute-start.8) | collective-permute-done | bytes 24608 | tf_op jit(solution)/shard_map/ppermute | solution.py:639
  78.4 0.0 collective-permute-done.6.right_ref
  78.4 0.0 collective-permute-done.7.below_ref
  78.4 0.7 collective-permute-start.9
  79.1 5.1 %collective-permute-done.9 = f32[1,2,2,2,8,256]{5,4,3,2,1,0:T(8,128)S(1)} collective-permute-done((f32[1,2,2,2,8,256]{5,4,3,2,1,0:T(8,128)S(1)}, f32[1,2,2,2,8,256]{5,4,3,2,1,0:T(8,128)S(1)}, u32[]{:S(2)}, u32[]{:S(2)}) %collective-permute-start.9) | collective-permute-done | bytes 65568 | tf_op jit(solution)/shard_map/ppermute | solution.py:647
  84.3 0.1 collective-permute-start.10
  84.4 3.2 %collective-permute-start.12 = (f32[2,2,2,2,8,256]{5,4,3,2,1,0:T(8,128)S(1)}, f32[2,2,2,2,8,256]{5,4,3,2,1,0:T(8,128)S(1)}, u32[]{:S(2)}, u32[]{:S(2)}) collective-permute-start(f32[2,2,2,2,8,256]{5,4,3,2,1,0:T(8,128)S(1)} %pad_maximum_fusion), channel_id=1, source_target_pairs={{0,96},{8,104},{16,112},{24,120},{32,0},{40,8},{48,16},{56,24},{64... | collective-permute-start | bytes 393224 | tf_op jit(solution)/shard_map/ppermute | solution.py:647
  87.6 0.0 collective-permute-start.11
  87.6 4.0 %collective-permute-done.10 = f32[2,2,2,2,8,256]{5,4,3,2,1,0:T(8,128)S(1)} collective-permute-done((f32[2,2,2,2,8,256]{5,4,3,2,1,0:T(8,128)S(1)}, f32[2,2,2,2,8,256]{5,4,3,2,1,0:T(8,128)S(1)}, u32[]{:S(2)}, u32[]{:S(2)}) %collective-permute-start.10) | collective-permute-done | bytes 131104 | tf_op jit(solution)/shard_map/ppermute | solution.py:647
  91.6 2.4 %collective-permute-done.11 = f32[2,2,2,2,8,256]{5,4,3,2,1,0:T(8,128)S(1)} collective-permute-done((f32[2,2,2,2,8,256]{5,4,3,2,1,0:T(8,128)S(1)}, f32[2,2,2,2,8,256]{5,4,3,2,1,0:T(8,128)S(1)}, u32[]{:S(2)}, u32[]{:S(2)}) %collective-permute-start.11) | collective-permute-done | bytes 131104 | tf_op jit(solution)/shard_map/ppermute | solution.py:647
  94.1 0.0 collective-permute-done.12
  94.1 0.1 collective-permute-start.13
  94.2 1.9 %collective-permute-done.13.refs_1_ = f32[8,2,2,2,8,256]{5,4,3,2,1,0:T(8,128)S(1)} collective-permute-done((f32[8,2,2,2,8,256]{5,4,3,2,1,0:T(8,128)S(1)}, f32[8,2,2,2,8,256]{5,4,3,2,1,0:T(8,128)S(1)}, u32[]{:S(2)}, u32[]{:S(2)}) %collective-permute-start.13) | collective-permute-done | bytes 524320 | tf_op jit(solution)/shard_map/ppermute | solution.py:647
  96.1 1.1 %place.1 = f32[2,2,256,256]{3,2,1,0:T(8,128)} custom-call(s32[1]{0:T(128)} %bitcast.me_ref, f32[8,2,2,2,8,256]{5,4,3,2,1,0:T(8,128)S(1)} %constant_dynamic-update-slice_fusion.refs_0_, f32[8,2,2,2,8,256]{5,4,3,2,1,0:T(8,128)S(1)} %collective-permute-done.13.refs_1_), custom_call_target="tpu_custom_call" | custom-call | tf_op jit(solution)/shard_map/place/pallas_call | solution.py:615
  (7 shorter events, 0.1 us)
Async XLA Ops:
  0.0 1.2 %copy-start = (f32[2,2,256,256]{3,2,1,0:T(8,128)S(1)}, f32[2,2,256,256]{3,2,1,0:T(8,128)}, u32[]{:S(2)}) copy-start(f32[2,2,256,256]{3,2,1,0:T(8,128)} %object_ref.3) | copy-start | bytes 3145732
  1.6 11.1 %collective-permute-start = (f32[2,128,256]{2,1,0:T(8,128)S(1)}, f32[2,128,256]{2,1,0:T(8,128)S(1)}, u32[]{:S(2)}, u32[]{:S(2)}) collective-permute-start(f32[2,128,256]{2,1,0:T(8,128)S(1)} %get-tuple-element.21), channel_id=1, source_target_pairs={{2,0},{4,2},{6,4},{3,1},{5,3},{7,5},{10,8},{12,10},{14,12},{11,9},... | collective-permute-start | bytes 786440 | tf_op jit(solution)/shard_map/ppermute | solution.py:628
  4.1 9.9 %collective-permute-start.1 = (f32[2,256,128]{2,1,0:T(8,128)S(1)}, f32[2,256,128]{2,1,0:T(8,128)S(1)}, u32[]{:S(2)}, u32[]{:S(2)}) collective-permute-start(f32[2,256,128]{2,1,0:T(8,128)S(1)} %get-tuple-element.22), channel_id=1, source_target_pairs={{1,0},{3,2},{5,4},{7,6},{9,8},{11,10},{13,12},{15,14},{17,16},{19,... | collective-permute-start | bytes 786440 | tf_op jit(solution)/shard_map/ppermute | solution.py:628
  6.0 6.6 %collective-permute-start.2 = (f32[2,128,128]{2,1,0:T(8,128)S(1)}, f32[2,128,128]{2,1,0:T(8,128)S(1)}, u32[]{:S(2)}, u32[]{:S(2)}) collective-permute-start(f32[2,128,128]{2,1,0:T(8,128)S(1)} %get-tuple-element.23), channel_id=1, source_target_pairs={{3,0},{5,2},{7,4},{11,8},{13,10},{15,12},{19,16},{21,18},{23,20},{... | collective-permute-start | bytes 393224 | tf_op jit(solution)/shard_map/ppermute | solution.py:639
  7.3 2.2 %copy-start.2 = (f32[2,8,256,256]{3,2,1,0:T(8,128)S(1)}, f32[2,8,256,256]{3,2,1,0:T(8,128)}, u32[]{:S(2)}) copy-start(f32[2,8,256,256]{3,2,1,0:T(8,128)} %probe_ref.1) | copy-start | bytes 12582916
  9.5 0.9 copy-start.5
  10.5 5.6 %copy-start.1 = (f32[2,2,256,256]{3,2,1,0:T(8,128)S(1)}, f32[2,2,256,256]{3,2,1,0:T(8,128)}, u32[]{:S(2)}) copy-start(f32[2,2,256,256]{3,2,1,0:T(8,128)} %object_ref.3) | copy-start | bytes 3145732
  10.5 5.6 %copy-start.3 = (bf16[4,256,768]{2,1,0:T(8,128)(2,1)S(1)}, bf16[4,256,768]{2,1,0:T(8,128)(2,1)}, u32[]{:S(2)}) copy-start(bf16[4,256,768]{2,1,0:T(8,128)(2,1)} %constant.11.clone.row_far) | copy-start | bytes 4718596
  10.5 5.6 %copy-start.4 = (bf16[4,768,256]{2,1,0:T(8,128)(2,1)S(1)}, bf16[4,768,256]{2,1,0:T(8,128)(2,1)}, u32[]{:S(2)}) copy-start(bf16[4,768,256]{2,1,0:T(8,128)(2,1)} %constant.10.clone.col_far) | copy-start | bytes 4718596
  10.5 5.6 %copy-start.6 = (s32[1,1,1,2]{3,2,1,0:T(1,128)S(1)}, s32[1,1,1,2]{3,2,1,0:T(1,128)}, u32[]{:S(2)}) copy-start(s32[1,1,1,2]{3,2,1,0:T(1,128)} %param.8) | copy-start | bytes 28
  14.0 2.1 %collective-permute-start.3 = (f32[2,128,256]{2,1,0:T(8,128)S(1)}, f32[2,128,256]{2,1,0:T(8,128)S(1)}, u32[]{:S(2)}, u32[]{:S(2)}) collective-permute-start(f32[2,128,256]{2,1,0:T(8,128)S(1)} %collective-permute-done.below_far), channel_id=1, source_target_pairs={{0,8},{8,0},{16,24},{24,16},{32,40},{40,32},{48,56},{56,48},{64,72... | collective-permute-start | bytes 786440 | tf_op jit(solution)/shard_map/ppermute | solution.py:647
  14.0 2.1 %collective-permute-start.4 = (f32[2,256,128]{2,1,0:T(8,128)S(1)}, f32[2,256,128]{2,1,0:T(8,128)S(1)}, u32[]{:S(2)}, u32[]{:S(2)}) collective-permute-start(f32[2,256,128]{2,1,0:T(8,128)S(1)} %collective-permute-done.1.right_far), channel_id=1, source_target_pairs={{0,8},{8,0},{16,24},{24,16},{32,40},{40,32},{48,56},{56,48},{64,72... | collective-permute-start | bytes 786440 | tf_op jit(solution)/shard_map/ppermute | solution.py:647
  14.5 1.6 %collective-permute-start.5 = (f32[2,128,128]{2,1,0:T(8,128)S(1)}, f32[2,128,128]{2,1,0:T(8,128)S(1)}, u32[]{:S(2)}, u32[]{:S(2)}) collective-permute-start(f32[2,128,128]{2,1,0:T(8,128)S(1)} %collective-permute-done.2.diag_far), channel_id=1, source_target_pairs={{0,8},{8,0},{16,24},{24,16},{32,40},{40,32},{48,56},{56,48},{64,72... | collective-permute-start | bytes 393224 | tf_op jit(solution)/shard_map/ppermute | solution.py:647
  67.0 11.4 %collective-permute-start.6 = (f32[6,2,8,128]{3,2,1,0:T(8,128)S(1)}, f32[6,2,8,128]{3,2,1,0:T(8,128)S(1)}, u32[]{:S(2)}, u32[]{:S(2)}) collective-permute-start(f32[6,2,8,128]{3,2,1,0:T(8,128)S(1)} %get-tuple-element.34), channel_id=1, source_target_pairs={{0,1},{2,3},{4,5},{6,7},{8,9},{10,11},{12,13},{14,15},{16,17},{18,... | collective-permute-start | bytes 147464 | tf_op jit(solution)/shard_map/ppermute | solution.py:628
  68.3 10.1 %collective-permute-start.7 = (f32[6,8,256]{2,1,0:T(8,128)S(1)}, f32[6,8,256]{2,1,0:T(8,128)S(1)}, u32[]{:S(2)}, u32[]{:S(2)}) collective-permute-start(f32[6,8,256]{2,1,0:T(8,128)S(1)} %get-tuple-element.35), channel_id=1, source_target_pairs={{0,2},{2,4},{4,6},{1,3},{3,5},{5,7},{8,10},{10,12},{12,14},{9,11},... | collective-permute-start | bytes 147464 | tf_op jit(solution)/shard_map/ppermute | solution.py:628
  71.7 6.6 %collective-permute-start.8 = (f32[6,8,128]{2,1,0:T(8,128)S(1)}, f32[6,8,128]{2,1,0:T(8,128)S(1)}, u32[]{:S(2)}, u32[]{:S(2)}) collective-permute-start(f32[6,8,128]{2,1,0:T(8,128)S(1)} %get-tuple-element.36), channel_id=1, source_target_pairs={{0,3},{2,5},{4,7},{8,11},{10,13},{12,15},{16,19},{18,21},{20,23},{... | collective-permute-start | bytes 73736 | tf_op jit(solution)/shard_map/ppermute | solution.py:639
  78.4 5.8 %collective-permute-start.9 = (f32[1,2,2,2,8,256]{5,4,3,2,1,0:T(8,128)S(1)}, f32[1,2,2,2,8,256]{5,4,3,2,1,0:T(8,128)S(1)}, u32[]{:S(2)}, u32[]{:S(2)}) collective-permute-start(f32[1,2,2,2,8,256]{5,4,3,2,1,0:T(8,128)S(1)} %bitcast.5), channel_id=1, source_target_pairs={{0,16},{8,24},{16,0},{24,8},{32,48},{40,56},{48,32},{56,40},{64,80... | collective-permute-start | bytes 196616 | tf_op jit(solution)/shard_map/ppermute | solution.py:647
  84.3 7.3 %collective-permute-start.10 = (f32[2,2,2,2,8,256]{5,4,3,2,1,0:T(8,128)S(1)}, f32[2,2,2,2,8,256]{5,4,3,2,1,0:T(8,128)S(1)}, u32[]{:S(2)}, u32[]{:S(2)}) collective-permute-start(f32[2,2,2,2,8,256]{5,4,3,2,1,0:T(8,128)S(1)} %pad_maximum_fusion), channel_id=1, source_target_pairs={{0,32},{8,40},{16,48},{24,56},{32,64},{40,72},{48,80},{56,88},{64,... | collective-permute-start | bytes 393224 | tf_op jit(solution)/shard_map/ppermute | solution.py:647
  84.4 9.7 %collective-permute-start.12 = (f32[2,2,2,2,8,256]{5,4,3,2,1,0:T(8,128)S(1)}, f32[2,2,2,2,8,256]{5,4,3,2,1,0:T(8,128)S(1)}, u32[]{:S(2)}, u32[]{:S(2)}) collective-permute-start(f32[2,2,2,2,8,256]{5,4,3,2,1,0:T(8,128)S(1)} %pad_maximum_fusion), channel_id=1, source_target_pairs={{0,96},{8,104},{16,112},{24,120},{32,0},{40,8},{48,16},{56,24},{64... | collective-permute-start | bytes 393224 | tf_op jit(solution)/shard_map/ppermute | solution.py:647
  87.6 6.5 %collective-permute-start.11 = (f32[2,2,2,2,8,256]{5,4,3,2,1,0:T(8,128)S(1)}, f32[2,2,2,2,8,256]{5,4,3,2,1,0:T(8,128)S(1)}, u32[]{:S(2)}, u32[]{:S(2)}) collective-permute-start(f32[2,2,2,2,8,256]{5,4,3,2,1,0:T(8,128)S(1)} %pad_maximum_fusion), channel_id=1, source_target_pairs={{0,64},{8,72},{16,80},{24,88},{32,96},{40,104},{48,112},{56,120},{... | collective-permute-start | bytes 393224 | tf_op jit(solution)/shard_map/ppermute | solution.py:647
  94.1 2.0 %collective-permute-start.13 = (f32[8,2,2,2,8,256]{5,4,3,2,1,0:T(8,128)S(1)}, f32[8,2,2,2,8,256]{5,4,3,2,1,0:T(8,128)S(1)}, u32[]{:S(2)}, u32[]{:S(2)}) collective-permute-start(f32[8,2,2,2,8,256]{5,4,3,2,1,0:T(8,128)S(1)} %constant_dynamic-update-slice_fusion.refs_0_), channel_id=1, source_target_pairs={{0,8},{8,0},{16,24},{24,16},{32,40},{40,32},{48,56},{56,48},{64,72... | collective-permute-start | bytes 1572872 | tf_op jit(solution)/shard_map/ppermute | solution.py:647

commit v5 on v4

--- a/solution.py
+++ b/solution.py
@@ -356,11 +356,13 @@
         for n in range(SIDE // 8):
             rows = pl.ds(SIDE - r + 8 * n, 8)
             block = jnp.concatenate([hold[0, rows], hold[1, rows]], axis=1)
-            out_ref[n % 16, 2 * k + n // 16] = pltpu.roll(block, c, 1)
-    lane = lax.broadcasted_iota(jnp.int32, (8, SIDE), 1)
+            block = pltpu.roll(block, c, 1)
+            for h in range(2):
+                out_ref[n % 16, 4 * k + 2 * h + n // 16] = block[:, h * HALF : (h + 1) * HALF]
+    lane = lax.broadcasted_iota(jnp.int32, (8, HALF), 1)
     mark = jnp.where(lane == 0, r, c).astype(f32)
     for i in range(SCANS):
-        out_ref[i, 10] = mark
+        out_ref[i, 20] = mark
 
 
 def glow_kernel(probe_ref, measured_ref, light_ref, expected_ref, halves_ref):
@@ -462,7 +464,7 @@
     wide = (2, 2, SIDE + 2 * PAD, HALF)
     return pl.pallas_call(
         wave_kernel,
-        out_shape=jax.ShapeDtypeStruct((SCANS, 11, 8, SIDE), f32),
+        out_shape=jax.ShapeDtypeStruct((SCANS, 21, 8, HALF), f32),
         in_specs=[pl.BlockSpec(memory_space=pltpu.SMEM)] * 2
         + [pl.BlockSpec(memory_space=pl.ANY)] * 7
         + [vmem]
@@ -509,7 +511,7 @@
     me_ref, parts_ref, light_ref, own_ref, right_ref, below_ref, diag_ref, marks_ref, sem
 ):
     me = me_ref[0]
-    copy = pltpu.make_async_copy(parts_ref.at[:, 10, :, pl.ds(0, HALF)], marks_ref, sem)
+    copy = pltpu.make_async_copy(parts_ref.at[:, 20], marks_ref, sem)
     copy.start()
     own_ref[...] = jnp.zeros_like(own_ref)
     right_ref[...] = jnp.zeros_like(right_ref)
@@ -533,7 +535,10 @@
         light = jnp.concatenate(lights, axis=0)
         inside_row, inside_col = rows >= r, cols >= c
         for k in range(6):
-            value = parts_ref[j, 2 * k : 2 * k + 2] if k < 5 else light
+            value = light
+            if k < 5:
+                halves = [parts_ref[j, 4 * k + 2 * h : 4 * k + 2 * h + 2] for h in range(2)]
+                value = jnp.concatenate(halves, axis=2)
             here = jnp.where(inside_row, value, 0.0)
             there = (value - here)[0]
             own_ref[k] += jnp.where(inside_col, here, 0.0)
@@ -651,7 +656,8 @@
     me = lax.axis_index("scan").astype(jnp.int32).reshape(1)
     corner = corners.reshape(2)
     rims = run_cut(me, object_slices)
-    rims = (shift(rims[0], "tx", -1), shift(rims[1], "ty", -1), shift_both(rims[2], -1))
+    diag = shift_both(rims[2], -1)
+    rims = (shift(rims[0], "tx", -1), shift(rims[1], "ty", -1), diag)
     light, expected, halves = run_glow(probe_modes, measured.reshape(SIDE, SIDE))
     rims, light, expected, halves = lax.optimization_barrier((rims, light, expected, halves))
     others = tuple(along_scan(rim, 0, 0, 1) for rim in rims)
@@ -672,9 +678,7 @@
     mine = run_update(me, object_slices, own, to_right, to_below, to_diag)[None]
     pair = jnp.concatenate([mine, along_scan(mine, 0, 1, 0)], axis=0)
     ring = [pair] + [along_scan(pair, dy, 0, 0) for dy in (1, 2, 3)]
-    ring = jnp.concatenate(ring, axis=0)
-    other = along_scan(ring, 0, 0, 1)
-    return run_place(me, [ring, other])
+    return run_place(me, ring + [along_scan(block, 0, 0, 1) for block in ring])
 
 
 def solution(mesh):

time: 98.2 us -> 96.1 us (0.979)
    ppermute x8 -> x11, starting transfers between devices: 4.59 us -> 3.99 us  [along_scan(): return lax.ppermute(array, 'scan', pairs)]
    ppermute x8 -> x11, waiting for transfers between devices: 15.1 us -> 14.5 us  [along_scan(): return lax.ppermute(array, 'scan', pairs)]
    unnamed x18 -> x14, local copies, waits for them, and re-layouts: 4.4 us -> 4.37 us
  transfers between devices with their start and end apart: 14 -> 17, of which waited for: 7 -> 8; matrix products, arithmetic and copies ran while one was open for 0% -> 0% of each run, Pallas kernels for 2% -> 2%
where the time goes in v5:
time: 96.1 us; the launch traced here: 95 us
  blocking collectives  28.4 us (30%)
  Pallas kernels  25.2 us (26%)
  waiting for transfers between devices  21.2 us (22%)
  starting transfers between devices  15.7 us (16%)
  local copies, waits for them, and re-layouts  4.37 us (5%)
    all_to_all x1, blocking collectives, on_device(): parts = lax.all_to_all(parts, 'scan', 0, 0)  28.4 us
    pallas_call x1, Pallas kernels, run_wave(): pl.pallas_call(wave_kernel, out_shape=jax.ShapeDtypeStruct((SCANS, 21, 8,...  19.3 us
    ppermute x11, waiting for transfers between devices, along_scan(): return lax.ppermute(array, 'scan', pairs)  14.5 us
    ppermute x4, starting transfers between devices, shift(): return lax.ppermute(array, axis, pairs)  9.09 us
    ppermute x2, waiting for transfers between devices, shift_both(): return lax.ppermute(array, ('tx', 'ty'), pairs)  5.32 us
    unnamed x14, local copies, waits for them, and re-layouts  4.37 us
    ppermute x11, starting transfers between devices, along_scan(): return lax.ppermute(array, 'scan', pairs)  3.99 us
    ppermute x2, starting transfers between devices, shift_both(): return lax.ppermute(array, ('tx', 'ty'), pairs)  2.59 us
  transfers between devices with their start and end apart: 17, of which 8 were waited for; matrix products, arithmetic and copies ran while one was open for 0% of the time, Pallas kernels for 2%

profile of v5, /device:TPU:34, one launch (start us, length us, event | category | flops | bytes accessed | tf_op | source)
XLA Modules:
  0.0 95.0 jit_solution(9612565193088341014)
XLA Ops:
  0.0 0.0 copy-start
  0.0 1.2 %copy-done = f32[2,2,256,256]{3,2,1,0:T(8,128)S(1)} copy-done((f32[2,2,256,256]{3,2,1,0:T(8,128)S(1)}, f32[2,2,256,256]{3,2,1,0:T(8,128)}, u32[]{:S(2)}) %copy-start) | copy-done | bytes 1048600
  1.2 0.4 cut.1
  1.6 2.4 %collective-permute-start = (f32[2,128,256]{2,1,0:T(8,128)S(1)}, f32[2,128,256]{2,1,0:T(8,128)S(1)}, u32[]{:S(2)}, u32[]{:S(2)}) collective-permute-start(f32[2,128,256]{2,1,0:T(8,128)S(1)} %get-tuple-element.21), channel_id=1, source_target_pairs={{2,0},{4,2},{6,4},{3,1},{5,3},{7,5},{10,8},{12,10},{14,12},{11,9},... | collective-permute-start | bytes 786440 | tf_op jit(solution)/shard_map/ppermute | solution.py:633
  4.1 1.9 %collective-permute-start.1 = (f32[2,256,128]{2,1,0:T(8,128)S(1)}, f32[2,256,128]{2,1,0:T(8,128)S(1)}, u32[]{:S(2)}, u32[]{:S(2)}) collective-permute-start(f32[2,256,128]{2,1,0:T(8,128)S(1)} %get-tuple-element.22), channel_id=1, source_target_pairs={{1,0},{3,2},{5,4},{7,6},{9,8},{11,10},{13,12},{15,14},{17,16},{19,... | collective-permute-start | bytes 786440 | tf_op jit(solution)/shard_map/ppermute | solution.py:633
  6.0 1.3 %collective-permute-start.2 = (f32[2,128,128]{2,1,0:T(8,128)S(1)}, f32[2,128,128]{2,1,0:T(8,128)S(1)}, u32[]{:S(2)}, u32[]{:S(2)}) collective-permute-start(f32[2,128,128]{2,1,0:T(8,128)S(1)} %get-tuple-element.23), channel_id=1, source_target_pairs={{3,0},{5,2},{7,4},{11,8},{13,10},{15,12},{19,16},{21,18},{23,20},{... | collective-permute-start | bytes 393224 | tf_op jit(solution)/shard_map/ppermute | solution.py:644
  7.3 0.0 copy-start.2
  7.4 2.2 %copy-done.2 = f32[2,8,256,256]{3,2,1,0:T(8,128)S(1)} copy-done((f32[2,8,256,256]{3,2,1,0:T(8,128)S(1)}, f32[2,8,256,256]{3,2,1,0:T(8,128)}, u32[]{:S(2)}) %copy-start.2) | copy-done | bytes 4194328
  9.5 0.0 copy-start.5
  9.5 0.9 copy-done.5
  10.5 0.0 copy-start.1
  10.5 0.0 copy-start.3
  10.5 0.0 copy-start.4
  10.5 0.0 copy-start.6
  10.5 2.2 %glow.1 = (f32[512,256]{1,0:T(8,128)S(1)}, f32[256,256]{1,0:T(8,128)S(1)}, f32[2,8,2,256,128]{4,3,2,1,0:T(8,128)S(1)}) custom-call(f32[2,8,256,256]{3,2,1,0:T(8,128)S(1)} %copy-done.2, f32[256,256]{1,0:T(8,128)S(1)} %bitcast.4), custom_call_target="tpu_custom_call" | custom-call | flops 2097152 | bytes 4194304 | tf_op jit(solution)/shard_map/glow/pallas_call | solution.py:397
  12.7 0.0 collective-permute-done.2.diag_far
  12.7 0.0 collective-permute-done.below_far
  12.7 1.2 %collective-permute-done.1.right_far = f32[2,256,128]{2,1,0:T(8,128)S(1)} collective-permute-done((f32[2,256,128]{2,1,0:T(8,128)S(1)}, f32[2,256,128]{2,1,0:T(8,128)S(1)}, u32[]{:S(2)}, u32[]{:S(2)}) %collective-permute-start.1) | collective-permute-done | bytes 262176 | tf_op jit(solution)/shard_map/ppermute | solution.py:633
  14.0 0.0 collective-permute-start.3
  14.0 0.5 collective-permute-start.4
  14.5 0.0 collective-permute-start.5
  14.5 1.6 %collective-permute-done.5.other_diag_far = f32[2,128,128]{2,1,0:T(8,128)S(1)} collective-permute-done((f32[2,128,128]{2,1,0:T(8,128)S(1)}, f32[2,128,128]{2,1,0:T(8,128)S(1)}, u32[]{:S(2)}, u32[]{:S(2)}) %collective-permute-start.5) | collective-permute-done | bytes 131104 | tf_op jit(solution)/shard_map/ppermute | solution.py:652
  16.1 0.0 collective-permute-done.3.other_below_far
  16.1 0.0 collective-permute-done.4.other_right_far
  16.1 0.0 copy-done.1
  16.1 0.0 copy-done.3
  16.1 0.0 copy-done.4
  16.1 0.0 copy-done.6
  16.1 19.3 %wave.1 = f32[16,21,8,128]{3,2,1,0:T(8,128)S(1)} custom-call(s32[2]{0:T(128)S(1)} %bitcast.7, s32[1]{0:T(128)} %bitcast.me_ref, f32[2,128,256]{2,1,0:T(8,128)S(1)} %collective-permute-done.below_far, f32[2,256,128]{2,1,0:T(8,128)S(1)} %collective-permute-done.1.right_far, f32[2,128,128]{2,1,0:T(8,128)S(1)} %collective-permute-done.2.diag_far, ...), custom_call_target="tpu_custom_call" | custom-call | tf_op jit(solution)/shard_map/wave/pallas_call | solution.py:465
  35.4 28.4 %all_to_all.5.parts_ref = f32[16,21,8,128]{3,2,1,0:T(8,128)S(1)} all-to-all(f32[16,21,8,128]{3,2,1,0:T(8,128)S(1)} %wave.1), channel_id=1, replica_groups=mesh['scan'=16,'tx'=4,'ty'=2] {'scan'}, dimensions={0} | all-to-all | bytes 2752512 | tf_op jit(solution)/shard_map/all_to_all | solution.py:673
  63.8 2.3 %sum.1 = (f32[6,2,8,256]{3,2,1,0:T(8,128)S(1)}, f32[6,2,8,128]{3,2,1,0:T(8,128)S(1)}, f32[6,8,256]{2,1,0:T(8,128)S(1)}, f32[6,8,128]{2,1,0:T(8,128)S(1)}) custom-call(s32[1]{0:T(128)} %bitcast.me_ref, f32[16,21,8,128]{3,2,1,0:T(8,128)S(1)} %all_to_all.5.parts_ref, f32[512,256]{1,0:T(8,128)S(1)} %get-tuple-element.32.light_ref), custom_call_target="tpu_custom_call" | custom-call | tf_op jit(solution)/shard_map/sum/pallas_call | solution.py:553
  66.1 1.3 %collective-permute-start.6 = (f32[6,2,8,128]{3,2,1,0:T(8,128)S(1)}, f32[6,2,8,128]{3,2,1,0:T(8,128)S(1)}, u32[]{:S(2)}, u32[]{:S(2)}) collective-permute-start(f32[6,2,8,128]{3,2,1,0:T(8,128)S(1)} %get-tuple-element.34), channel_id=1, source_target_pairs={{0,1},{2,3},{4,5},{6,7},{8,9},{10,11},{12,13},{14,15},{16,17},{18,... | collective-permute-start | bytes 147464 | tf_op jit(solution)/shard_map/ppermute | solution.py:633
  67.4 3.4 %collective-permute-start.7 = (f32[6,8,256]{2,1,0:T(8,128)S(1)}, f32[6,8,256]{2,1,0:T(8,128)S(1)}, u32[]{:S(2)}, u32[]{:S(2)}) collective-permute-start(f32[6,8,256]{2,1,0:T(8,128)S(1)} %get-tuple-element.35), channel_id=1, source_target_pairs={{0,2},{2,4},{4,6},{1,3},{3,5},{5,7},{8,10},{10,12},{12,14},{9,11},... | collective-permute-start | bytes 147464 | tf_op jit(solution)/shard_map/ppermute | solution.py:633
  70.9 1.3 %collective-permute-start.8 = (f32[6,8,128]{2,1,0:T(8,128)S(1)}, f32[6,8,128]{2,1,0:T(8,128)S(1)}, u32[]{:S(2)}, u32[]{:S(2)}) collective-permute-start(f32[6,8,128]{2,1,0:T(8,128)S(1)} %get-tuple-element.36), channel_id=1, source_target_pairs={{0,3},{2,5},{4,7},{8,11},{10,13},{12,15},{16,19},{18,21},{20,23},{... | collective-permute-start | bytes 73736 | tf_op jit(solution)/shard_map/ppermute | solution.py:644
  72.2 5.3 %collective-permute-done.8.diag_ref = f32[6,8,128]{2,1,0:T(8,128)S(1)} collective-permute-done((f32[6,8,128]{2,1,0:T(8,128)S(1)}, f32[6,8,128]{2,1,0:T(8,128)S(1)}, u32[]{:S(2)}, u32[]{:S(2)}) %collective-permute-start.8) | collective-permute-done | bytes 24608 | tf_op jit(solution)/shard_map/ppermute | solution.py:644
  77.5 0.0 collective-permute-done.6.right_ref
  77.5 0.0 collective-permute-done.7.below_ref
  77.5 0.8 collective-permute-start.9
  78.3 5.1 %collective-permute-done.9 = f32[1,2,2,2,8,256]{5,4,3,2,1,0:T(8,128)S(1)} collective-permute-done((f32[1,2,2,2,8,256]{5,4,3,2,1,0:T(8,128)S(1)}, f32[1,2,2,2,8,256]{5,4,3,2,1,0:T(8,128)S(1)}, u32[]{:S(2)}, u32[]{:S(2)}) %collective-permute-start.9) | collective-permute-done | bytes 65568 | tf_op jit(solution)/shard_map/ppermute | solution.py:652
  83.4 1.4 %collective-permute-start.12 = (f32[2,2,2,2,8,256]{5,4,3,2,1,0:T(8,128)S(1)}, f32[2,2,2,2,8,256]{5,4,3,2,1,0:T(8,128)S(1)}, u32[]{:S(2)}, u32[]{:S(2)}) collective-permute-start(f32[2,2,2,2,8,256]{5,4,3,2,1,0:T(8,128)S(1)} %pad_maximum_fusion.refs_0_), channel_id=1, source_target_pairs={{0,96},{8,104},{16,112},{24,120},{32,0},{40,8},{48,16},{56,24},{64... | collective-permute-start | bytes 393224 | tf_op jit(solution)/shard_map/ppermute | solution.py:652
  84.7 0.5 collective-permute-start.11
  85.2 0.8 collective-permute-start.10
  86.1 0.0 collective-permute-start.13
  86.1 2.4 %collective-permute-done.12.refs_3_ = f32[2,2,2,2,8,256]{5,4,3,2,1,0:T(8,128)S(1)} collective-permute-done((f32[2,2,2,2,8,256]{5,4,3,2,1,0:T(8,128)S(1)}, f32[2,2,2,2,8,256]{5,4,3,2,1,0:T(8,128)S(1)}, u32[]{:S(2)}, u32[]{:S(2)}) %collective-permute-start.12) | collective-permute-done | bytes 131104 | tf_op jit(solution)/shard_map/ppermute | solution.py:652
  88.4 0.0 collective-permute-start.16
  88.4 2.9 %collective-permute-done.11.refs_2_ = f32[2,2,2,2,8,256]{5,4,3,2,1,0:T(8,128)S(1)} collective-permute-done((f32[2,2,2,2,8,256]{5,4,3,2,1,0:T(8,128)S(1)}, f32[2,2,2,2,8,256]{5,4,3,2,1,0:T(8,128)S(1)}, u32[]{:S(2)}, u32[]{:S(2)}) %collective-permute-start.11) | collective-permute-done | bytes 131104 | tf_op jit(solution)/shard_map/ppermute | solution.py:652
  91.3 0.0 collective-permute-start.15
  91.3 1.3 %collective-permute-done.10.refs_1_ = f32[2,2,2,2,8,256]{5,4,3,2,1,0:T(8,128)S(1)} collective-permute-done((f32[2,2,2,2,8,256]{5,4,3,2,1,0:T(8,128)S(1)}, f32[2,2,2,2,8,256]{5,4,3,2,1,0:T(8,128)S(1)}, u32[]{:S(2)}, u32[]{:S(2)}) %collective-permute-start.10) | collective-permute-done | bytes 131104 | tf_op jit(solution)/shard_map/ppermute | solution.py:652
  92.6 0.0 collective-permute-start.14
  92.6 0.0 collective-permute-done.13.refs_4_
  92.6 0.0 collective-permute-done.16.refs_7_
  92.6 0.0 collective-permute-done.15.refs_6_
  92.7 1.3 %collective-permute-done.14.refs_5_ = f32[2,2,2,2,8,256]{5,4,3,2,1,0:T(8,128)S(1)} collective-permute-done((f32[2,2,2,2,8,256]{5,4,3,2,1,0:T(8,128)S(1)}, f32[2,2,2,2,8,256]{5,4,3,2,1,0:T(8,128)S(1)}, u32[]{:S(2)}, u32[]{:S(2)}) %collective-permute-start.14) | collective-permute-done | bytes 131104 | tf_op jit(solution)/shard_map/ppermute | solution.py:652
  94.0 1.1 %place.1 = f32[2,2,256,256]{3,2,1,0:T(8,128)} custom-call(s32[1]{0:T(128)} %bitcast.me_ref, f32[2,2,2,2,8,256]{5,4,3,2,1,0:T(8,128)S(1)} %pad_maximum_fusion.refs_0_, f32[2,2,2,2,8,256]{5,4,3,2,1,0:T(8,128)S(1)} %collective-permute-done.10.refs_1_, f32[2,2,2,2,8,256]{5,4,3,2,1,0:T(8,128)S(1)} %collective-permute-done.11.refs_2_, ...), custom_call_target="tpu_custom_call" | custom-call | tf_op jit(solution)/shard_map/place/pallas_call | solution.py:620
  (2 shorter events, 0.0 us)
Async XLA Ops:
  0.0 1.2 %copy-start = (f32[2,2,256,256]{3,2,1,0:T(8,128)S(1)}, f32[2,2,256,256]{3,2,1,0:T(8,128)}, u32[]{:S(2)}) copy-start(f32[2,2,256,256]{3,2,1,0:T(8,128)} %object_ref.3) | copy-start | bytes 3145732
  1.6 11.1 %collective-permute-start = (f32[2,128,256]{2,1,0:T(8,128)S(1)}, f32[2,128,256]{2,1,0:T(8,128)S(1)}, u32[]{:S(2)}, u32[]{:S(2)}) collective-permute-start(f32[2,128,256]{2,1,0:T(8,128)S(1)} %get-tuple-element.21), channel_id=1, source_target_pairs={{2,0},{4,2},{6,4},{3,1},{5,3},{7,5},{10,8},{12,10},{14,12},{11,9},... | collective-permute-start | bytes 786440 | tf_op jit(solution)/shard_map/ppermute | solution.py:633
  4.1 9.9 %collective-permute-start.1 = (f32[2,256,128]{2,1,0:T(8,128)S(1)}, f32[2,256,128]{2,1,0:T(8,128)S(1)}, u32[]{:S(2)}, u32[]{:S(2)}) collective-permute-start(f32[2,256,128]{2,1,0:T(8,128)S(1)} %get-tuple-element.22), channel_id=1, source_target_pairs={{1,0},{3,2},{5,4},{7,6},{9,8},{11,10},{13,12},{15,14},{17,16},{19,... | collective-permute-start | bytes 786440 | tf_op jit(solution)/shard_map/ppermute | solution.py:633
  6.0 6.6 %collective-permute-start.2 = (f32[2,128,128]{2,1,0:T(8,128)S(1)}, f32[2,128,128]{2,1,0:T(8,128)S(1)}, u32[]{:S(2)}, u32[]{:S(2)}) collective-permute-start(f32[2,128,128]{2,1,0:T(8,128)S(1)} %get-tuple-element.23), channel_id=1, source_target_pairs={{3,0},{5,2},{7,4},{11,8},{13,10},{15,12},{19,16},{21,18},{23,20},{... | collective-permute-start | bytes 393224 | tf_op jit(solution)/shard_map/ppermute | solution.py:644
  7.3 2.2 %copy-start.2 = (f32[2,8,256,256]{3,2,1,0:T(8,128)S(1)}, f32[2,8,256,256]{3,2,1,0:T(8,128)}, u32[]{:S(2)}) copy-start(f32[2,8,256,256]{3,2,1,0:T(8,128)} %probe_ref.1) | copy-start | bytes 12582916
  9.5 0.9 copy-start.5
  10.5 5.6 %copy-start.1 = (f32[2,2,256,256]{3,2,1,0:T(8,128)S(1)}, f32[2,2,256,256]{3,2,1,0:T(8,128)}, u32[]{:S(2)}) copy-start(f32[2,2,256,256]{3,2,1,0:T(8,128)} %object_ref.3) | copy-start | bytes 3145732
  10.5 5.6 %copy-start.3 = (bf16[4,256,768]{2,1,0:T(8,128)(2,1)S(1)}, bf16[4,256,768]{2,1,0:T(8,128)(2,1)}, u32[]{:S(2)}) copy-start(bf16[4,256,768]{2,1,0:T(8,128)(2,1)} %constant.11.clone.row_far) | copy-start | bytes 4718596
  10.5 5.6 %copy-start.4 = (bf16[4,768,256]{2,1,0:T(8,128)(2,1)S(1)}, bf16[4,768,256]{2,1,0:T(8,128)(2,1)}, u32[]{:S(2)}) copy-start(bf16[4,768,256]{2,1,0:T(8,128)(2,1)} %constant.10.clone.col_far) | copy-start | bytes 4718596
  10.5 5.6 %copy-start.6 = (s32[1,1,1,2]{3,2,1,0:T(1,128)S(1)}, s32[1,1,1,2]{3,2,1,0:T(1,128)}, u32[]{:S(2)}) copy-start(s32[1,1,1,2]{3,2,1,0:T(1,128)} %param.8) | copy-start | bytes 28
  14.0 2.1 %collective-permute-start.3 = (f32[2,128,256]{2,1,0:T(8,128)S(1)}, f32[2,128,256]{2,1,0:T(8,128)S(1)}, u32[]{:S(2)}, u32[]{:S(2)}) collective-permute-start(f32[2,128,256]{2,1,0:T(8,128)S(1)} %collective-permute-done.below_far), channel_id=1, source_target_pairs={{0,8},{8,0},{16,24},{24,16},{32,40},{40,32},{48,56},{56,48},{64,72... | collective-permute-start | bytes 786440 | tf_op jit(solution)/shard_map/ppermute | solution.py:652
  14.0 2.1 %collective-permute-start.4 = (f32[2,256,128]{2,1,0:T(8,128)S(1)}, f32[2,256,128]{2,1,0:T(8,128)S(1)}, u32[]{:S(2)}, u32[]{:S(2)}) collective-permute-start(f32[2,256,128]{2,1,0:T(8,128)S(1)} %collective-permute-done.1.right_far), channel_id=1, source_target_pairs={{0,8},{8,0},{16,24},{24,16},{32,40},{40,32},{48,56},{56,48},{64,72... | collective-permute-start | bytes 786440 | tf_op jit(solution)/shard_map/ppermute | solution.py:652
  14.5 1.6 %collective-permute-start.5 = (f32[2,128,128]{2,1,0:T(8,128)S(1)}, f32[2,128,128]{2,1,0:T(8,128)S(1)}, u32[]{:S(2)}, u32[]{:S(2)}) collective-permute-start(f32[2,128,128]{2,1,0:T(8,128)S(1)} %collective-permute-done.2.diag_far), channel_id=1, source_target_pairs={{0,8},{8,0},{16,24},{24,16},{32,40},{40,32},{48,56},{56,48},{64,72... | collective-permute-start | bytes 393224 | tf_op jit(solution)/shard_map/ppermute | solution.py:652
  66.1 11.3 %collective-permute-start.6 = (f32[6,2,8,128]{3,2,1,0:T(8,128)S(1)}, f32[6,2,8,128]{3,2,1,0:T(8,128)S(1)}, u32[]{:S(2)}, u32[]{:S(2)}) collective-permute-start(f32[6,2,8,128]{3,2,1,0:T(8,128)S(1)} %get-tuple-element.34), channel_id=1, source_target_pairs={{0,1},{2,3},{4,5},{6,7},{8,9},{10,11},{12,13},{14,15},{16,17},{18,... | collective-permute-start | bytes 147464 | tf_op jit(solution)/shard_map/ppermute | solution.py:633
  67.4 10.0 %collective-permute-start.7 = (f32[6,8,256]{2,1,0:T(8,128)S(1)}, f32[6,8,256]{2,1,0:T(8,128)S(1)}, u32[]{:S(2)}, u32[]{:S(2)}) collective-permute-start(f32[6,8,256]{2,1,0:T(8,128)S(1)} %get-tuple-element.35), channel_id=1, source_target_pairs={{0,2},{2,4},{4,6},{1,3},{3,5},{5,7},{8,10},{10,12},{12,14},{9,11},... | collective-permute-start | bytes 147464 | tf_op jit(solution)/shard_map/ppermute | solution.py:633
  70.9 6.6 %collective-permute-start.8 = (f32[6,8,128]{2,1,0:T(8,128)S(1)}, f32[6,8,128]{2,1,0:T(8,128)S(1)}, u32[]{:S(2)}, u32[]{:S(2)}) collective-permute-start(f32[6,8,128]{2,1,0:T(8,128)S(1)} %get-tuple-element.36), channel_id=1, source_target_pairs={{0,3},{2,5},{4,7},{8,11},{10,13},{12,15},{16,19},{18,21},{20,23},{... | collective-permute-start | bytes 73736 | tf_op jit(solution)/shard_map/ppermute | solution.py:644
  77.5 5.8 %collective-permute-start.9 = (f32[1,2,2,2,8,256]{5,4,3,2,1,0:T(8,128)S(1)}, f32[1,2,2,2,8,256]{5,4,3,2,1,0:T(8,128)S(1)}, u32[]{:S(2)}, u32[]{:S(2)}) collective-permute-start(f32[1,2,2,2,8,256]{5,4,3,2,1,0:T(8,128)S(1)} %bitcast.5), channel_id=1, source_target_pairs={{0,16},{8,24},{16,0},{24,8},{32,48},{40,56},{48,32},{56,40},{64,80... | collective-permute-start | bytes 196616 | tf_op jit(solution)/shard_map/ppermute | solution.py:652
  83.4 5.0 %collective-permute-start.12 = (f32[2,2,2,2,8,256]{5,4,3,2,1,0:T(8,128)S(1)}, f32[2,2,2,2,8,256]{5,4,3,2,1,0:T(8,128)S(1)}, u32[]{:S(2)}, u32[]{:S(2)}) collective-permute-start(f32[2,2,2,2,8,256]{5,4,3,2,1,0:T(8,128)S(1)} %pad_maximum_fusion.refs_0_), channel_id=1, source_target_pairs={{0,96},{8,104},{16,112},{24,120},{32,0},{40,8},{48,16},{56,24},{64... | collective-permute-start | bytes 393224 | tf_op jit(solution)/shard_map/ppermute | solution.py:652
  84.7 6.6 %collective-permute-start.11 = (f32[2,2,2,2,8,256]{5,4,3,2,1,0:T(8,128)S(1)}, f32[2,2,2,2,8,256]{5,4,3,2,1,0:T(8,128)S(1)}, u32[]{:S(2)}, u32[]{:S(2)}) collective-permute-start(f32[2,2,2,2,8,256]{5,4,3,2,1,0:T(8,128)S(1)} %pad_maximum_fusion.refs_0_), channel_id=1, source_target_pairs={{0,64},{8,72},{16,80},{24,88},{32,96},{40,104},{48,112},{56,120},{... | collective-permute-start | bytes 393224 | tf_op jit(solution)/shard_map/ppermute | solution.py:652
  85.2 7.4 %collective-permute-start.10 = (f32[2,2,2,2,8,256]{5,4,3,2,1,0:T(8,128)S(1)}, f32[2,2,2,2,8,256]{5,4,3,2,1,0:T(8,128)S(1)}, u32[]{:S(2)}, u32[]{:S(2)}) collective-permute-start(f32[2,2,2,2,8,256]{5,4,3,2,1,0:T(8,128)S(1)} %pad_maximum_fusion.refs_0_), channel_id=1, source_target_pairs={{0,32},{8,40},{16,48},{24,56},{32,64},{40,72},{48,80},{56,88},{64,... | collective-permute-start | bytes 393224 | tf_op jit(solution)/shard_map/ppermute | solution.py:652
  86.1 6.6 %collective-permute-start.13 = (f32[2,2,2,2,8,256]{5,4,3,2,1,0:T(8,128)S(1)}, f32[2,2,2,2,8,256]{5,4,3,2,1,0:T(8,128)S(1)}, u32[]{:S(2)}, u32[]{:S(2)}) collective-permute-start(f32[2,2,2,2,8,256]{5,4,3,2,1,0:T(8,128)S(1)} %pad_maximum_fusion.refs_0_), channel_id=1, source_target_pairs={{0,8},{8,0},{16,24},{24,16},{32,40},{40,32},{48,56},{56,48},{64,72... | collective-permute-start | bytes 393224 | tf_op jit(solution)/shard_map/ppermute | solution.py:652
  88.4 4.2 %collective-permute-start.16 = (f32[2,2,2,2,8,256]{5,4,3,2,1,0:T(8,128)S(1)}, f32[2,2,2,2,8,256]{5,4,3,2,1,0:T(8,128)S(1)}, u32[]{:S(2)}, u32[]{:S(2)}) collective-permute-start(f32[2,2,2,2,8,256]{5,4,3,2,1,0:T(8,128)S(1)} %collective-permute-done.12.refs_3_), channel_id=1, source_target_pairs={{0,8},{8,0},{16,24},{24,16},{32,40},{40,32},{48,56},{56,48},{64,72... | collective-permute-start | bytes 393224 | tf_op jit(solution)/shard_map/ppermute | solution.py:652
  91.3 1.3 %collective-permute-start.15 = (f32[2,2,2,2,8,256]{5,4,3,2,1,0:T(8,128)S(1)}, f32[2,2,2,2,8,256]{5,4,3,2,1,0:T(8,128)S(1)}, u32[]{:S(2)}, u32[]{:S(2)}) collective-permute-start(f32[2,2,2,2,8,256]{5,4,3,2,1,0:T(8,128)S(1)} %collective-permute-done.11.refs_2_), channel_id=1, source_target_pairs={{0,8},{8,0},{16,24},{24,16},{32,40},{40,32},{48,56},{56,48},{64,72... | collective-permute-start | bytes 393224 | tf_op jit(solution)/shard_map/ppermute | solution.py:652
  92.6 1.3 %collective-permute-start.14 = (f32[2,2,2,2,8,256]{5,4,3,2,1,0:T(8,128)S(1)}, f32[2,2,2,2,8,256]{5,4,3,2,1,0:T(8,128)S(1)}, u32[]{:S(2)}, u32[]{:S(2)}) collective-permute-start(f32[2,2,2,2,8,256]{5,4,3,2,1,0:T(8,128)S(1)} %collective-permute-done.10.refs_1_), channel_id=1, source_target_pairs={{0,8},{8,0},{16,24},{24,16},{32,40},{40,32},{48,56},{56,48},{64,72... | collective-permute-start | bytes 393224 | tf_op jit(solution)/shard_map/ppermute | solution.py:652

commit v6 on v5

--- a/solution.py
+++ b/solution.py
@@ -204,15 +204,13 @@
     total[...] = jnp.zeros_like(total)
     field[...] = jnp.zeros_like(field)
     turned[...] = jnp.zeros_like(turned)
-    far[modes] = jnp.zeros_like(far[modes])
     starts = range(0, SIDE, ROWS)
 
     def enter(m, side):
-        held = jnp.minimum(m, modes - 1)
         for start in starts:
             rows, inner = pl.ds(start, ROWS), pl.ds(start + PAD, ROWS)
             for h in range(2):
-                p_re, p_im = probe[0, held, h, rows], probe[1, held, h, rows]
+                p_re, p_im = probe[0, m, h, rows], probe[1, m, h, rows]
                 t_re, t_im = trans[0, 0, h, rows], trans[0, 1, h, rows]
                 field[side, 0, h, inner] = p_re * t_re - p_im * t_im
                 field[side, 1, h, inner] = p_re * t_im + p_im * t_re
@@ -280,7 +278,9 @@
         beside(transform(2 * j + 1, 1), enter(2 * j + 2, 0))
         return carry
 
-    lax.fori_loop(0, modes // 2, forward, 0)
+    lax.fori_loop(0, modes // 2 - 1, forward, 0)
+    beside(transform(modes - 2, 0), enter(modes - 1, 1))
+    beside(transform(modes - 1, 1))
     misfit[...] = 2.0 * (misfit[...] - measured_ref[...])
 
     def restore(m, side):
@@ -340,6 +340,21 @@
                 total[4, h, rows] += p_re * d_im - p_im * d_re
             yield
 
+    def hand_out(*planes):
+        for k in planes:
+            for h in range(2):
+                hold[h, :SIDE] = total[k, h]
+                hold[h, SIDE:] = total[k, h]
+                yield
+            for n in range(SIDE // 8):
+                rows = pl.ds(SIDE - r + 8 * n, 8)
+                block = jnp.concatenate([hold[0, rows], hold[1, rows]], axis=1)
+                block = pltpu.roll(block, c, 1)
+                for h in range(2):
+                    out_ref[n % 16, 4 * k + 2 * h + n // 16] = block[:, h * HALF : (h + 1) * HALF]
+                if n % 4 == 3:
+                    yield
+
     beside(restore(0, 0))
 
     def backward(j, carry):
@@ -347,18 +362,11 @@
         beside(restore(2 * j + 2, 0), leave(2 * j + 1, 1))
         return carry
 
-    lax.fori_loop(0, modes // 2, backward, 0)
-
-    for k in range(5):
-        for h in range(2):
-            hold[h, :SIDE] = total[k, h]
-            hold[h, SIDE:] = total[k, h]
-        for n in range(SIDE // 8):
-            rows = pl.ds(SIDE - r + 8 * n, 8)
-            block = jnp.concatenate([hold[0, rows], hold[1, rows]], axis=1)
-            block = pltpu.roll(block, c, 1)
-            for h in range(2):
-                out_ref[n % 16, 4 * k + 2 * h + n // 16] = block[:, h * HALF : (h + 1) * HALF]
+    lax.fori_loop(0, modes // 2 - 1, backward, 0)
+    beside(restore(modes - 1, 1), leave(modes - 2, 0))
+    beside(leave(modes - 1, 1), hand_out(0, 1, 2))
+    beside(hand_out(3, 4))
+
     lane = lax.broadcasted_iota(jnp.int32, (8, HALF), 1)
     mark = jnp.where(lane == 0, r, c).astype(f32)
     for i in range(SCANS):
@@ -477,8 +485,8 @@
             pltpu.VMEM((4, SIDE, 3 * SIDE), bf16),
             pltpu.VMEM((2, 2 * SIDE, HALF), f32),
             pltpu.VMEM((LAYERS, 2) + field, f32),
-            pltpu.VMEM((2, modes + 1) + field, f32),
-            pltpu.VMEM((modes + 1, 2, SIDE, SIDE), f32),
+            pltpu.VMEM((2, modes) + field, f32),
+            pltpu.VMEM((modes, 2, SIDE, SIDE), f32),
             pltpu.VMEM((SIDE, SIDE), f32),
             pltpu.VMEM((5,) + field, f32),
             pltpu.SemaphoreType.DMA((4,)),
@@ -511,7 +519,7 @@
     me_ref, parts_ref, light_ref, own_ref, right_ref, below_ref, diag_ref, marks_ref, sem
 ):
     me = me_ref[0]
-    copy = pltpu.make_async_copy(parts_ref.at[:, 20], marks_ref, sem)
+    copy = pltpu.make_async_copy(parts_ref.at[:, 20, pl.ds(0, 1)], marks_ref, sem)
     copy.start()
     own_ref[...] = jnp.zeros_like(own_ref)
     right_ref[...] = jnp.zeros_like(right_ref)
@@ -560,7 +568,7 @@
         ),
         in_specs=[smem, vmem, vmem],
         out_specs=(vmem,) * 4,
-        scratch_shapes=[pltpu.SMEM((SCANS, 8, HALF), f32), pltpu.SemaphoreType.DMA],
+        scratch_shapes=[pltpu.SMEM((SCANS, 1, HALF), f32), pltpu.SemaphoreType.DMA],
         compiler_params=pltpu.CompilerParams(vmem_limit_bytes=8 * 1024 * 1024),
         name="sum",
     )(me, parts, light)

time: 96.1 us -> 94.5 us (0.983)
  Pallas kernels: 25.2 us -> 23.5 us
where the time goes in v6:
time: 94.5 us; the launch traced here: 93.5 us
  blocking collectives  28.5 us (30%)
  Pallas kernels  23.5 us (25%)
  waiting for transfers between devices  21.2 us (22%)
  starting transfers between devices  15.8 us (17%)
  local copies, waits for them, and re-layouts  4.37 us (5%)
    all_to_all x1, blocking collectives, on_device(): parts = lax.all_to_all(parts, 'scan', 0, 0)  28.5 us
    pallas_call x1, Pallas kernels, run_wave(): pl.pallas_call(wave_kernel, out_shape=jax.ShapeDtypeStruct((SCANS, 21, 8,...  18.5 us
    ppermute x11, waiting for transfers between devices, along_scan(): return lax.ppermute(array, 'scan', pairs)  14.5 us
    ppermute x4, starting transfers between devices, shift(): return lax.ppermute(array, axis, pairs)  9.26 us
    ppermute x2, waiting for transfers between devices, shift_both(): return lax.ppermute(array, ('tx', 'ty'), pairs)  5.32 us
    unnamed x14, local copies, waits for them, and re-layouts  4.37 us
    ppermute x11, starting transfers between devices, along_scan(): return lax.ppermute(array, 'scan', pairs)  3.99 us
    ppermute x2, starting transfers between devices, shift_both(): return lax.ppermute(array, ('tx', 'ty'), pairs)  2.59 us
  transfers between devices with their start and end apart: 17, of which 8 were waited for; matrix products, arithmetic and copies ran while one was open for 0% of the time, Pallas kernels for 2%

profile of v6, /device:TPU:34, one launch (start us, length us, event | category | flops | bytes accessed | tf_op | source)
XLA Modules:
  0.0 93.5 jit_solution(3633510290508149049)
XLA Ops:
  0.0 0.0 copy-start
  0.0 1.2 %copy-done = f32[2,2,256,256]{3,2,1,0:T(8,128)S(1)} copy-done((f32[2,2,256,256]{3,2,1,0:T(8,128)S(1)}, f32[2,2,256,256]{3,2,1,0:T(8,128)}, u32[]{:S(2)}) %copy-start) | copy-done | bytes 1048600
  1.2 0.4 cut.1
  1.6 2.4 %collective-permute-start = (f32[2,128,256]{2,1,0:T(8,128)S(1)}, f32[2,128,256]{2,1,0:T(8,128)S(1)}, u32[]{:S(2)}, u32[]{:S(2)}) collective-permute-start(f32[2,128,256]{2,1,0:T(8,128)S(1)} %get-tuple-element.21), channel_id=1, source_target_pairs={{2,0},{4,2},{6,4},{3,1},{5,3},{7,5},{10,8},{12,10},{14,12},{11,9},... | collective-permute-start | bytes 786440 | tf_op jit(solution)/shard_map/ppermute | solution.py:641
  4.1 1.9 %collective-permute-start.1 = (f32[2,256,128]{2,1,0:T(8,128)S(1)}, f32[2,256,128]{2,1,0:T(8,128)S(1)}, u32[]{:S(2)}, u32[]{:S(2)}) collective-permute-start(f32[2,256,128]{2,1,0:T(8,128)S(1)} %get-tuple-element.22), channel_id=1, source_target_pairs={{1,0},{3,2},{5,4},{7,6},{9,8},{11,10},{13,12},{15,14},{17,16},{19,... | collective-permute-start | bytes 786440 | tf_op jit(solution)/shard_map/ppermute | solution.py:641
  6.0 1.3 %collective-permute-start.2 = (f32[2,128,128]{2,1,0:T(8,128)S(1)}, f32[2,128,128]{2,1,0:T(8,128)S(1)}, u32[]{:S(2)}, u32[]{:S(2)}) collective-permute-start(f32[2,128,128]{2,1,0:T(8,128)S(1)} %get-tuple-element.23), channel_id=1, source_target_pairs={{3,0},{5,2},{7,4},{11,8},{13,10},{15,12},{19,16},{21,18},{23,20},{... | collective-permute-start | bytes 393224 | tf_op jit(solution)/shard_map/ppermute | solution.py:652
  7.3 0.0 copy-start.2
  7.4 2.2 %copy-done.2 = f32[2,8,256,256]{3,2,1,0:T(8,128)S(1)} copy-done((f32[2,8,256,256]{3,2,1,0:T(8,128)S(1)}, f32[2,8,256,256]{3,2,1,0:T(8,128)}, u32[]{:S(2)}) %copy-start.2) | copy-done | bytes 4194328
  9.5 0.0 copy-start.5
  9.5 0.9 %copy-done.5 = f32[1,1,1,256,256]{4,3,2,1,0:T(8,128)S(1)} copy-done((f32[1,1,1,256,256]{4,3,2,1,0:T(8,128)S(1)}, f32[1,1,1,256,256]{4,3,2,1,0:T(8,128)}, u32[]{:S(2)}) %copy-start.5) | copy-done | bytes 262168
  10.5 0.0 copy-start.1
  10.5 0.0 copy-start.3
  10.5 0.0 copy-start.4
  10.5 0.0 copy-start.6
  10.5 2.2 %glow.1 = (f32[512,256]{1,0:T(8,128)S(1)}, f32[256,256]{1,0:T(8,128)S(1)}, f32[2,8,2,256,128]{4,3,2,1,0:T(8,128)S(1)}) custom-call(f32[2,8,256,256]{3,2,1,0:T(8,128)S(1)} %copy-done.2, f32[256,256]{1,0:T(8,128)S(1)} %bitcast.4), custom_call_target="tpu_custom_call" | custom-call | flops 2097152 | bytes 4194304 | tf_op jit(solution)/shard_map/glow/pallas_call | solution.py:405
  12.7 0.0 collective-permute-done.2.diag_far
  12.7 0.0 collective-permute-done.below_far
  12.7 1.2 %collective-permute-done.1.right_far = f32[2,256,128]{2,1,0:T(8,128)S(1)} collective-permute-done((f32[2,256,128]{2,1,0:T(8,128)S(1)}, f32[2,256,128]{2,1,0:T(8,128)S(1)}, u32[]{:S(2)}, u32[]{:S(2)}) %collective-permute-start.1) | collective-permute-done | bytes 262176 | tf_op jit(solution)/shard_map/ppermute | solution.py:641
  14.0 0.0 collective-permute-start.3
  14.0 0.5 collective-permute-start.4
  14.5 0.0 collective-permute-start.5
  14.5 1.6 %collective-permute-done.5.other_diag_far = f32[2,128,128]{2,1,0:T(8,128)S(1)} collective-permute-done((f32[2,128,128]{2,1,0:T(8,128)S(1)}, f32[2,128,128]{2,1,0:T(8,128)S(1)}, u32[]{:S(2)}, u32[]{:S(2)}) %collective-permute-start.5) | collective-permute-done | bytes 131104 | tf_op jit(solution)/shard_map/ppermute | solution.py:660
  16.1 0.0 collective-permute-done.3.other_below_far
  16.1 0.0 collective-permute-done.4.other_right_far
  16.1 0.0 copy-done.1
  16.1 0.0 copy-done.3
  16.1 0.0 copy-done.4
  16.1 0.0 copy-done.6
  16.1 18.5 %wave.1 = f32[16,21,8,128]{3,2,1,0:T(8,128)S(1)} custom-call(s32[2]{0:T(128)S(1)} %bitcast.7, s32[1]{0:T(128)} %bitcast.me_ref, f32[2,128,256]{2,1,0:T(8,128)S(1)} %collective-permute-done.below_far, f32[2,256,128]{2,1,0:T(8,128)S(1)} %collective-permute-done.1.right_far, f32[2,128,128]{2,1,0:T(8,128)S(1)} %collective-permute-done.2.diag_far, ...), custom_call_target="tpu_custom_call" | custom-call | tf_op jit(solution)/shard_map/wave/pallas_call | solution.py:473
  34.6 28.5 %all_to_all.5.parts_ref = f32[16,21,8,128]{3,2,1,0:T(8,128)S(1)} all-to-all(f32[16,21,8,128]{3,2,1,0:T(8,128)S(1)} %wave.1), channel_id=1, replica_groups=mesh['scan'=16,'tx'=4,'ty'=2] {'scan'}, dimensions={0} | all-to-all | bytes 2752512 | tf_op jit(solution)/shard_map/all_to_all | solution.py:681
  63.0 1.4 %sum.1 = (f32[6,2,8,256]{3,2,1,0:T(8,128)S(1)}, f32[6,2,8,128]{3,2,1,0:T(8,128)S(1)}, f32[6,8,256]{2,1,0:T(8,128)S(1)}, f32[6,8,128]{2,1,0:T(8,128)S(1)}) custom-call(s32[1]{0:T(128)} %bitcast.me_ref, f32[16,21,8,128]{3,2,1,0:T(8,128)S(1)} %all_to_all.5.parts_ref, f32[512,256]{1,0:T(8,128)S(1)} %get-tuple-element.32.light_ref), custom_call_target="tpu_custom_call" | custom-call | tf_op jit(solution)/shard_map/sum/pallas_call | solution.py:561
  64.4 1.3 %collective-permute-start.6 = (f32[6,2,8,128]{3,2,1,0:T(8,128)S(1)}, f32[6,2,8,128]{3,2,1,0:T(8,128)S(1)}, u32[]{:S(2)}, u32[]{:S(2)}) collective-permute-start(f32[6,2,8,128]{3,2,1,0:T(8,128)S(1)} %get-tuple-element.34), channel_id=1, source_target_pairs={{0,1},{2,3},{4,5},{6,7},{8,9},{10,11},{12,13},{14,15},{16,17},{18,... | collective-permute-start | bytes 147464 | tf_op jit(solution)/shard_map/ppermute | solution.py:641
  65.7 3.6 %collective-permute-start.7 = (f32[6,8,256]{2,1,0:T(8,128)S(1)}, f32[6,8,256]{2,1,0:T(8,128)S(1)}, u32[]{:S(2)}, u32[]{:S(2)}) collective-permute-start(f32[6,8,256]{2,1,0:T(8,128)S(1)} %get-tuple-element.35), channel_id=1, source_target_pairs={{0,2},{2,4},{4,6},{1,3},{3,5},{5,7},{8,10},{10,12},{12,14},{9,11},... | collective-permute-start | bytes 147464 | tf_op jit(solution)/shard_map/ppermute | solution.py:641
  69.3 1.3 %collective-permute-start.8 = (f32[6,8,128]{2,1,0:T(8,128)S(1)}, f32[6,8,128]{2,1,0:T(8,128)S(1)}, u32[]{:S(2)}, u32[]{:S(2)}) collective-permute-start(f32[6,8,128]{2,1,0:T(8,128)S(1)} %get-tuple-element.36), channel_id=1, source_target_pairs={{0,3},{2,5},{4,7},{8,11},{10,13},{12,15},{16,19},{18,21},{20,23},{... | collective-permute-start | bytes 73736 | tf_op jit(solution)/shard_map/ppermute | solution.py:652
  70.6 5.3 %collective-permute-done.8.diag_ref = f32[6,8,128]{2,1,0:T(8,128)S(1)} collective-permute-done((f32[6,8,128]{2,1,0:T(8,128)S(1)}, f32[6,8,128]{2,1,0:T(8,128)S(1)}, u32[]{:S(2)}, u32[]{:S(2)}) %collective-permute-start.8) | collective-permute-done | bytes 24608 | tf_op jit(solution)/shard_map/ppermute | solution.py:652
  76.0 0.0 collective-permute-done.6.right_ref
  76.0 0.0 collective-permute-done.7.below_ref
  76.0 0.8 collective-permute-start.9
  76.8 5.1 %collective-permute-done.9 = f32[1,2,2,2,8,256]{5,4,3,2,1,0:T(8,128)S(1)} collective-permute-done((f32[1,2,2,2,8,256]{5,4,3,2,1,0:T(8,128)S(1)}, f32[1,2,2,2,8,256]{5,4,3,2,1,0:T(8,128)S(1)}, u32[]{:S(2)}, u32[]{:S(2)}) %collective-permute-start.9) | collective-permute-done | bytes 65568 | tf_op jit(solution)/shard_map/ppermute | solution.py:660
  81.8 1.4 %collective-permute-start.12 = (f32[2,2,2,2,8,256]{5,4,3,2,1,0:T(8,128)S(1)}, f32[2,2,2,2,8,256]{5,4,3,2,1,0:T(8,128)S(1)}, u32[]{:S(2)}, u32[]{:S(2)}) collective-permute-start(f32[2,2,2,2,8,256]{5,4,3,2,1,0:T(8,128)S(1)} %pad_maximum_fusion.refs_0_), channel_id=1, source_target_pairs={{0,96},{8,104},{16,112},{24,120},{32,0},{40,8},{48,16},{56,24},{64... | collective-permute-start | bytes 393224 | tf_op jit(solution)/shard_map/ppermute | solution.py:660
  83.2 0.5 collective-permute-start.11
  83.7 0.8 collective-permute-start.10
  84.5 0.0 collective-permute-start.13
  84.5 2.4 %collective-permute-done.12.refs_3_ = f32[2,2,2,2,8,256]{5,4,3,2,1,0:T(8,128)S(1)} collective-permute-done((f32[2,2,2,2,8,256]{5,4,3,2,1,0:T(8,128)S(1)}, f32[2,2,2,2,8,256]{5,4,3,2,1,0:T(8,128)S(1)}, u32[]{:S(2)}, u32[]{:S(2)}) %collective-permute-start.12) | collective-permute-done | bytes 131104 | tf_op jit(solution)/shard_map/ppermute | solution.py:660
  86.9 0.0 collective-permute-start.16
  86.9 2.9 %collective-permute-done.11.refs_2_ = f32[2,2,2,2,8,256]{5,4,3,2,1,0:T(8,128)S(1)} collective-permute-done((f32[2,2,2,2,8,256]{5,4,3,2,1,0:T(8,128)S(1)}, f32[2,2,2,2,8,256]{5,4,3,2,1,0:T(8,128)S(1)}, u32[]{:S(2)}, u32[]{:S(2)}) %collective-permute-start.11) | collective-permute-done | bytes 131104 | tf_op jit(solution)/shard_map/ppermute | solution.py:660
  89.8 0.0 collective-permute-start.15
  89.8 1.3 %collective-permute-done.10.refs_1_ = f32[2,2,2,2,8,256]{5,4,3,2,1,0:T(8,128)S(1)} collective-permute-done((f32[2,2,2,2,8,256]{5,4,3,2,1,0:T(8,128)S(1)}, f32[2,2,2,2,8,256]{5,4,3,2,1,0:T(8,128)S(1)}, u32[]{:S(2)}, u32[]{:S(2)}) %collective-permute-start.10) | collective-permute-done | bytes 131104 | tf_op jit(solution)/shard_map/ppermute | solution.py:660
  91.1 0.0 collective-permute-start.14
  91.1 0.0 collective-permute-done.13.refs_4_
  91.1 0.0 collective-permute-done.16.refs_7_
  91.1 0.0 collective-permute-done.15.refs_6_
  91.1 1.3 %collective-permute-done.14.refs_5_ = f32[2,2,2,2,8,256]{5,4,3,2,1,0:T(8,128)S(1)} collective-permute-done((f32[2,2,2,2,8,256]{5,4,3,2,1,0:T(8,128)S(1)}, f32[2,2,2,2,8,256]{5,4,3,2,1,0:T(8,128)S(1)}, u32[]{:S(2)}, u32[]{:S(2)}) %collective-permute-start.14) | collective-permute-done | bytes 131104 | tf_op jit(solution)/shard_map/ppermute | solution.py:660
  92.4 1.1 %place.1 = f32[2,2,256,256]{3,2,1,0:T(8,128)} custom-call(s32[1]{0:T(128)} %bitcast.me_ref, f32[2,2,2,2,8,256]{5,4,3,2,1,0:T(8,128)S(1)} %pad_maximum_fusion.refs_0_, f32[2,2,2,2,8,256]{5,4,3,2,1,0:T(8,128)S(1)} %collective-permute-done.10.refs_1_, f32[2,2,2,2,8,256]{5,4,3,2,1,0:T(8,128)S(1)} %collective-permute-done.11.refs_2_, ...), custom_call_target="tpu_custom_call" | custom-call | tf_op jit(solution)/shard_map/place/pallas_call | solution.py:628
  (2 shorter events, 0.0 us)
Async XLA Ops:
  0.0 1.2 %copy-start = (f32[2,2,256,256]{3,2,1,0:T(8,128)S(1)}, f32[2,2,256,256]{3,2,1,0:T(8,128)}, u32[]{:S(2)}) copy-start(f32[2,2,256,256]{3,2,1,0:T(8,128)} %object_ref.3) | copy-start | bytes 3145732
  1.6 11.1 %collective-permute-start = (f32[2,128,256]{2,1,0:T(8,128)S(1)}, f32[2,128,256]{2,1,0:T(8,128)S(1)}, u32[]{:S(2)}, u32[]{:S(2)}) collective-permute-start(f32[2,128,256]{2,1,0:T(8,128)S(1)} %get-tuple-element.21), channel_id=1, source_target_pairs={{2,0},{4,2},{6,4},{3,1},{5,3},{7,5},{10,8},{12,10},{14,12},{11,9},... | collective-permute-start | bytes 786440 | tf_op jit(solution)/shard_map/ppermute | solution.py:641
  4.1 9.9 %collective-permute-start.1 = (f32[2,256,128]{2,1,0:T(8,128)S(1)}, f32[2,256,128]{2,1,0:T(8,128)S(1)}, u32[]{:S(2)}, u32[]{:S(2)}) collective-permute-start(f32[2,256,128]{2,1,0:T(8,128)S(1)} %get-tuple-element.22), channel_id=1, source_target_pairs={{1,0},{3,2},{5,4},{7,6},{9,8},{11,10},{13,12},{15,14},{17,16},{19,... | collective-permute-start | bytes 786440 | tf_op jit(solution)/shard_map/ppermute | solution.py:641
  6.0 6.6 %collective-permute-start.2 = (f32[2,128,128]{2,1,0:T(8,128)S(1)}, f32[2,128,128]{2,1,0:T(8,128)S(1)}, u32[]{:S(2)}, u32[]{:S(2)}) collective-permute-start(f32[2,128,128]{2,1,0:T(8,128)S(1)} %get-tuple-element.23), channel_id=1, source_target_pairs={{3,0},{5,2},{7,4},{11,8},{13,10},{15,12},{19,16},{21,18},{23,20},{... | collective-permute-start | bytes 393224 | tf_op jit(solution)/shard_map/ppermute | solution.py:652
  7.3 2.2 %copy-start.2 = (f32[2,8,256,256]{3,2,1,0:T(8,128)S(1)}, f32[2,8,256,256]{3,2,1,0:T(8,128)}, u32[]{:S(2)}) copy-start(f32[2,8,256,256]{3,2,1,0:T(8,128)} %probe_ref.1) | copy-start | bytes 12582916
  9.5 0.9 %copy-start.5 = (f32[1,1,1,256,256]{4,3,2,1,0:T(8,128)S(1)}, f32[1,1,1,256,256]{4,3,2,1,0:T(8,128)}, u32[]{:S(2)}) copy-start(f32[1,1,1,256,256]{4,3,2,1,0:T(8,128)} %param.9) | copy-start | bytes 786436
  10.5 5.6 %copy-start.1 = (f32[2,2,256,256]{3,2,1,0:T(8,128)S(1)}, f32[2,2,256,256]{3,2,1,0:T(8,128)}, u32[]{:S(2)}) copy-start(f32[2,2,256,256]{3,2,1,0:T(8,128)} %object_ref.3) | copy-start | bytes 3145732
  10.5 5.6 %copy-start.3 = (bf16[4,256,768]{2,1,0:T(8,128)(2,1)S(1)}, bf16[4,256,768]{2,1,0:T(8,128)(2,1)}, u32[]{:S(2)}) copy-start(bf16[4,256,768]{2,1,0:T(8,128)(2,1)} %constant.11.clone.row_far) | copy-start | bytes 4718596
  10.5 5.6 %copy-start.4 = (bf16[4,768,256]{2,1,0:T(8,128)(2,1)S(1)}, bf16[4,768,256]{2,1,0:T(8,128)(2,1)}, u32[]{:S(2)}) copy-start(bf16[4,768,256]{2,1,0:T(8,128)(2,1)} %constant.10.clone.col_far) | copy-start | bytes 4718596
  10.5 5.6 %copy-start.6 = (s32[1,1,1,2]{3,2,1,0:T(1,128)S(1)}, s32[1,1,1,2]{3,2,1,0:T(1,128)}, u32[]{:S(2)}) copy-start(s32[1,1,1,2]{3,2,1,0:T(1,128)} %param.8) | copy-start | bytes 28
  14.0 2.1 %collective-permute-start.3 = (f32[2,128,256]{2,1,0:T(8,128)S(1)}, f32[2,128,256]{2,1,0:T(8,128)S(1)}, u32[]{:S(2)}, u32[]{:S(2)}) collective-permute-start(f32[2,128,256]{2,1,0:T(8,128)S(1)} %collective-permute-done.below_far), channel_id=1, source_target_pairs={{0,8},{8,0},{16,24},{24,16},{32,40},{40,32},{48,56},{56,48},{64,72... | collective-permute-start | bytes 786440 | tf_op jit(solution)/shard_map/ppermute | solution.py:660
  14.0 2.1 %collective-permute-start.4 = (f32[2,256,128]{2,1,0:T(8,128)S(1)}, f32[2,256,128]{2,1,0:T(8,128)S(1)}, u32[]{:S(2)}, u32[]{:S(2)}) collective-permute-start(f32[2,256,128]{2,1,0:T(8,128)S(1)} %collective-permute-done.1.right_far), channel_id=1, source_target_pairs={{0,8},{8,0},{16,24},{24,16},{32,40},{40,32},{48,56},{56,48},{64,72... | collective-permute-start | bytes 786440 | tf_op jit(solution)/shard_map/ppermute | solution.py:660
  14.5 1.6 %collective-permute-start.5 = (f32[2,128,128]{2,1,0:T(8,128)S(1)}, f32[2,128,128]{2,1,0:T(8,128)S(1)}, u32[]{:S(2)}, u32[]{:S(2)}) collective-permute-start(f32[2,128,128]{2,1,0:T(8,128)S(1)} %collective-permute-done.2.diag_far), channel_id=1, source_target_pairs={{0,8},{8,0},{16,24},{24,16},{32,40},{40,32},{48,56},{56,48},{64,72... | collective-permute-start | bytes 393224 | tf_op jit(solution)/shard_map/ppermute | solution.py:660
  64.4 11.5 %collective-permute-start.6 = (f32[6,2,8,128]{3,2,1,0:T(8,128)S(1)}, f32[6,2,8,128]{3,2,1,0:T(8,128)S(1)}, u32[]{:S(2)}, u32[]{:S(2)}) collective-permute-start(f32[6,2,8,128]{3,2,1,0:T(8,128)S(1)} %get-tuple-element.34), channel_id=1, source_target_pairs={{0,1},{2,3},{4,5},{6,7},{8,9},{10,11},{12,13},{14,15},{16,17},{18,... | collective-permute-start | bytes 147464 | tf_op jit(solution)/shard_map/ppermute | solution.py:641
  65.7 10.2 %collective-permute-start.7 = (f32[6,8,256]{2,1,0:T(8,128)S(1)}, f32[6,8,256]{2,1,0:T(8,128)S(1)}, u32[]{:S(2)}, u32[]{:S(2)}) collective-permute-start(f32[6,8,256]{2,1,0:T(8,128)S(1)} %get-tuple-element.35), channel_id=1, source_target_pairs={{0,2},{2,4},{4,6},{1,3},{3,5},{5,7},{8,10},{10,12},{12,14},{9,11},... | collective-permute-start | bytes 147464 | tf_op jit(solution)/shard_map/ppermute | solution.py:641
  69.3 6.6 %collective-permute-start.8 = (f32[6,8,128]{2,1,0:T(8,128)S(1)}, f32[6,8,128]{2,1,0:T(8,128)S(1)}, u32[]{:S(2)}, u32[]{:S(2)}) collective-permute-start(f32[6,8,128]{2,1,0:T(8,128)S(1)} %get-tuple-element.36), channel_id=1, source_target_pairs={{0,3},{2,5},{4,7},{8,11},{10,13},{12,15},{16,19},{18,21},{20,23},{... | collective-permute-start | bytes 73736 | tf_op jit(solution)/shard_map/ppermute | solution.py:652
  76.0 5.8 %collective-permute-start.9 = (f32[1,2,2,2,8,256]{5,4,3,2,1,0:T(8,128)S(1)}, f32[1,2,2,2,8,256]{5,4,3,2,1,0:T(8,128)S(1)}, u32[]{:S(2)}, u32[]{:S(2)}) collective-permute-start(f32[1,2,2,2,8,256]{5,4,3,2,1,0:T(8,128)S(1)} %bitcast.5), channel_id=1, source_target_pairs={{0,16},{8,24},{16,0},{24,8},{32,48},{40,56},{48,32},{56,40},{64,80... | collective-permute-start | bytes 196616 | tf_op jit(solution)/shard_map/ppermute | solution.py:660
  81.8 5.0 %collective-permute-start.12 = (f32[2,2,2,2,8,256]{5,4,3,2,1,0:T(8,128)S(1)}, f32[2,2,2,2,8,256]{5,4,3,2,1,0:T(8,128)S(1)}, u32[]{:S(2)}, u32[]{:S(2)}) collective-permute-start(f32[2,2,2,2,8,256]{5,4,3,2,1,0:T(8,128)S(1)} %pad_maximum_fusion.refs_0_), channel_id=1, source_target_pairs={{0,96},{8,104},{16,112},{24,120},{32,0},{40,8},{48,16},{56,24},{64... | collective-permute-start | bytes 393224 | tf_op jit(solution)/shard_map/ppermute | solution.py:660
  83.2 6.6 %collective-permute-start.11 = (f32[2,2,2,2,8,256]{5,4,3,2,1,0:T(8,128)S(1)}, f32[2,2,2,2,8,256]{5,4,3,2,1,0:T(8,128)S(1)}, u32[]{:S(2)}, u32[]{:S(2)}) collective-permute-start(f32[2,2,2,2,8,256]{5,4,3,2,1,0:T(8,128)S(1)} %pad_maximum_fusion.refs_0_), channel_id=1, source_target_pairs={{0,64},{8,72},{16,80},{24,88},{32,96},{40,104},{48,112},{56,120},{... | collective-permute-start | bytes 393224 | tf_op jit(solution)/shard_map/ppermute | solution.py:660
  83.7 7.4 %collective-permute-start.10 = (f32[2,2,2,2,8,256]{5,4,3,2,1,0:T(8,128)S(1)}, f32[2,2,2,2,8,256]{5,4,3,2,1,0:T(8,128)S(1)}, u32[]{:S(2)}, u32[]{:S(2)}) collective-permute-start(f32[2,2,2,2,8,256]{5,4,3,2,1,0:T(8,128)S(1)} %pad_maximum_fusion.refs_0_), channel_id=1, source_target_pairs={{0,32},{8,40},{16,48},{24,56},{32,64},{40,72},{48,80},{56,88},{64,... | collective-permute-start | bytes 393224 | tf_op jit(solution)/shard_map/ppermute | solution.py:660
  84.5 6.6 %collective-permute-start.13 = (f32[2,2,2,2,8,256]{5,4,3,2,1,0:T(8,128)S(1)}, f32[2,2,2,2,8,256]{5,4,3,2,1,0:T(8,128)S(1)}, u32[]{:S(2)}, u32[]{:S(2)}) collective-permute-start(f32[2,2,2,2,8,256]{5,4,3,2,1,0:T(8,128)S(1)} %pad_maximum_fusion.refs_0_), channel_id=1, source_target_pairs={{0,8},{8,0},{16,24},{24,16},{32,40},{40,32},{48,56},{56,48},{64,72... | collective-permute-start | bytes 393224 | tf_op jit(solution)/shard_map/ppermute | solution.py:660
  86.9 4.2 %collective-permute-start.16 = (f32[2,2,2,2,8,256]{5,4,3,2,1,0:T(8,128)S(1)}, f32[2,2,2,2,8,256]{5,4,3,2,1,0:T(8,128)S(1)}, u32[]{:S(2)}, u32[]{:S(2)}) collective-permute-start(f32[2,2,2,2,8,256]{5,4,3,2,1,0:T(8,128)S(1)} %collective-permute-done.12.refs_3_), channel_id=1, source_target_pairs={{0,8},{8,0},{16,24},{24,16},{32,40},{40,32},{48,56},{56,48},{64,72... | collective-permute-start | bytes 393224 | tf_op jit(solution)/shard_map/ppermute | solution.py:660
  89.8 1.3 %collective-permute-start.15 = (f32[2,2,2,2,8,256]{5,4,3,2,1,0:T(8,128)S(1)}, f32[2,2,2,2,8,256]{5,4,3,2,1,0:T(8,128)S(1)}, u32[]{:S(2)}, u32[]{:S(2)}) collective-permute-start(f32[2,2,2,2,8,256]{5,4,3,2,1,0:T(8,128)S(1)} %collective-permute-done.11.refs_2_), channel_id=1, source_target_pairs={{0,8},{8,0},{16,24},{24,16},{32,40},{40,32},{48,56},{56,48},{64,72... | collective-permute-start | bytes 393224 | tf_op jit(solution)/shard_map/ppermute | solution.py:660
  91.1 1.3 %collective-permute-start.14 = (f32[2,2,2,2,8,256]{5,4,3,2,1,0:T(8,128)S(1)}, f32[2,2,2,2,8,256]{5,4,3,2,1,0:T(8,128)S(1)}, u32[]{:S(2)}, u32[]{:S(2)}) collective-permute-start(f32[2,2,2,2,8,256]{5,4,3,2,1,0:T(8,128)S(1)} %collective-permute-done.10.refs_1_), channel_id=1, source_target_pairs={{0,8},{8,0},{16,24},{24,16},{32,40},{40,32},{48,56},{56,48},{64,72... | collective-permute-start | bytes 393224 | tf_op jit(solution)/shard_map/ppermute | solution.py:660

commit v7 on v6

--- a/solution.py
+++ b/solution.py
@@ -15,7 +15,7 @@
 HALF = 128
 LAYERS = 2
 SCANS = 16
-ROWS = 32
+ROWS = 16
 PAD = 8
 f32 = jnp.float32
 bf16 = jnp.bfloat16

time: 94.5 us -> 93.7 us (level)
  no operation moved by 1% of the time
where the time goes in v7:
time: 93.7 us; the launch traced here: 92.7 us
  blocking collectives  28.4 us (30%)
  Pallas kernels  22.9 us (24%)
  waiting for transfers between devices  21.1 us (23%)
  starting transfers between devices  15.7 us (17%)
  local copies, waits for them, and re-layouts  4.37 us (5%)
    all_to_all x1, blocking collectives, on_device(): parts = lax.all_to_all(parts, 'scan', 0, 0)  28.4 us
    pallas_call x1, Pallas kernels, run_wave(): pl.pallas_call(wave_kernel, out_shape=jax.ShapeDtypeStruct((SCANS, 21, 8,...  17.8 us
    ppermute x11, waiting for transfers between devices, along_scan(): return lax.ppermute(array, 'scan', pairs)  14.5 us
    ppermute x4, starting transfers between devices, shift(): return lax.ppermute(array, axis, pairs)  9.08 us
    ppermute x2, waiting for transfers between devices, shift_both(): return lax.ppermute(array, ('tx', 'ty'), pairs)  5.32 us
    unnamed x14, local copies, waits for them, and re-layouts  4.37 us
    ppermute x11, starting transfers between devices, along_scan(): return lax.ppermute(array, 'scan', pairs)  3.99 us
    ppermute x2, starting transfers between devices, shift_both(): return lax.ppermute(array, ('tx', 'ty'), pairs)  2.59 us
  transfers between devices with their start and end apart: 17, of which 8 were waited for; matrix products, arithmetic and copies ran while one was open for 0% of the time, Pallas kernels for 2%

profile of v7, /device:TPU:34, one launch (start us, length us, event | category | flops | bytes accessed | tf_op | source)
XLA Modules:
  0.0 92.7 jit_solution(14171999724611791802)
XLA Ops:
  0.0 0.0 copy-start
  0.0 1.2 %copy-done = f32[2,2,256,256]{3,2,1,0:T(8,128)S(1)} copy-done((f32[2,2,256,256]{3,2,1,0:T(8,128)S(1)}, f32[2,2,256,256]{3,2,1,0:T(8,128)}, u32[]{:S(2)}) %copy-start) | copy-done | bytes 1048600
  1.2 0.4 cut.1
  1.6 2.4 %collective-permute-start = (f32[2,128,256]{2,1,0:T(8,128)S(1)}, f32[2,128,256]{2,1,0:T(8,128)S(1)}, u32[]{:S(2)}, u32[]{:S(2)}) collective-permute-start(f32[2,128,256]{2,1,0:T(8,128)S(1)} %get-tuple-element.21), channel_id=1, source_target_pairs={{2,0},{4,2},{6,4},{3,1},{5,3},{7,5},{10,8},{12,10},{14,12},{11,9},... | collective-permute-start | bytes 786440 | tf_op jit(solution)/shard_map/ppermute | solution.py:641
  4.1 1.9 %collective-permute-start.1 = (f32[2,256,128]{2,1,0:T(8,128)S(1)}, f32[2,256,128]{2,1,0:T(8,128)S(1)}, u32[]{:S(2)}, u32[]{:S(2)}) collective-permute-start(f32[2,256,128]{2,1,0:T(8,128)S(1)} %get-tuple-element.22), channel_id=1, source_target_pairs={{1,0},{3,2},{5,4},{7,6},{9,8},{11,10},{13,12},{15,14},{17,16},{19,... | collective-permute-start | bytes 786440 | tf_op jit(solution)/shard_map/ppermute | solution.py:641
  6.0 1.3 %collective-permute-start.2 = (f32[2,128,128]{2,1,0:T(8,128)S(1)}, f32[2,128,128]{2,1,0:T(8,128)S(1)}, u32[]{:S(2)}, u32[]{:S(2)}) collective-permute-start(f32[2,128,128]{2,1,0:T(8,128)S(1)} %get-tuple-element.23), channel_id=1, source_target_pairs={{3,0},{5,2},{7,4},{11,8},{13,10},{15,12},{19,16},{21,18},{23,20},{... | collective-permute-start | bytes 393224 | tf_op jit(solution)/shard_map/ppermute | solution.py:652
  7.3 0.0 copy-start.2
  7.4 2.2 %copy-done.2 = f32[2,8,256,256]{3,2,1,0:T(8,128)S(1)} copy-done((f32[2,8,256,256]{3,2,1,0:T(8,128)S(1)}, f32[2,8,256,256]{3,2,1,0:T(8,128)}, u32[]{:S(2)}) %copy-start.2) | copy-done | bytes 4194328
  9.5 0.0 copy-start.5
  9.5 0.9 %copy-done.5 = f32[1,1,1,256,256]{4,3,2,1,0:T(8,128)S(1)} copy-done((f32[1,1,1,256,256]{4,3,2,1,0:T(8,128)S(1)}, f32[1,1,1,256,256]{4,3,2,1,0:T(8,128)}, u32[]{:S(2)}) %copy-start.5) | copy-done | bytes 262168
  10.5 0.0 copy-start.1
  10.5 0.0 copy-start.3
  10.5 0.0 copy-start.4
  10.5 0.0 copy-start.6
  10.5 2.2 %glow.1 = (f32[512,256]{1,0:T(8,128)S(1)}, f32[256,256]{1,0:T(8,128)S(1)}, f32[2,8,2,256,128]{4,3,2,1,0:T(8,128)S(1)}) custom-call(f32[2,8,256,256]{3,2,1,0:T(8,128)S(1)} %copy-done.2, f32[256,256]{1,0:T(8,128)S(1)} %bitcast.4), custom_call_target="tpu_custom_call" | custom-call | flops 2097152 | bytes 4194304 | tf_op jit(solution)/shard_map/glow/pallas_call | solution.py:405
  12.7 0.0 collective-permute-done.2.diag_far
  12.7 0.0 collective-permute-done.below_far
  12.7 1.2 %collective-permute-done.1.right_far = f32[2,256,128]{2,1,0:T(8,128)S(1)} collective-permute-done((f32[2,256,128]{2,1,0:T(8,128)S(1)}, f32[2,256,128]{2,1,0:T(8,128)S(1)}, u32[]{:S(2)}, u32[]{:S(2)}) %collective-permute-start.1) | collective-permute-done | bytes 262176 | tf_op jit(solution)/shard_map/ppermute | solution.py:641
  14.0 0.0 collective-permute-start.3
  14.0 0.5 collective-permute-start.4
  14.5 0.0 collective-permute-start.5
  14.5 1.6 %collective-permute-done.5.other_diag_far = f32[2,128,128]{2,1,0:T(8,128)S(1)} collective-permute-done((f32[2,128,128]{2,1,0:T(8,128)S(1)}, f32[2,128,128]{2,1,0:T(8,128)S(1)}, u32[]{:S(2)}, u32[]{:S(2)}) %collective-permute-start.5) | collective-permute-done | bytes 131104 | tf_op jit(solution)/shard_map/ppermute | solution.py:660
  16.1 0.0 collective-permute-done.3.other_below_far
  16.1 0.0 collective-permute-done.4.other_right_far
  16.1 0.0 copy-done.1
  16.1 0.0 copy-done.3
  16.1 0.0 copy-done.4
  16.1 0.0 copy-done.6
  16.1 17.8 %wave.1 = f32[16,21,8,128]{3,2,1,0:T(8,128)S(1)} custom-call(s32[2]{0:T(128)S(1)} %bitcast.7, s32[1]{0:T(128)} %bitcast.me_ref, f32[2,128,256]{2,1,0:T(8,128)S(1)} %collective-permute-done.below_far, f32[2,256,128]{2,1,0:T(8,128)S(1)} %collective-permute-done.1.right_far, f32[2,128,128]{2,1,0:T(8,128)S(1)} %collective-permute-done.2.diag_far, ...), custom_call_target="tpu_custom_call" | custom-call | tf_op jit(solution)/shard_map/wave/pallas_call | solution.py:473
  34.0 28.4 %all_to_all.5.parts_ref = f32[16,21,8,128]{3,2,1,0:T(8,128)S(1)} all-to-all(f32[16,21,8,128]{3,2,1,0:T(8,128)S(1)} %wave.1), channel_id=1, replica_groups=mesh['scan'=16,'tx'=4,'ty'=2] {'scan'}, dimensions={0} | all-to-all | bytes 2752512 | tf_op jit(solution)/shard_map/all_to_all | solution.py:681
  62.4 1.4 %sum.1 = (f32[6,2,8,256]{3,2,1,0:T(8,128)S(1)}, f32[6,2,8,128]{3,2,1,0:T(8,128)S(1)}, f32[6,8,256]{2,1,0:T(8,128)S(1)}, f32[6,8,128]{2,1,0:T(8,128)S(1)}) custom-call(s32[1]{0:T(128)} %bitcast.me_ref, f32[16,21,8,128]{3,2,1,0:T(8,128)S(1)} %all_to_all.5.parts_ref, f32[512,256]{1,0:T(8,128)S(1)} %get-tuple-element.32.light_ref), custom_call_target="tpu_custom_call" | custom-call | tf_op jit(solution)/shard_map/sum/pallas_call | solution.py:561
  63.8 1.3 %collective-permute-start.6 = (f32[6,2,8,128]{3,2,1,0:T(8,128)S(1)}, f32[6,2,8,128]{3,2,1,0:T(8,128)S(1)}, u32[]{:S(2)}, u32[]{:S(2)}) collective-permute-start(f32[6,2,8,128]{3,2,1,0:T(8,128)S(1)} %get-tuple-element.34), channel_id=1, source_target_pairs={{0,1},{2,3},{4,5},{6,7},{8,9},{10,11},{12,13},{14,15},{16,17},{18,... | collective-permute-start | bytes 147464 | tf_op jit(solution)/shard_map/ppermute | solution.py:641
  65.1 3.4 %collective-permute-start.7 = (f32[6,8,256]{2,1,0:T(8,128)S(1)}, f32[6,8,256]{2,1,0:T(8,128)S(1)}, u32[]{:S(2)}, u32[]{:S(2)}) collective-permute-start(f32[6,8,256]{2,1,0:T(8,128)S(1)} %get-tuple-element.35), channel_id=1, source_target_pairs={{0,2},{2,4},{4,6},{1,3},{3,5},{5,7},{8,10},{10,12},{12,14},{9,11},... | collective-permute-start | bytes 147464 | tf_op jit(solution)/shard_map/ppermute | solution.py:641
  68.5 1.3 %collective-permute-start.8 = (f32[6,8,128]{2,1,0:T(8,128)S(1)}, f32[6,8,128]{2,1,0:T(8,128)S(1)}, u32[]{:S(2)}, u32[]{:S(2)}) collective-permute-start(f32[6,8,128]{2,1,0:T(8,128)S(1)} %get-tuple-element.36), channel_id=1, source_target_pairs={{0,3},{2,5},{4,7},{8,11},{10,13},{12,15},{16,19},{18,21},{20,23},{... | collective-permute-start | bytes 73736 | tf_op jit(solution)/shard_map/ppermute | solution.py:652
  69.8 5.3 %collective-permute-done.8.diag_ref = f32[6,8,128]{2,1,0:T(8,128)S(1)} collective-permute-done((f32[6,8,128]{2,1,0:T(8,128)S(1)}, f32[6,8,128]{2,1,0:T(8,128)S(1)}, u32[]{:S(2)}, u32[]{:S(2)}) %collective-permute-start.8) | collective-permute-done | bytes 24608 | tf_op jit(solution)/shard_map/ppermute | solution.py:652
  75.1 0.0 collective-permute-done.6.right_ref
  75.1 0.0 collective-permute-done.7.below_ref
  75.1 0.8 collective-permute-start.9
  75.9 5.1 %collective-permute-done.9 = f32[1,2,2,2,8,256]{5,4,3,2,1,0:T(8,128)S(1)} collective-permute-done((f32[1,2,2,2,8,256]{5,4,3,2,1,0:T(8,128)S(1)}, f32[1,2,2,2,8,256]{5,4,3,2,1,0:T(8,128)S(1)}, u32[]{:S(2)}, u32[]{:S(2)}) %collective-permute-start.9) | collective-permute-done | bytes 65568 | tf_op jit(solution)/shard_map/ppermute | solution.py:660
  81.0 1.4 %collective-permute-start.12 = (f32[2,2,2,2,8,256]{5,4,3,2,1,0:T(8,128)S(1)}, f32[2,2,2,2,8,256]{5,4,3,2,1,0:T(8,128)S(1)}, u32[]{:S(2)}, u32[]{:S(2)}) collective-permute-start(f32[2,2,2,2,8,256]{5,4,3,2,1,0:T(8,128)S(1)} %pad_maximum_fusion.refs_0_), channel_id=1, source_target_pairs={{0,96},{8,104},{16,112},{24,120},{32,0},{40,8},{48,16},{56,24},{64... | collective-permute-start | bytes 393224 | tf_op jit(solution)/shard_map/ppermute | solution.py:660
  82.4 0.5 collective-permute-start.11
  82.9 0.8 collective-permute-start.10
  83.7 0.0 collective-permute-start.13
  83.7 2.4 %collective-permute-done.12.refs_3_ = f32[2,2,2,2,8,256]{5,4,3,2,1,0:T(8,128)S(1)} collective-permute-done((f32[2,2,2,2,8,256]{5,4,3,2,1,0:T(8,128)S(1)}, f32[2,2,2,2,8,256]{5,4,3,2,1,0:T(8,128)S(1)}, u32[]{:S(2)}, u32[]{:S(2)}) %collective-permute-start.12) | collective-permute-done | bytes 131104 | tf_op jit(solution)/shard_map/ppermute | solution.py:660
  86.0 0.0 collective-permute-start.16
  86.1 2.9 %collective-permute-done.11.refs_2_ = f32[2,2,2,2,8,256]{5,4,3,2,1,0:T(8,128)S(1)} collective-permute-done((f32[2,2,2,2,8,256]{5,4,3,2,1,0:T(8,128)S(1)}, f32[2,2,2,2,8,256]{5,4,3,2,1,0:T(8,128)S(1)}, u32[]{:S(2)}, u32[]{:S(2)}) %collective-permute-start.11) | collective-permute-done | bytes 131104 | tf_op jit(solution)/shard_map/ppermute | solution.py:660
  88.9 0.0 collective-permute-start.15
  88.9 1.3 %collective-permute-done.10.refs_1_ = f32[2,2,2,2,8,256]{5,4,3,2,1,0:T(8,128)S(1)} collective-permute-done((f32[2,2,2,2,8,256]{5,4,3,2,1,0:T(8,128)S(1)}, f32[2,2,2,2,8,256]{5,4,3,2,1,0:T(8,128)S(1)}, u32[]{:S(2)}, u32[]{:S(2)}) %collective-permute-start.10) | collective-permute-done | bytes 131104 | tf_op jit(solution)/shard_map/ppermute | solution.py:660
  90.2 0.0 collective-permute-start.14
  90.2 0.0 collective-permute-done.13.refs_4_
  90.3 0.0 collective-permute-done.16.refs_7_
  90.3 0.0 collective-permute-done.15.refs_6_
  90.3 1.3 %collective-permute-done.14.refs_5_ = f32[2,2,2,2,8,256]{5,4,3,2,1,0:T(8,128)S(1)} collective-permute-done((f32[2,2,2,2,8,256]{5,4,3,2,1,0:T(8,128)S(1)}, f32[2,2,2,2,8,256]{5,4,3,2,1,0:T(8,128)S(1)}, u32[]{:S(2)}, u32[]{:S(2)}) %collective-permute-start.14) | collective-permute-done | bytes 131104 | tf_op jit(solution)/shard_map/ppermute | solution.py:660
  91.6 1.1 %place.1 = f32[2,2,256,256]{3,2,1,0:T(8,128)} custom-call(s32[1]{0:T(128)} %bitcast.me_ref, f32[2,2,2,2,8,256]{5,4,3,2,1,0:T(8,128)S(1)} %pad_maximum_fusion.refs_0_, f32[2,2,2,2,8,256]{5,4,3,2,1,0:T(8,128)S(1)} %collective-permute-done.10.refs_1_, f32[2,2,2,2,8,256]{5,4,3,2,1,0:T(8,128)S(1)} %collective-permute-done.11.refs_2_, ...), custom_call_target="tpu_custom_call" | custom-call | tf_op jit(solution)/shard_map/place/pallas_call | solution.py:628
  (2 shorter events, 0.0 us)
Async XLA Ops:
  0.0 1.2 %copy-start = (f32[2,2,256,256]{3,2,1,0:T(8,128)S(1)}, f32[2,2,256,256]{3,2,1,0:T(8,128)}, u32[]{:S(2)}) copy-start(f32[2,2,256,256]{3,2,1,0:T(8,128)} %object_ref.3) | copy-start | bytes 3145732
  1.6 11.1 %collective-permute-start = (f32[2,128,256]{2,1,0:T(8,128)S(1)}, f32[2,128,256]{2,1,0:T(8,128)S(1)}, u32[]{:S(2)}, u32[]{:S(2)}) collective-permute-start(f32[2,128,256]{2,1,0:T(8,128)S(1)} %get-tuple-element.21), channel_id=1, source_target_pairs={{2,0},{4,2},{6,4},{3,1},{5,3},{7,5},{10,8},{12,10},{14,12},{11,9},... | collective-permute-start | bytes 786440 | tf_op jit(solution)/shard_map/ppermute | solution.py:641
  4.1 9.9 %collective-permute-start.1 = (f32[2,256,128]{2,1,0:T(8,128)S(1)}, f32[2,256,128]{2,1,0:T(8,128)S(1)}, u32[]{:S(2)}, u32[]{:S(2)}) collective-permute-start(f32[2,256,128]{2,1,0:T(8,128)S(1)} %get-tuple-element.22), channel_id=1, source_target_pairs={{1,0},{3,2},{5,4},{7,6},{9,8},{11,10},{13,12},{15,14},{17,16},{19,... | collective-permute-start | bytes 786440 | tf_op jit(solution)/shard_map/ppermute | solution.py:641
  6.0 6.6 %collective-permute-start.2 = (f32[2,128,128]{2,1,0:T(8,128)S(1)}, f32[2,128,128]{2,1,0:T(8,128)S(1)}, u32[]{:S(2)}, u32[]{:S(2)}) collective-permute-start(f32[2,128,128]{2,1,0:T(8,128)S(1)} %get-tuple-element.23), channel_id=1, source_target_pairs={{3,0},{5,2},{7,4},{11,8},{13,10},{15,12},{19,16},{21,18},{23,20},{... | collective-permute-start | bytes 393224 | tf_op jit(solution)/shard_map/ppermute | solution.py:652
  7.3 2.2 %copy-start.2 = (f32[2,8,256,256]{3,2,1,0:T(8,128)S(1)}, f32[2,8,256,256]{3,2,1,0:T(8,128)}, u32[]{:S(2)}) copy-start(f32[2,8,256,256]{3,2,1,0:T(8,128)} %probe_ref.1) | copy-start | bytes 12582916
  9.5 0.9 %copy-start.5 = (f32[1,1,1,256,256]{4,3,2,1,0:T(8,128)S(1)}, f32[1,1,1,256,256]{4,3,2,1,0:T(8,128)}, u32[]{:S(2)}) copy-start(f32[1,1,1,256,256]{4,3,2,1,0:T(8,128)} %param.9) | copy-start | bytes 786436
  10.5 5.6 %copy-start.1 = (f32[2,2,256,256]{3,2,1,0:T(8,128)S(1)}, f32[2,2,256,256]{3,2,1,0:T(8,128)}, u32[]{:S(2)}) copy-start(f32[2,2,256,256]{3,2,1,0:T(8,128)} %object_ref.3) | copy-start | bytes 3145732
  10.5 5.6 %copy-start.3 = (bf16[4,256,768]{2,1,0:T(8,128)(2,1)S(1)}, bf16[4,256,768]{2,1,0:T(8,128)(2,1)}, u32[]{:S(2)}) copy-start(bf16[4,256,768]{2,1,0:T(8,128)(2,1)} %constant.11.clone.row_far) | copy-start | bytes 4718596
  10.5 5.6 %copy-start.4 = (bf16[4,768,256]{2,1,0:T(8,128)(2,1)S(1)}, bf16[4,768,256]{2,1,0:T(8,128)(2,1)}, u32[]{:S(2)}) copy-start(bf16[4,768,256]{2,1,0:T(8,128)(2,1)} %constant.10.clone.col_far) | copy-start | bytes 4718596
  10.5 5.6 %copy-start.6 = (s32[1,1,1,2]{3,2,1,0:T(1,128)S(1)}, s32[1,1,1,2]{3,2,1,0:T(1,128)}, u32[]{:S(2)}) copy-start(s32[1,1,1,2]{3,2,1,0:T(1,128)} %param.8) | copy-start | bytes 28
  14.0 2.1 %collective-permute-start.3 = (f32[2,128,256]{2,1,0:T(8,128)S(1)}, f32[2,128,256]{2,1,0:T(8,128)S(1)}, u32[]{:S(2)}, u32[]{:S(2)}) collective-permute-start(f32[2,128,256]{2,1,0:T(8,128)S(1)} %collective-permute-done.below_far), channel_id=1, source_target_pairs={{0,8},{8,0},{16,24},{24,16},{32,40},{40,32},{48,56},{56,48},{64,72... | collective-permute-start | bytes 786440 | tf_op jit(solution)/shard_map/ppermute | solution.py:660
  14.0 2.1 %collective-permute-start.4 = (f32[2,256,128]{2,1,0:T(8,128)S(1)}, f32[2,256,128]{2,1,0:T(8,128)S(1)}, u32[]{:S(2)}, u32[]{:S(2)}) collective-permute-start(f32[2,256,128]{2,1,0:T(8,128)S(1)} %collective-permute-done.1.right_far), channel_id=1, source_target_pairs={{0,8},{8,0},{16,24},{24,16},{32,40},{40,32},{48,56},{56,48},{64,72... | collective-permute-start | bytes 786440 | tf_op jit(solution)/shard_map/ppermute | solution.py:660
  14.5 1.6 %collective-permute-start.5 = (f32[2,128,128]{2,1,0:T(8,128)S(1)}, f32[2,128,128]{2,1,0:T(8,128)S(1)}, u32[]{:S(2)}, u32[]{:S(2)}) collective-permute-start(f32[2,128,128]{2,1,0:T(8,128)S(1)} %collective-permute-done.2.diag_far), channel_id=1, source_target_pairs={{0,8},{8,0},{16,24},{24,16},{32,40},{40,32},{48,56},{56,48},{64,72... | collective-permute-start | bytes 393224 | tf_op jit(solution)/shard_map/ppermute | solution.py:660
  63.8 11.3 %collective-permute-start.6 = (f32[6,2,8,128]{3,2,1,0:T(8,128)S(1)}, f32[6,2,8,128]{3,2,1,0:T(8,128)S(1)}, u32[]{:S(2)}, u32[]{:S(2)}) collective-permute-start(f32[6,2,8,128]{3,2,1,0:T(8,128)S(1)} %get-tuple-element.34), channel_id=1, source_target_pairs={{0,1},{2,3},{4,5},{6,7},{8,9},{10,11},{12,13},{14,15},{16,17},{18,... | collective-permute-start | bytes 147464 | tf_op jit(solution)/shard_map/ppermute | solution.py:641
  65.1 10.0 %collective-permute-start.7 = (f32[6,8,256]{2,1,0:T(8,128)S(1)}, f32[6,8,256]{2,1,0:T(8,128)S(1)}, u32[]{:S(2)}, u32[]{:S(2)}) collective-permute-start(f32[6,8,256]{2,1,0:T(8,128)S(1)} %get-tuple-element.35), channel_id=1, source_target_pairs={{0,2},{2,4},{4,6},{1,3},{3,5},{5,7},{8,10},{10,12},{12,14},{9,11},... | collective-permute-start | bytes 147464 | tf_op jit(solution)/shard_map/ppermute | solution.py:641
  68.5 6.6 %collective-permute-start.8 = (f32[6,8,128]{2,1,0:T(8,128)S(1)}, f32[6,8,128]{2,1,0:T(8,128)S(1)}, u32[]{:S(2)}, u32[]{:S(2)}) collective-permute-start(f32[6,8,128]{2,1,0:T(8,128)S(1)} %get-tuple-element.36), channel_id=1, source_target_pairs={{0,3},{2,5},{4,7},{8,11},{10,13},{12,15},{16,19},{18,21},{20,23},{... | collective-permute-start | bytes 73736 | tf_op jit(solution)/shard_map/ppermute | solution.py:652
  75.1 5.8 %collective-permute-start.9 = (f32[1,2,2,2,8,256]{5,4,3,2,1,0:T(8,128)S(1)}, f32[1,2,2,2,8,256]{5,4,3,2,1,0:T(8,128)S(1)}, u32[]{:S(2)}, u32[]{:S(2)}) collective-permute-start(f32[1,2,2,2,8,256]{5,4,3,2,1,0:T(8,128)S(1)} %bitcast.5), channel_id=1, source_target_pairs={{0,16},{8,24},{16,0},{24,8},{32,48},{40,56},{48,32},{56,40},{64,80... | collective-permute-start | bytes 196616 | tf_op jit(solution)/shard_map/ppermute | solution.py:660
  81.0 5.0 %collective-permute-start.12 = (f32[2,2,2,2,8,256]{5,4,3,2,1,0:T(8,128)S(1)}, f32[2,2,2,2,8,256]{5,4,3,2,1,0:T(8,128)S(1)}, u32[]{:S(2)}, u32[]{:S(2)}) collective-permute-start(f32[2,2,2,2,8,256]{5,4,3,2,1,0:T(8,128)S(1)} %pad_maximum_fusion.refs_0_), channel_id=1, source_target_pairs={{0,96},{8,104},{16,112},{24,120},{32,0},{40,8},{48,16},{56,24},{64... | collective-permute-start | bytes 393224 | tf_op jit(solution)/shard_map/ppermute | solution.py:660
  82.4 6.6 %collective-permute-start.11 = (f32[2,2,2,2,8,256]{5,4,3,2,1,0:T(8,128)S(1)}, f32[2,2,2,2,8,256]{5,4,3,2,1,0:T(8,128)S(1)}, u32[]{:S(2)}, u32[]{:S(2)}) collective-permute-start(f32[2,2,2,2,8,256]{5,4,3,2,1,0:T(8,128)S(1)} %pad_maximum_fusion.refs_0_), channel_id=1, source_target_pairs={{0,64},{8,72},{16,80},{24,88},{32,96},{40,104},{48,112},{56,120},{... | collective-permute-start | bytes 393224 | tf_op jit(solution)/shard_map/ppermute | solution.py:660
  82.9 7.4 %collective-permute-start.10 = (f32[2,2,2,2,8,256]{5,4,3,2,1,0:T(8,128)S(1)}, f32[2,2,2,2,8,256]{5,4,3,2,1,0:T(8,128)S(1)}, u32[]{:S(2)}, u32[]{:S(2)}) collective-permute-start(f32[2,2,2,2,8,256]{5,4,3,2,1,0:T(8,128)S(1)} %pad_maximum_fusion.refs_0_), channel_id=1, source_target_pairs={{0,32},{8,40},{16,48},{24,56},{32,64},{40,72},{48,80},{56,88},{64,... | collective-permute-start | bytes 393224 | tf_op jit(solution)/shard_map/ppermute | solution.py:660
  83.7 6.6 %collective-permute-start.13 = (f32[2,2,2,2,8,256]{5,4,3,2,1,0:T(8,128)S(1)}, f32[2,2,2,2,8,256]{5,4,3,2,1,0:T(8,128)S(1)}, u32[]{:S(2)}, u32[]{:S(2)}) collective-permute-start(f32[2,2,2,2,8,256]{5,4,3,2,1,0:T(8,128)S(1)} %pad_maximum_fusion.refs_0_), channel_id=1, source_target_pairs={{0,8},{8,0},{16,24},{24,16},{32,40},{40,32},{48,56},{56,48},{64,72... | collective-permute-start | bytes 393224 | tf_op jit(solution)/shard_map/ppermute | solution.py:660
  86.0 4.2 %collective-permute-start.16 = (f32[2,2,2,2,8,256]{5,4,3,2,1,0:T(8,128)S(1)}, f32[2,2,2,2,8,256]{5,4,3,2,1,0:T(8,128)S(1)}, u32[]{:S(2)}, u32[]{:S(2)}) collective-permute-start(f32[2,2,2,2,8,256]{5,4,3,2,1,0:T(8,128)S(1)} %collective-permute-done.12.refs_3_), channel_id=1, source_target_pairs={{0,8},{8,0},{16,24},{24,16},{32,40},{40,32},{48,56},{56,48},{64,72... | collective-permute-start | bytes 393224 | tf_op jit(solution)/shard_map/ppermute | solution.py:660
  88.9 1.3 %collective-permute-start.15 = (f32[2,2,2,2,8,256]{5,4,3,2,1,0:T(8,128)S(1)}, f32[2,2,2,2,8,256]{5,4,3,2,1,0:T(8,128)S(1)}, u32[]{:S(2)}, u32[]{:S(2)}) collective-permute-start(f32[2,2,2,2,8,256]{5,4,3,2,1,0:T(8,128)S(1)} %collective-permute-done.11.refs_2_), channel_id=1, source_target_pairs={{0,8},{8,0},{16,24},{24,16},{32,40},{40,32},{48,56},{56,48},{64,72... | collective-permute-start | bytes 393224 | tf_op jit(solution)/shard_map/ppermute | solution.py:660
  90.2 1.3 %collective-permute-start.14 = (f32[2,2,2,2,8,256]{5,4,3,2,1,0:T(8,128)S(1)}, f32[2,2,2,2,8,256]{5,4,3,2,1,0:T(8,128)S(1)}, u32[]{:S(2)}, u32[]{:S(2)}) collective-permute-start(f32[2,2,2,2,8,256]{5,4,3,2,1,0:T(8,128)S(1)} %collective-permute-done.10.refs_1_), channel_id=1, source_target_pairs={{0,8},{8,0},{16,24},{24,16},{32,40},{40,32},{48,56},{56,48},{64,72... | collective-permute-start | bytes 393224 | tf_op jit(solution)/shard_map/ppermute | solution.py:660

commit v8 on v7

--- a/solution.py
+++ b/solution.py
@@ -521,10 +521,8 @@
     me = me_ref[0]
     copy = pltpu.make_async_copy(parts_ref.at[:, 20, pl.ds(0, 1)], marks_ref, sem)
     copy.start()
-    own_ref[...] = jnp.zeros_like(own_ref)
-    right_ref[...] = jnp.zeros_like(right_ref)
-    below_ref[...] = jnp.zeros_like(below_ref)
-    diag_ref[...] = jnp.zeros_like(diag_ref)
+    targets = (own_ref, right_ref, below_ref, diag_ref)
+    sums = [[jnp.zeros(ref.shape[1:], f32) for ref in targets] for _ in range(6)]
     sub = lax.broadcasted_iota(jnp.int32, (2, 8, SIDE), 1)
     side = lax.broadcasted_iota(jnp.int32, (2, 8, SIDE), 0)
     cols = lax.broadcasted_iota(jnp.int32, (2, 8, SIDE), 2)
@@ -549,10 +547,13 @@
                 value = jnp.concatenate(halves, axis=2)
             here = jnp.where(inside_row, value, 0.0)
             there = (value - here)[0]
-            own_ref[k] += jnp.where(inside_col, here, 0.0)
-            right_ref[k] += jnp.where(inside_col, 0.0, here)[:, :, :HALF]
-            below_ref[k] += jnp.where(inside_col[0], there, 0.0)
-            diag_ref[k] += jnp.where(inside_col[0], 0.0, there)[:, :HALF]
+            sums[k][0] += jnp.where(inside_col, here, 0.0)
+            sums[k][1] += jnp.where(inside_col, 0.0, here)[:, :, :HALF]
+            sums[k][2] += jnp.where(inside_col[0], there, 0.0)
+            sums[k][3] += jnp.where(inside_col[0], 0.0, there)[:, :HALF]
+    for k in range(6):
+        for ref, value in zip(targets, sums[k]):
+            ref[k] = value
 
 
 def run_sum(me, parts, light):

time: 93.7 us -> 93.9 us (level)
  no operation moved by 1% of the time
where the time goes in v8:
time: 93.9 us; the launch traced here: 92.8 us
  blocking collectives  28.5 us (30%)
  Pallas kernels  22.9 us (24%)
  waiting for transfers between devices  21.1 us (22%)
  starting transfers between devices  15.8 us (17%)
  local copies, waits for them, and re-layouts  4.37 us (5%)
    all_to_all x1, blocking collectives, on_device(): parts = lax.all_to_all(parts, 'scan', 0, 0)  28.5 us
    pallas_call x1, Pallas kernels, run_wave(): pl.pallas_call(wave_kernel, out_shape=jax.ShapeDtypeStruct((SCANS, 21, 8,...  17.8 us
    ppermute x11, waiting for transfers between devices, along_scan(): return lax.ppermute(array, 'scan', pairs)  14.5 us
    ppermute x4, starting transfers between devices, shift(): return lax.ppermute(array, axis, pairs)  9.08 us
    ppermute x2, waiting for transfers between devices, shift_both(): return lax.ppermute(array, ('tx', 'ty'), pairs)  5.32 us
    unnamed x14, local copies, waits for them, and re-layouts  4.37 us
    ppermute x11, starting transfers between devices, along_scan(): return lax.ppermute(array, 'scan', pairs)  4.17 us
    ppermute x2, starting transfers between devices, shift_both(): return lax.ppermute(array, ('tx', 'ty'), pairs)  2.59 us
  transfers between devices with their start and end apart: 17, of which 8 were waited for; matrix products, arithmetic and copies ran while one was open for 0% of the time, Pallas kernels for 2%

profile of v8, /device:TPU:34, one launch (start us, length us, event | category | flops | bytes accessed | tf_op | source)
XLA Modules:
  0.0 92.8 jit_solution(4239646358706058063)
XLA Ops:
  0.0 0.0 copy-start
  0.0 1.2 %copy-done = f32[2,2,256,256]{3,2,1,0:T(8,128)S(1)} copy-done((f32[2,2,256,256]{3,2,1,0:T(8,128)S(1)}, f32[2,2,256,256]{3,2,1,0:T(8,128)}, u32[]{:S(2)}) %copy-start) | copy-done | bytes 1048600
  1.2 0.4 cut.1
  1.6 2.4 %collective-permute-start = (f32[2,128,256]{2,1,0:T(8,128)S(1)}, f32[2,128,256]{2,1,0:T(8,128)S(1)}, u32[]{:S(2)}, u32[]{:S(2)}) collective-permute-start(f32[2,128,256]{2,1,0:T(8,128)S(1)} %get-tuple-element.21), channel_id=1, source_target_pairs={{2,0},{4,2},{6,4},{3,1},{5,3},{7,5},{10,8},{12,10},{14,12},{11,9},... | collective-permute-start | bytes 786440 | tf_op jit(solution)/shard_map/ppermute | solution.py:642
  4.1 1.9 %collective-permute-start.1 = (f32[2,256,128]{2,1,0:T(8,128)S(1)}, f32[2,256,128]{2,1,0:T(8,128)S(1)}, u32[]{:S(2)}, u32[]{:S(2)}) collective-permute-start(f32[2,256,128]{2,1,0:T(8,128)S(1)} %get-tuple-element.22), channel_id=1, source_target_pairs={{1,0},{3,2},{5,4},{7,6},{9,8},{11,10},{13,12},{15,14},{17,16},{19,... | collective-permute-start | bytes 786440 | tf_op jit(solution)/shard_map/ppermute | solution.py:642
  6.0 1.3 %collective-permute-start.2 = (f32[2,128,128]{2,1,0:T(8,128)S(1)}, f32[2,128,128]{2,1,0:T(8,128)S(1)}, u32[]{:S(2)}, u32[]{:S(2)}) collective-permute-start(f32[2,128,128]{2,1,0:T(8,128)S(1)} %get-tuple-element.23), channel_id=1, source_target_pairs={{3,0},{5,2},{7,4},{11,8},{13,10},{15,12},{19,16},{21,18},{23,20},{... | collective-permute-start | bytes 393224 | tf_op jit(solution)/shard_map/ppermute | solution.py:653
  7.3 0.0 copy-start.2
  7.4 2.2 %copy-done.2 = f32[2,8,256,256]{3,2,1,0:T(8,128)S(1)} copy-done((f32[2,8,256,256]{3,2,1,0:T(8,128)S(1)}, f32[2,8,256,256]{3,2,1,0:T(8,128)}, u32[]{:S(2)}) %copy-start.2) | copy-done | bytes 4194328
  9.5 0.0 copy-start.5
  9.5 0.9 %copy-done.5 = f32[1,1,1,256,256]{4,3,2,1,0:T(8,128)S(1)} copy-done((f32[1,1,1,256,256]{4,3,2,1,0:T(8,128)S(1)}, f32[1,1,1,256,256]{4,3,2,1,0:T(8,128)}, u32[]{:S(2)}) %copy-start.5) | copy-done | bytes 262168
  10.5 0.0 copy-start.1
  10.5 0.0 copy-start.3
  10.5 0.0 copy-start.4
  10.5 0.0 copy-start.6
  10.5 2.2 %glow.1 = (f32[512,256]{1,0:T(8,128)S(1)}, f32[256,256]{1,0:T(8,128)S(1)}, f32[2,8,2,256,128]{4,3,2,1,0:T(8,128)S(1)}) custom-call(f32[2,8,256,256]{3,2,1,0:T(8,128)S(1)} %copy-done.2, f32[256,256]{1,0:T(8,128)S(1)} %bitcast.4), custom_call_target="tpu_custom_call" | custom-call | flops 2097152 | bytes 4194304 | tf_op jit(solution)/shard_map/glow/pallas_call | solution.py:405
  12.7 0.0 collective-permute-done.2.diag_far
  12.7 0.0 collective-permute-done.below_far
  12.7 1.2 %collective-permute-done.1.right_far = f32[2,256,128]{2,1,0:T(8,128)S(1)} collective-permute-done((f32[2,256,128]{2,1,0:T(8,128)S(1)}, f32[2,256,128]{2,1,0:T(8,128)S(1)}, u32[]{:S(2)}, u32[]{:S(2)}) %collective-permute-start.1) | collective-permute-done | bytes 262176 | tf_op jit(solution)/shard_map/ppermute | solution.py:642
  14.0 0.0 collective-permute-start.3
  14.0 0.5 collective-permute-start.4
  14.5 0.0 collective-permute-start.5
  14.5 1.6 %collective-permute-done.5.other_diag_far = f32[2,128,128]{2,1,0:T(8,128)S(1)} collective-permute-done((f32[2,128,128]{2,1,0:T(8,128)S(1)}, f32[2,128,128]{2,1,0:T(8,128)S(1)}, u32[]{:S(2)}, u32[]{:S(2)}) %collective-permute-start.5) | collective-permute-done | bytes 131104 | tf_op jit(solution)/shard_map/ppermute | solution.py:661
  16.1 0.0 collective-permute-done.3.other_below_far
  16.1 0.0 collective-permute-done.4.other_right_far
  16.1 0.0 copy-done.1
  16.1 0.0 copy-done.3
  16.1 0.0 copy-done.4
  16.1 0.0 copy-done.6
  16.1 17.8 %wave.1 = f32[16,21,8,128]{3,2,1,0:T(8,128)S(1)} custom-call(s32[2]{0:T(128)S(1)} %bitcast.7, s32[1]{0:T(128)} %bitcast.me_ref, f32[2,128,256]{2,1,0:T(8,128)S(1)} %collective-permute-done.below_far, f32[2,256,128]{2,1,0:T(8,128)S(1)} %collective-permute-done.1.right_far, f32[2,128,128]{2,1,0:T(8,128)S(1)} %collective-permute-done.2.diag_far, ...), custom_call_target="tpu_custom_call" | custom-call | tf_op jit(solution)/shard_map/wave/pallas_call | solution.py:473
  33.9 28.5 %all_to_all.5.parts_ref = f32[16,21,8,128]{3,2,1,0:T(8,128)S(1)} all-to-all(f32[16,21,8,128]{3,2,1,0:T(8,128)S(1)} %wave.1), channel_id=1, replica_groups=mesh['scan'=16,'tx'=4,'ty'=2] {'scan'}, dimensions={0} | all-to-all | bytes 2752512 | tf_op jit(solution)/shard_map/all_to_all | solution.py:682
  62.4 1.4 %sum.1 = (f32[6,2,8,256]{3,2,1,0:T(8,128)S(1)}, f32[6,2,8,128]{3,2,1,0:T(8,128)S(1)}, f32[6,8,256]{2,1,0:T(8,128)S(1)}, f32[6,8,128]{2,1,0:T(8,128)S(1)}) custom-call(s32[1]{0:T(128)} %bitcast.me_ref, f32[16,21,8,128]{3,2,1,0:T(8,128)S(1)} %all_to_all.5.parts_ref, f32[512,256]{1,0:T(8,128)S(1)} %get-tuple-element.32.light_ref), custom_call_target="tpu_custom_call" | custom-call | tf_op jit(solution)/shard_map/sum/pallas_call | solution.py:562
  63.8 1.3 %collective-permute-start.6 = (f32[6,2,8,128]{3,2,1,0:T(8,128)S(1)}, f32[6,2,8,128]{3,2,1,0:T(8,128)S(1)}, u32[]{:S(2)}, u32[]{:S(2)}) collective-permute-start(f32[6,2,8,128]{3,2,1,0:T(8,128)S(1)} %get-tuple-element.34), channel_id=1, source_target_pairs={{0,1},{2,3},{4,5},{6,7},{8,9},{10,11},{12,13},{14,15},{16,17},{18,... | collective-permute-start | bytes 147464 | tf_op jit(solution)/shard_map/ppermute | solution.py:642
  65.1 3.4 %collective-permute-start.7 = (f32[6,8,256]{2,1,0:T(8,128)S(1)}, f32[6,8,256]{2,1,0:T(8,128)S(1)}, u32[]{:S(2)}, u32[]{:S(2)}) collective-permute-start(f32[6,8,256]{2,1,0:T(8,128)S(1)} %get-tuple-element.35), channel_id=1, source_target_pairs={{0,2},{2,4},{4,6},{1,3},{3,5},{5,7},{8,10},{10,12},{12,14},{9,11},... | collective-permute-start | bytes 147464 | tf_op jit(solution)/shard_map/ppermute | solution.py:642
  68.5 1.3 %collective-permute-start.8 = (f32[6,8,128]{2,1,0:T(8,128)S(1)}, f32[6,8,128]{2,1,0:T(8,128)S(1)}, u32[]{:S(2)}, u32[]{:S(2)}) collective-permute-start(f32[6,8,128]{2,1,0:T(8,128)S(1)} %get-tuple-element.36), channel_id=1, source_target_pairs={{0,3},{2,5},{4,7},{8,11},{10,13},{12,15},{16,19},{18,21},{20,23},{... | collective-permute-start | bytes 73736 | tf_op jit(solution)/shard_map/ppermute | solution.py:653
  69.8 5.3 %collective-permute-done.8.diag_ref = f32[6,8,128]{2,1,0:T(8,128)S(1)} collective-permute-done((f32[6,8,128]{2,1,0:T(8,128)S(1)}, f32[6,8,128]{2,1,0:T(8,128)S(1)}, u32[]{:S(2)}, u32[]{:S(2)}) %collective-permute-start.8) | collective-permute-done | bytes 24608 | tf_op jit(solution)/shard_map/ppermute | solution.py:653
  75.2 0.0 collective-permute-done.6.right_ref
  75.2 0.0 collective-permute-done.7.below_ref
  75.2 1.0 %collective-permute-start.9 = (f32[1,2,2,2,8,256]{5,4,3,2,1,0:T(8,128)S(1)}, f32[1,2,2,2,8,256]{5,4,3,2,1,0:T(8,128)S(1)}, u32[]{:S(2)}, u32[]{:S(2)}) collective-permute-start(f32[1,2,2,2,8,256]{5,4,3,2,1,0:T(8,128)S(1)} %bitcast.5), channel_id=1, source_target_pairs={{0,16},{8,24},{16,0},{24,8},{32,48},{40,56},{48,32},{56,40},{64,80... | collective-permute-start | bytes 196616 | tf_op jit(solution)/shard_map/ppermute | solution.py:661
  76.2 5.1 %collective-permute-done.9 = f32[1,2,2,2,8,256]{5,4,3,2,1,0:T(8,128)S(1)} collective-permute-done((f32[1,2,2,2,8,256]{5,4,3,2,1,0:T(8,128)S(1)}, f32[1,2,2,2,8,256]{5,4,3,2,1,0:T(8,128)S(1)}, u32[]{:S(2)}, u32[]{:S(2)}) %collective-permute-start.9) | collective-permute-done | bytes 65568 | tf_op jit(solution)/shard_map/ppermute | solution.py:661
  81.2 1.3 %collective-permute-start.12 = (f32[2,2,2,2,8,256]{5,4,3,2,1,0:T(8,128)S(1)}, f32[2,2,2,2,8,256]{5,4,3,2,1,0:T(8,128)S(1)}, u32[]{:S(2)}, u32[]{:S(2)}) collective-permute-start(f32[2,2,2,2,8,256]{5,4,3,2,1,0:T(8,128)S(1)} %pad_maximum_fusion.refs_0_), channel_id=1, source_target_pairs={{0,96},{8,104},{16,112},{24,120},{32,0},{40,8},{48,16},{56,24},{64... | collective-permute-start | bytes 393224 | tf_op jit(solution)/shard_map/ppermute | solution.py:661
  82.5 0.6 collective-permute-start.11
  83.1 0.8 collective-permute-start.10
  83.9 0.0 collective-permute-start.13
  83.9 2.4 %collective-permute-done.12.refs_3_ = f32[2,2,2,2,8,256]{5,4,3,2,1,0:T(8,128)S(1)} collective-permute-done((f32[2,2,2,2,8,256]{5,4,3,2,1,0:T(8,128)S(1)}, f32[2,2,2,2,8,256]{5,4,3,2,1,0:T(8,128)S(1)}, u32[]{:S(2)}, u32[]{:S(2)}) %collective-permute-start.12) | collective-permute-done | bytes 131104 | tf_op jit(solution)/shard_map/ppermute | solution.py:661
  86.3 0.0 collective-permute-start.16
  86.3 2.8 %collective-permute-done.11.refs_2_ = f32[2,2,2,2,8,256]{5,4,3,2,1,0:T(8,128)S(1)} collective-permute-done((f32[2,2,2,2,8,256]{5,4,3,2,1,0:T(8,128)S(1)}, f32[2,2,2,2,8,256]{5,4,3,2,1,0:T(8,128)S(1)}, u32[]{:S(2)}, u32[]{:S(2)}) %collective-permute-start.11) | collective-permute-done | bytes 131104 | tf_op jit(solution)/shard_map/ppermute | solution.py:661
  89.1 0.0 collective-permute-start.15
  89.1 1.3 %collective-permute-done.10.refs_1_ = f32[2,2,2,2,8,256]{5,4,3,2,1,0:T(8,128)S(1)} collective-permute-done((f32[2,2,2,2,8,256]{5,4,3,2,1,0:T(8,128)S(1)}, f32[2,2,2,2,8,256]{5,4,3,2,1,0:T(8,128)S(1)}, u32[]{:S(2)}, u32[]{:S(2)}) %collective-permute-start.10) | collective-permute-done | bytes 131104 | tf_op jit(solution)/shard_map/ppermute | solution.py:661
  90.4 0.0 collective-permute-start.14
  90.4 0.0 collective-permute-done.13.refs_4_
  90.4 0.0 collective-permute-done.16.refs_7_
  90.4 0.0 collective-permute-done.15.refs_6_
  90.4 1.3 %collective-permute-done.14.refs_5_ = f32[2,2,2,2,8,256]{5,4,3,2,1,0:T(8,128)S(1)} collective-permute-done((f32[2,2,2,2,8,256]{5,4,3,2,1,0:T(8,128)S(1)}, f32[2,2,2,2,8,256]{5,4,3,2,1,0:T(8,128)S(1)}, u32[]{:S(2)}, u32[]{:S(2)}) %collective-permute-start.14) | collective-permute-done | bytes 131104 | tf_op jit(solution)/shard_map/ppermute | solution.py:661
  91.7 1.1 %place.1 = f32[2,2,256,256]{3,2,1,0:T(8,128)} custom-call(s32[1]{0:T(128)} %bitcast.me_ref, f32[2,2,2,2,8,256]{5,4,3,2,1,0:T(8,128)S(1)} %pad_maximum_fusion.refs_0_, f32[2,2,2,2,8,256]{5,4,3,2,1,0:T(8,128)S(1)} %collective-permute-done.10.refs_1_, f32[2,2,2,2,8,256]{5,4,3,2,1,0:T(8,128)S(1)} %collective-permute-done.11.refs_2_, ...), custom_call_target="tpu_custom_call" | custom-call | tf_op jit(solution)/shard_map/place/pallas_call | solution.py:629
  (2 shorter events, 0.0 us)
Async XLA Ops:
  0.0 1.2 %copy-start = (f32[2,2,256,256]{3,2,1,0:T(8,128)S(1)}, f32[2,2,256,256]{3,2,1,0:T(8,128)}, u32[]{:S(2)}) copy-start(f32[2,2,256,256]{3,2,1,0:T(8,128)} %object_ref.3) | copy-start | bytes 3145732
  1.6 11.1 %collective-permute-start = (f32[2,128,256]{2,1,0:T(8,128)S(1)}, f32[2,128,256]{2,1,0:T(8,128)S(1)}, u32[]{:S(2)}, u32[]{:S(2)}) collective-permute-start(f32[2,128,256]{2,1,0:T(8,128)S(1)} %get-tuple-element.21), channel_id=1, source_target_pairs={{2,0},{4,2},{6,4},{3,1},{5,3},{7,5},{10,8},{12,10},{14,12},{11,9},... | collective-permute-start | bytes 786440 | tf_op jit(solution)/shard_map/ppermute | solution.py:642
  4.1 9.9 %collective-permute-start.1 = (f32[2,256,128]{2,1,0:T(8,128)S(1)}, f32[2,256,128]{2,1,0:T(8,128)S(1)}, u32[]{:S(2)}, u32[]{:S(2)}) collective-permute-start(f32[2,256,128]{2,1,0:T(8,128)S(1)} %get-tuple-element.22), channel_id=1, source_target_pairs={{1,0},{3,2},{5,4},{7,6},{9,8},{11,10},{13,12},{15,14},{17,16},{19,... | collective-permute-start | bytes 786440 | tf_op jit(solution)/shard_map/ppermute | solution.py:642
  6.0 6.6 %collective-permute-start.2 = (f32[2,128,128]{2,1,0:T(8,128)S(1)}, f32[2,128,128]{2,1,0:T(8,128)S(1)}, u32[]{:S(2)}, u32[]{:S(2)}) collective-permute-start(f32[2,128,128]{2,1,0:T(8,128)S(1)} %get-tuple-element.23), channel_id=1, source_target_pairs={{3,0},{5,2},{7,4},{11,8},{13,10},{15,12},{19,16},{21,18},{23,20},{... | collective-permute-start | bytes 393224 | tf_op jit(solution)/shard_map/ppermute | solution.py:653
  7.3 2.2 %copy-start.2 = (f32[2,8,256,256]{3,2,1,0:T(8,128)S(1)}, f32[2,8,256,256]{3,2,1,0:T(8,128)}, u32[]{:S(2)}) copy-start(f32[2,8,256,256]{3,2,1,0:T(8,128)} %probe_ref.1) | copy-start | bytes 12582916
  9.5 0.9 %copy-start.5 = (f32[1,1,1,256,256]{4,3,2,1,0:T(8,128)S(1)}, f32[1,1,1,256,256]{4,3,2,1,0:T(8,128)}, u32[]{:S(2)}) copy-start(f32[1,1,1,256,256]{4,3,2,1,0:T(8,128)} %param.9) | copy-start | bytes 786436
  10.5 5.6 %copy-start.1 = (f32[2,2,256,256]{3,2,1,0:T(8,128)S(1)}, f32[2,2,256,256]{3,2,1,0:T(8,128)}, u32[]{:S(2)}) copy-start(f32[2,2,256,256]{3,2,1,0:T(8,128)} %object_ref.3) | copy-start | bytes 3145732
  10.5 5.6 %copy-start.3 = (bf16[4,256,768]{2,1,0:T(8,128)(2,1)S(1)}, bf16[4,256,768]{2,1,0:T(8,128)(2,1)}, u32[]{:S(2)}) copy-start(bf16[4,256,768]{2,1,0:T(8,128)(2,1)} %constant.11.clone.row_far) | copy-start | bytes 4718596
  10.5 5.6 %copy-start.4 = (bf16[4,768,256]{2,1,0:T(8,128)(2,1)S(1)}, bf16[4,768,256]{2,1,0:T(8,128)(2,1)}, u32[]{:S(2)}) copy-start(bf16[4,768,256]{2,1,0:T(8,128)(2,1)} %constant.10.clone.col_far) | copy-start | bytes 4718596
  10.5 5.6 %copy-start.6 = (s32[1,1,1,2]{3,2,1,0:T(1,128)S(1)}, s32[1,1,1,2]{3,2,1,0:T(1,128)}, u32[]{:S(2)}) copy-start(s32[1,1,1,2]{3,2,1,0:T(1,128)} %param.8) | copy-start | bytes 28
  14.0 2.1 %collective-permute-start.3 = (f32[2,128,256]{2,1,0:T(8,128)S(1)}, f32[2,128,256]{2,1,0:T(8,128)S(1)}, u32[]{:S(2)}, u32[]{:S(2)}) collective-permute-start(f32[2,128,256]{2,1,0:T(8,128)S(1)} %collective-permute-done.below_far), channel_id=1, source_target_pairs={{0,8},{8,0},{16,24},{24,16},{32,40},{40,32},{48,56},{56,48},{64,72... | collective-permute-start | bytes 786440 | tf_op jit(solution)/shard_map/ppermute | solution.py:661
  14.0 2.1 %collective-permute-start.4 = (f32[2,256,128]{2,1,0:T(8,128)S(1)}, f32[2,256,128]{2,1,0:T(8,128)S(1)}, u32[]{:S(2)}, u32[]{:S(2)}) collective-permute-start(f32[2,256,128]{2,1,0:T(8,128)S(1)} %collective-permute-done.1.right_far), channel_id=1, source_target_pairs={{0,8},{8,0},{16,24},{24,16},{32,40},{40,32},{48,56},{56,48},{64,72... | collective-permute-start | bytes 786440 | tf_op jit(solution)/shard_map/ppermute | solution.py:661
  14.5 1.6 %collective-permute-start.5 = (f32[2,128,128]{2,1,0:T(8,128)S(1)}, f32[2,128,128]{2,1,0:T(8,128)S(1)}, u32[]{:S(2)}, u32[]{:S(2)}) collective-permute-start(f32[2,128,128]{2,1,0:T(8,128)S(1)} %collective-permute-done.2.diag_far), channel_id=1, source_target_pairs={{0,8},{8,0},{16,24},{24,16},{32,40},{40,32},{48,56},{56,48},{64,72... | collective-permute-start | bytes 393224 | tf_op jit(solution)/shard_map/ppermute | solution.py:661
  63.8 11.3 %collective-permute-start.6 = (f32[6,2,8,128]{3,2,1,0:T(8,128)S(1)}, f32[6,2,8,128]{3,2,1,0:T(8,128)S(1)}, u32[]{:S(2)}, u32[]{:S(2)}) collective-permute-start(f32[6,2,8,128]{3,2,1,0:T(8,128)S(1)} %get-tuple-element.34), channel_id=1, source_target_pairs={{0,1},{2,3},{4,5},{6,7},{8,9},{10,11},{12,13},{14,15},{16,17},{18,... | collective-permute-start | bytes 147464 | tf_op jit(solution)/shard_map/ppermute | solution.py:642
  65.1 10.0 %collective-permute-start.7 = (f32[6,8,256]{2,1,0:T(8,128)S(1)}, f32[6,8,256]{2,1,0:T(8,128)S(1)}, u32[]{:S(2)}, u32[]{:S(2)}) collective-permute-start(f32[6,8,256]{2,1,0:T(8,128)S(1)} %get-tuple-element.35), channel_id=1, source_target_pairs={{0,2},{2,4},{4,6},{1,3},{3,5},{5,7},{8,10},{10,12},{12,14},{9,11},... | collective-permute-start | bytes 147464 | tf_op jit(solution)/shard_map/ppermute | solution.py:642
  68.5 6.6 %collective-permute-start.8 = (f32[6,8,128]{2,1,0:T(8,128)S(1)}, f32[6,8,128]{2,1,0:T(8,128)S(1)}, u32[]{:S(2)}, u32[]{:S(2)}) collective-permute-start(f32[6,8,128]{2,1,0:T(8,128)S(1)} %get-tuple-element.36), channel_id=1, source_target_pairs={{0,3},{2,5},{4,7},{8,11},{10,13},{12,15},{16,19},{18,21},{20,23},{... | collective-permute-start | bytes 73736 | tf_op jit(solution)/shard_map/ppermute | solution.py:653
  75.2 6.0 %collective-permute-start.9 = (f32[1,2,2,2,8,256]{5,4,3,2,1,0:T(8,128)S(1)}, f32[1,2,2,2,8,256]{5,4,3,2,1,0:T(8,128)S(1)}, u32[]{:S(2)}, u32[]{:S(2)}) collective-permute-start(f32[1,2,2,2,8,256]{5,4,3,2,1,0:T(8,128)S(1)} %bitcast.5), channel_id=1, source_target_pairs={{0,16},{8,24},{16,0},{24,8},{32,48},{40,56},{48,32},{56,40},{64,80... | collective-permute-start | bytes 196616 | tf_op jit(solution)/shard_map/ppermute | solution.py:661
  81.2 5.0 %collective-permute-start.12 = (f32[2,2,2,2,8,256]{5,4,3,2,1,0:T(8,128)S(1)}, f32[2,2,2,2,8,256]{5,4,3,2,1,0:T(8,128)S(1)}, u32[]{:S(2)}, u32[]{:S(2)}) collective-permute-start(f32[2,2,2,2,8,256]{5,4,3,2,1,0:T(8,128)S(1)} %pad_maximum_fusion.refs_0_), channel_id=1, source_target_pairs={{0,96},{8,104},{16,112},{24,120},{32,0},{40,8},{48,16},{56,24},{64... | collective-permute-start | bytes 393224 | tf_op jit(solution)/shard_map/ppermute | solution.py:661
  82.5 6.6 %collective-permute-start.11 = (f32[2,2,2,2,8,256]{5,4,3,2,1,0:T(8,128)S(1)}, f32[2,2,2,2,8,256]{5,4,3,2,1,0:T(8,128)S(1)}, u32[]{:S(2)}, u32[]{:S(2)}) collective-permute-start(f32[2,2,2,2,8,256]{5,4,3,2,1,0:T(8,128)S(1)} %pad_maximum_fusion.refs_0_), channel_id=1, source_target_pairs={{0,64},{8,72},{16,80},{24,88},{32,96},{40,104},{48,112},{56,120},{... | collective-permute-start | bytes 393224 | tf_op jit(solution)/shard_map/ppermute | solution.py:661
  83.1 7.3 %collective-permute-start.10 = (f32[2,2,2,2,8,256]{5,4,3,2,1,0:T(8,128)S(1)}, f32[2,2,2,2,8,256]{5,4,3,2,1,0:T(8,128)S(1)}, u32[]{:S(2)}, u32[]{:S(2)}) collective-permute-start(f32[2,2,2,2,8,256]{5,4,3,2,1,0:T(8,128)S(1)} %pad_maximum_fusion.refs_0_), channel_id=1, source_target_pairs={{0,32},{8,40},{16,48},{24,56},{32,64},{40,72},{48,80},{56,88},{64,... | collective-permute-start | bytes 393224 | tf_op jit(solution)/shard_map/ppermute | solution.py:661
  83.9 6.5 %collective-permute-start.13 = (f32[2,2,2,2,8,256]{5,4,3,2,1,0:T(8,128)S(1)}, f32[2,2,2,2,8,256]{5,4,3,2,1,0:T(8,128)S(1)}, u32[]{:S(2)}, u32[]{:S(2)}) collective-permute-start(f32[2,2,2,2,8,256]{5,4,3,2,1,0:T(8,128)S(1)} %pad_maximum_fusion.refs_0_), channel_id=1, source_target_pairs={{0,8},{8,0},{16,24},{24,16},{32,40},{40,32},{48,56},{56,48},{64,72... | collective-permute-start | bytes 393224 | tf_op jit(solution)/shard_map/ppermute | solution.py:661
  86.3 4.1 %collective-permute-start.16 = (f32[2,2,2,2,8,256]{5,4,3,2,1,0:T(8,128)S(1)}, f32[2,2,2,2,8,256]{5,4,3,2,1,0:T(8,128)S(1)}, u32[]{:S(2)}, u32[]{:S(2)}) collective-permute-start(f32[2,2,2,2,8,256]{5,4,3,2,1,0:T(8,128)S(1)} %collective-permute-done.12.refs_3_), channel_id=1, source_target_pairs={{0,8},{8,0},{16,24},{24,16},{32,40},{40,32},{48,56},{56,48},{64,72... | collective-permute-start | bytes 393224 | tf_op jit(solution)/shard_map/ppermute | solution.py:661
  89.1 1.3 %collective-permute-start.15 = (f32[2,2,2,2,8,256]{5,4,3,2,1,0:T(8,128)S(1)}, f32[2,2,2,2,8,256]{5,4,3,2,1,0:T(8,128)S(1)}, u32[]{:S(2)}, u32[]{:S(2)}) collective-permute-start(f32[2,2,2,2,8,256]{5,4,3,2,1,0:T(8,128)S(1)} %collective-permute-done.11.refs_2_), channel_id=1, source_target_pairs={{0,8},{8,0},{16,24},{24,16},{32,40},{40,32},{48,56},{56,48},{64,72... | collective-permute-start | bytes 393224 | tf_op jit(solution)/shard_map/ppermute | solution.py:661
  90.4 1.3 %collective-permute-start.14 = (f32[2,2,2,2,8,256]{5,4,3,2,1,0:T(8,128)S(1)}, f32[2,2,2,2,8,256]{5,4,3,2,1,0:T(8,128)S(1)}, u32[]{:S(2)}, u32[]{:S(2)}) collective-permute-start(f32[2,2,2,2,8,256]{5,4,3,2,1,0:T(8,128)S(1)} %collective-permute-done.10.refs_1_), channel_id=1, source_target_pairs={{0,8},{8,0},{16,24},{24,16},{32,40},{40,32},{48,56},{56,48},{64,72... | collective-permute-start | bytes 393224 | tf_op jit(solution)/shard_map/ppermute | solution.py:661
